TPU v7x, 128 devices: a whole 4x4x4 slice. The times are simulated.
128 devices in a mesh: section: 2 (over y_lo), blk: 16 (over z, x), wshard: 4 (over y_hi, core).
Axes of the slice: x: 4, y: 4 (y_hi: 2, y_lo: 2; y = y_hi * 2 + y_lo), z: 4, core: 2. Of those that a mesh axis runs over, the one named last changes fastest.
Arguments:
- tokens: bfloat16 [2, 4, 2048, 960], P(None, 'wshard', 'blk'), may hold values from -6 to 6
- cotangent: bfloat16 [2, 4, 2048, 960], P(None, 'wshard', 'blk'), may hold values from -6 to 6
- span_order: int32 [16], replicated, may hold values from 0 to 15, each once
- norm_one: bfloat16 [2, 960], P('section', 'wshard'), may hold values from 0.5 to 1.5
- w_query: bfloat16 [2, 960, 960], P('section', 'wshard'), may hold values from -0.1875 to 0.1875
- w_key: bfloat16 [2, 960, 320], P('section', 'wshard'), may hold values from -0.1875 to 0.1875
- w_value: bfloat16 [2, 960, 320], P('section', 'wshard'), may hold values from -0.1875 to 0.1875
- w_out: bfloat16 [2, 960, 960], P('section', 'wshard'), may hold values from -1.5 to 1.5
- norm_two: bfloat16 [2, 960], P('section', 'wshard'), may hold values from 0.5 to 1.5
- w_gate: bfloat16 [2, 960, 2560], P('section', 'wshard'), may hold values from -0.1875 to 0.1875
- w_up: bfloat16 [2, 960, 2560], P('section', 'wshard'), may hold values from -0.1875 to 0.1875
- w_down: bfloat16 [2, 2560, 960], P('section', 'wshard'), may hold values from -0.125 to 0.125
Outputs:
- layer_outputs: bfloat16 [2, 2, 4, 2048, 960], P('section', None, 'wshard', 'blk')
- input_grads: float32 [2, 2, 4, 2048, 960], P('section', None, 'wshard', 'blk')
- grad_norm_one: float32 [2, 960], P('section', 'wshard')
- grad_query: float32 [2, 960, 960], P('section', 'wshard')
- grad_key: float32 [2, 960, 320], P('section', 'wshard')
- grad_value: float32 [2, 960, 320], P('section', 'wshard')
- grad_out: float32 [2, 960, 960], P('section', 'wshard')
- grad_norm_two: float32 [2, 960], P('section', 'wshard')
- grad_gate: float32 [2, 960, 2560], P('section', 'wshard')
- grad_up: float32 [2, 960, 2560], P('section', 'wshard')
- grad_down: float32 [2, 2560, 960], P('section', 'wshard')
Inputs may be any that keep to these rules, and one draw needn't show every extreme that they name: `span_order`: a permutation: each index of blk holds a different position block.
All inputs are finite; a program needn't handle non-finite values.
Results may differ from a plain program's by a relative error of at most 0.03.
Values may be sent and summed in bfloat16 or wider, within the bound.
No kernel may reach another device: no remote copies, remote signals or barrier semaphores. Data moves between devices by JAX's collectives and lax.ppermute only.
A program may use at most 256 MiB of HBM per device.

v0:
```python
import jax
import jax.numpy as jnp
from jax import lax
from jax.sharding import PartitionSpec as P

H = 15
KV = 5
HD = 64


eps_norm = 1e-05
rope_base = 10000.0


def shifted(array, axis, by):
    peers = lax.axis_size(axis)
    pairs = [(i, i + by) for i in range(peers) if 0 <= i + by < peers]
    return lax.ppermute(array, axis, pairs)


def for_sending(array):
    return jax.tree.map(lambda a: a.astype(jnp.bfloat16) if a.dtype == jnp.float32 else a, array)


def rms_scale(values, gain):
    return values * lax.rsqrt(jnp.mean(values * values, axis=-1, keepdims=True) + eps_norm) * gain


def rotate(values, cosine, sine):
    halfway = values.shape[-1] // 2
    turned = jnp.concatenate([-values[..., halfway:], values[..., :halfway]], axis=-1)
    return values * cosine + turned * sine


def rope_tables(positions, head_size):
    exponent = jnp.arange(head_size // 2, dtype=jnp.float32) * (2.0 / head_size)
    frequency = rope_base ** (-exponent)
    angles = positions.astype(jnp.float32)[:, None] * frequency[None, :]
    angles = jnp.concatenate([angles, angles], axis=-1)
    return (jnp.cos(angles), jnp.sin(angles))


def silu_product(gate_value, up_value):
    return jax.nn.silu(gate_value) * up_value


def token_positions(span_order, first_row, row_count, span_rows):
    row_ids = first_row + jnp.arange(row_count, dtype=jnp.int32)
    owners = row_ids // span_rows
    slots = jnp.arange(span_order.shape[0], dtype=jnp.int32)
    starts = jnp.sum(jnp.where(owners[:, None] == slots[None, :], span_order[None, :], 0), axis=1)
    return starts * span_rows + row_ids % span_rows


def forward_dot(left, right):
    return jnp.dot(left, right, preferred_element_type=jnp.float32)


def across(left, right):
    return lax.dot_general(
        left, right, (((0,), (0,)), ((), ())), preferred_element_type=jnp.float32
    )


def against(left, right):
    return lax.dot_general(
        left, right, (((1,), (1,)), ((), ())), preferred_element_type=jnp.float32
    )


def attention_scores(queries, whole_keys, allowed):
    row_count = queries.shape[0]
    grouped = queries.reshape(row_count, KV, H // KV, HD)
    raw_scores = jnp.einsum(
        "qkgd,skd->kgqs",
        grouped,
        whole_keys.reshape(-1, KV, HD),
        preferred_element_type=jnp.float32,
    )
    return jnp.where(allowed[None, None], raw_scores * HD ** (-0.5), -jnp.inf)


def rope_back(grad_rot, cosine, sine):

    def turn(values):
        return rotate(values, cosine[:, None, :], sine[:, None, :])

    unused, pullback = jax.vjp(turn, jnp.zeros(grad_rot.shape, jnp.float32))
    return pullback(grad_rot)[0]


def send_forward(values):
    return shifted(values, "section", 1)


def send_backward(values):
    return shifted(values, "section", -1)


def layer_forward(inputs, weights, cosine, sine, allowed):
    gain_one, query_w, key_w, value_w, out_w, gain_two, gate_w, up_w, down_w = weights
    row_count = inputs.shape[0]
    normed = rms_scale(inputs, gain_one.astype(jnp.float32)).astype(jnp.bfloat16)
    query_lin = forward_dot(normed, query_w)
    key_lin = forward_dot(normed, key_w)
    value_own = forward_dot(normed, value_w).astype(jnp.bfloat16)
    queries = rotate(
        query_lin.reshape(row_count, H, HD), cosine[:, None, :], sine[:, None, :]
    ).astype(jnp.bfloat16)
    key_own = rotate(
        key_lin.reshape(row_count, KV, HD), cosine[:, None, :], sine[:, None, :]
    ).astype(jnp.bfloat16)
    key_own = key_own.reshape(row_count, KV * HD)
    whole_keys, whole_values = (
        lax.all_gather(key_own, "blk", axis=0, tiled=True),
        lax.all_gather(value_own, "blk", axis=0, tiled=True),
    )
    scores = attention_scores(queries, whole_keys, allowed)
    row_peak = jnp.max(scores, axis=-1, keepdims=True)
    exponent_terms = jnp.exp(scores - row_peak)
    row_total = jnp.sum(exponent_terms, axis=-1, keepdims=True)
    log_total = row_peak + jnp.log(row_total)
    attend = (exponent_terms / row_total).astype(jnp.bfloat16)
    mixed = jnp.einsum(
        "kgqs,skd->qkgd",
        attend,
        whole_values.reshape(-1, KV, HD),
        preferred_element_type=jnp.float32,
    )
    mixed = mixed.reshape(row_count, H * HD).astype(jnp.bfloat16)
    residual = inputs + forward_dot(mixed, out_w)
    normed_two = rms_scale(residual, gain_two.astype(jnp.float32)).astype(jnp.bfloat16)
    gate_value = forward_dot(normed_two, gate_w)
    up_value = forward_dot(normed_two, up_w)
    hidden = silu_product(gate_value, up_value).astype(jnp.bfloat16)
    result = residual + forward_dot(hidden, down_w)
    kept_state = (
        inputs,
        normed,
        queries,
        key_own,
        value_own,
        whole_keys,
        whole_values,
        log_total,
        mixed,
        residual,
        normed_two,
        gate_value,
        up_value,
        hidden,
    )
    return (result, kept_state)


def layer_backward(out_grad, kept_state, weights, cosine, sine, allowed):
    gain_one, query_w, key_w, value_w, out_w, gain_two, gate_w, up_w, down_w = weights
    (
        inputs,
        normed,
        queries,
        key_own,
        value_own,
        whole_keys,
        whole_values,
        log_total,
        mixed,
        residual,
        normed_two,
        gate_value,
        up_value,
        hidden,
    ) = kept_state
    row_count = inputs.shape[0]
    whole_keys, whole_values = (
        lax.all_gather(key_own, "blk", axis=0, tiled=True),
        lax.all_gather(value_own, "blk", axis=0, tiled=True),
    )
    branch_grad = out_grad.astype(jnp.bfloat16)
    grad_down = across(hidden, branch_grad)
    hidden_grad = against(branch_grad, down_w)
    unused, pullback = jax.vjp(silu_product, gate_value, up_value)
    gate_grad, up_grad = pullback(hidden_grad)
    gate_grad = gate_grad.astype(jnp.bfloat16)
    up_grad = up_grad.astype(jnp.bfloat16)
    grad_gate = across(normed_two, gate_grad)
    grad_up = across(normed_two, up_grad)
    normed_two_grad = against(gate_grad, gate_w) + against(up_grad, up_w)
    unused, pullback = jax.vjp(rms_scale, residual, gain_two.astype(jnp.float32))
    residual_part, grad_gain_two = pullback(normed_two_grad)
    residual_grad = out_grad + residual_part
    attn_grad = residual_grad.astype(jnp.bfloat16)
    grad_out = across(mixed, attn_grad)
    mixed_grad = against(attn_grad, out_w).astype(jnp.bfloat16).reshape(row_count, KV, H // KV, HD)
    scores = attention_scores(queries, whole_keys, allowed)
    attend_full = jnp.exp(scores - log_total)
    attend = attend_full.astype(jnp.bfloat16)
    attend_grad = jnp.einsum(
        "qkgd,skd->kgqs",
        mixed_grad,
        whole_values.reshape(-1, KV, HD),
        preferred_element_type=jnp.float32,
    )
    value_grad_all = jnp.einsum(
        "kgqs,qkgd->skd", attend, mixed_grad, preferred_element_type=jnp.float32
    )
    inner_sum = jnp.sum(attend_full * attend_grad, axis=-1, keepdims=True)
    score_grad = (attend_full * (attend_grad - inner_sum)).astype(jnp.bfloat16)
    query_grad = jnp.einsum(
        "kgqs,skd->qkgd",
        score_grad,
        whole_keys.reshape(-1, KV, HD),
        preferred_element_type=jnp.float32,
    ) * HD ** (-0.5)
    grouped = queries.reshape(row_count, KV, H // KV, HD)
    key_grad_all = jnp.einsum(
        "kgqs,qkgd->skd", score_grad, grouped, preferred_element_type=jnp.float32
    ) * HD ** (-0.5)
    key_sum, value_sum = (
        lax.psum_scatter(
            key_grad_all.reshape(-1, KV * HD).astype(jnp.bfloat16),
            "blk",
            scatter_dimension=0,
            tiled=True,
        ).astype(jnp.float32),
        lax.psum_scatter(
            value_grad_all.reshape(-1, KV * HD).astype(jnp.bfloat16),
            "blk",
            scatter_dimension=0,
            tiled=True,
        ).astype(jnp.float32),
    )
    query_lin_grad = (
        rope_back(query_grad.reshape(row_count, H, HD), cosine, sine)
        .reshape(row_count, H * HD)
        .astype(jnp.bfloat16)
    )
    key_lin_grad = (
        rope_back(key_sum.reshape(row_count, KV, HD), cosine, sine)
        .reshape(row_count, KV * HD)
        .astype(jnp.bfloat16)
    )
    value_lin_grad = value_sum.astype(jnp.bfloat16)
    grad_query = across(normed, query_lin_grad)
    grad_key = across(normed, key_lin_grad)
    grad_value = across(normed, value_lin_grad)
    normed_grad = (
        against(query_lin_grad, query_w)
        + against(key_lin_grad, key_w)
        + against(value_lin_grad, value_w)
    )
    unused, pullback = jax.vjp(rms_scale, inputs, gain_one.astype(jnp.float32))
    input_part, grad_gain_one = pullback(normed_grad)
    input_grad = residual_grad + input_part
    return (
        input_grad,
        (
            grad_gain_one,
            grad_query,
            grad_key,
            grad_value,
            grad_out,
            grad_gain_two,
            grad_gate,
            grad_up,
            grad_down,
        ),
    )


def body(
    tokens,
    cotangent,
    span_order,
    norm_one,
    w_query,
    w_key,
    w_value,
    w_out,
    norm_two,
    w_gate,
    w_up,
    w_down,
):
    section_index = lax.axis_index("section")
    first_section = section_index == 0
    cycle_index = lax.axis_index("blk")
    micro_count = tokens.shape[0]
    span_rows = tokens.shape[2]
    length = span_rows * lax.axis_size("blk")
    shards = (
        norm_one[0],
        w_query[0],
        w_key[0],
        w_value[0],
        w_out[0],
        norm_two[0],
        w_gate[0],
        w_up[0],
        w_down[0],
    )
    weights = (
        lax.all_gather(shards[0], "wshard", axis=0, tiled=True),
        lax.all_gather(shards[1], "wshard", axis=0, tiled=True),
        lax.all_gather(shards[2], "wshard", axis=0, tiled=True),
        lax.all_gather(shards[3], "wshard", axis=0, tiled=True),
        lax.all_gather(shards[4], "wshard", axis=0, tiled=True),
        lax.all_gather(shards[5], "wshard", axis=0, tiled=True),
        lax.all_gather(shards[6], "wshard", axis=0, tiled=True),
        lax.all_gather(shards[7], "wshard", axis=0, tiled=True),
        lax.all_gather(shards[8], "wshard", axis=0, tiled=True),
    )
    own_positions = token_positions(span_order, cycle_index * span_rows, span_rows, span_rows)
    key_positions = token_positions(span_order, 0, length, span_rows)
    cosine, sine = rope_tables(own_positions, HD)
    allowed = key_positions[None, :] <= own_positions[:, None]
    zero_rows = jnp.zeros((span_rows, tokens.shape[3]), jnp.float32)
    layer_results = []
    kept_steps = []
    previous = None
    for step_index in range(micro_count + 1):
        own_input = tokens[min(step_index, micro_count - 1), 0].astype(jnp.float32)
        arriving = zero_rows if previous is None else send_forward(previous).astype(jnp.float32)
        layer_input = jnp.where(first_section, own_input, arriving)
        result, kept_state = layer_forward(layer_input, weights, cosine, sine, allowed)
        previous = result.astype(jnp.bfloat16)
        layer_results.append(previous)
        kept_steps.append(kept_state)
    layer_outputs = jnp.stack(
        [
            jnp.where(first_section, layer_results[index_mb], layer_results[index_mb + 1])
            for index_mb in range(micro_count)
        ]
    )
    back_weights = (
        lax.all_gather(shards[0], "wshard", axis=0, tiled=True),
        lax.all_gather(shards[1], "wshard", axis=0, tiled=True),
        lax.all_gather(shards[2], "wshard", axis=0, tiled=True),
        lax.all_gather(shards[3], "wshard", axis=0, tiled=True),
        lax.all_gather(shards[4], "wshard", axis=0, tiled=True),
        lax.all_gather(shards[5], "wshard", axis=0, tiled=True),
        lax.all_gather(shards[6], "wshard", axis=0, tiled=True),
        lax.all_gather(shards[7], "wshard", axis=0, tiled=True),
        lax.all_gather(shards[8], "wshard", axis=0, tiled=True),
    )
    grad_sum = None
    input_list = []
    returning = None
    for step_index in range(micro_count + 1):
        own_grad = (
            cotangent[step_index, 0].astype(jnp.float32) if step_index < micro_count else zero_rows
        )
        arriving = zero_rows if returning is None else send_backward(returning).astype(jnp.float32)
        out_grad = jnp.where(first_section, arriving, own_grad)
        earlier = kept_steps[max(step_index - 1, 0)]
        later = kept_steps[min(step_index + 1, micro_count)]
        chosen = jax.tree.map(
            lambda first_item, second_item: jnp.where(first_section, first_item, second_item),
            earlier,
            later,
        )
        input_grad, grads = layer_backward(out_grad, chosen, back_weights, cosine, sine, allowed)
        grad_sum = (
            grads
            if grad_sum is None
            else jax.tree.map(
                lambda first_item, second_item: first_item + second_item, grad_sum, grads
            )
        )
        input_list.append(input_grad)
        returning = input_grad.astype(jnp.bfloat16)
    input_grads = jnp.stack(
        [
            jnp.where(first_section, input_list[index_mb + 1], input_list[index_mb])
            for index_mb in range(micro_count)
        ]
    )
    partial_sums = jax.tree.map(
        lambda part: part.astype(jnp.float32),
        lax.psum_scatter(for_sending(grad_sum), "wshard", scatter_dimension=0, tiled=True),
    )
    shares = jax.tree.map(
        lambda part: part.astype(jnp.float32), lax.psum(for_sending(partial_sums), "blk")
    )
    return (layer_outputs[None, :, None], input_grads[None, :, None]) + tuple(
        (item[None] for item in shares)
    )


def solution(mesh):
    return jax.shard_map(
        body,
        mesh=mesh,
        in_specs=(
            P(None, "wshard", "blk", None),
            P(None, "wshard", "blk", None),
            P(),
            P("section", "wshard"),
            P("section", "wshard", None),
            P("section", "wshard", None),
            P("section", "wshard", None),
            P("section", "wshard", None),
            P("section", "wshard"),
            P("section", "wshard", None),
            P("section", "wshard", None),
            P("section", "wshard", None),
        ),
        out_specs=(
            P("section", None, "wshard", "blk", None),
            P("section", None, "wshard", "blk", None),
            P("section", "wshard"),
            P("section", "wshard", None),
            P("section", "wshard", None),
            P("section", "wshard", None),
            P("section", "wshard", None),
            P("section", "wshard"),
            P("section", "wshard", None),
            P("section", "wshard", None),
            P("section", "wshard", None),
        ),
        check_vma=False,
    )
```

profile of v0, /device:TPU:0, one launch (start us, length us, event | category | flops | bytes accessed | tf_op | source)
XLA Modules:
  0.0 1753.3 jit_solution(12149039949245594168)
XLA Ops:
  23.6 21.7 %all-gather.2 = bf16[1,960,320]{2,0,1:T(2,128)(2,1)} all-gather(bf16[1,240,320]{2,0,1:T(2,128)(2,1)S(1)} %copy.77), channel_id=4, replica_groups=mesh['section'=2,'blk'=16,'wshard'=4] {'wshard'}, dimensions={1}, use_global_device_ids=true | all-gather | bytes 768000 | tf_op jit(solution)/shard_map/all_gather | solution.py:305
  113.2 27.9 %all-gather.27.cloned.1.call-done = bf16[2048,320]{0,1:T(8,128)(2,1)} async-done(((bf16[128,320]{0,1:T(8,128)(2,1)}), bf16[2048,320]{0,1:T(8,128)(2,1)}) %all-gather.27.cloned.1.call-update) | async-done | bytes 1310736 | tf_op jit(solution)/shard_map/all_gather | solution.py:116
  151.2 16.6 all-gather.53.cloned.1.call-done
  170.5 40.9 %all-gather.55.cloned.1.call-done = bf16[1,960,2560]{2,1,0:T(8,128)(2,1)} async-done(((bf16[1,240,2560]{2,1,0:T(8,128)(2,1)}), bf16[1,960,2560]{2,1,0:T(8,128)(2,1)}) %all-gather.55.cloned.1.call-update) | async-done | bytes 4915216 | tf_op jit(solution)/shard_map/all_gather | solution.py:309
  216.2 38.8 %all-gather.57.cloned.1.call-done = bf16[1,960,2560]{2,1,0:T(8,128)(2,1)} async-done(((bf16[1,240,2560]{2,1,0:T(8,128)(2,1)}), bf16[1,960,2560]{2,1,0:T(8,128)(2,1)}) %all-gather.57.cloned.1.call-update) | async-done | bytes 4915216 | tf_op jit(solution)/shard_map/all_gather | solution.py:310
  260.0 38.7 %all-gather.59.cloned.1.call-done = bf16[1,2560,960]{1,2,0:T(8,128)(2,1)} async-done(((bf16[1,640,960]{1,2,0:T(8,128)(2,1)}), bf16[1,2560,960]{1,2,0:T(8,128)(2,1)}) %all-gather.59.cloned.1.call-update) | async-done | bytes 4915216 | tf_op jit(solution)/shard_map/all_gather | solution.py:311
  318.4 40.7 %all-gather.33.cloned.1.call-done = bf16[2048,320]{0,1:T(8,128)(2,1)} async-done(((bf16[128,320]{0,1:T(8,128)(2,1)}), bf16[2048,320]{0,1:T(8,128)(2,1)}) %all-gather.33.cloned.1.call-update) | async-done | bytes 1310736 | tf_op jit(solution)/shard_map/all_gather | solution.py:115
  377.7 27.3 %all-gather.31.cloned.1.call-done = bf16[2048,320]{0,1:T(8,128)(2,1)} async-done(((bf16[128,320]{0,1:T(8,128)(2,1)}), bf16[2048,320]{0,1:T(8,128)(2,1)}) %all-gather.31.cloned.1.call-update) | async-done | bytes 1310736 | tf_op jit(solution)/shard_map/all_gather | solution.py:116
  428.7 22.1 %all-gather.39.cloned.1.call-done = bf16[2048,320]{0,1:T(8,128)(2,1)} async-done(((bf16[128,320]{0,1:T(8,128)(2,1)}), bf16[2048,320]{0,1:T(8,128)(2,1)}) %all-gather.39.cloned.1.call-update) | async-done | bytes 1310736 | tf_op jit(solution)/shard_map/all_gather | solution.py:176
  459.9 37.3 %all-gather.41.cloned.1.call-done = bf16[2048,320]{0,1:T(8,128)(2,1)} async-done(((bf16[128,320]{0,1:T(8,128)(2,1)}), bf16[2048,320]{0,1:T(8,128)(2,1)}) %all-gather.41.cloned.1.call-update) | async-done | bytes 1310736 | tf_op jit(solution)/shard_map/all_gather | solution.py:177
  497.2 16.0 fusion.10
  555.6 45.1 %reduce-scatter.40.cloned.1.call-done = bf16[128,320]{1,0:T(8,128)(2,1)} async-done(((bf16[2048,320]{1,0:T(8,128)(2,1)}), bf16[128,320]{1,0:T(8,128)(2,1)}) %reduce-scatter.40.cloned.1.call-update) | async-done | bytes 81936
  604.8 72.6 %reduce-scatter.42.cloned.1.call-done = bf16[128,320]{1,0:T(8,128)(2,1)} async-done(((bf16[2048,320]{1,0:T(8,128)(2,1)}), bf16[128,320]{1,0:T(8,128)(2,1)}) %reduce-scatter.42.cloned.1.call-update) | async-done | bytes 81936
  701.3 30.3 %all-gather.37.cloned.1.call-done = bf16[2048,320]{0,1:T(8,128)(2,1)} async-done(((bf16[128,320]{0,1:T(8,128)(2,1)}), bf16[2048,320]{0,1:T(8,128)(2,1)}) %all-gather.37.cloned.1.call-update) | async-done | bytes 1310736 | tf_op jit(solution)/shard_map/all_gather | solution.py:115
  750.1 27.1 %all-gather.35.cloned.1.call-done = bf16[2048,320]{0,1:T(8,128)(2,1)} async-done(((bf16[128,320]{0,1:T(8,128)(2,1)}), bf16[2048,320]{0,1:T(8,128)(2,1)}) %all-gather.35.cloned.1.call-update) | async-done | bytes 1310736 | tf_op jit(solution)/shard_map/all_gather | solution.py:116
  802.4 20.6 %all-gather.43.cloned.1.call-done = bf16[2048,320]{0,1:T(8,128)(2,1)} async-done(((bf16[128,320]{0,1:T(8,128)(2,1)}), bf16[2048,320]{0,1:T(8,128)(2,1)}) %all-gather.43.cloned.1.call-update) | async-done | bytes 1310736 | tf_op jit(solution)/shard_map/all_gather | solution.py:176
  832.2 36.6 %all-gather.45.cloned.1.call-done = bf16[2048,320]{0,1:T(8,128)(2,1)} async-done(((bf16[128,320]{0,1:T(8,128)(2,1)}), bf16[2048,320]{0,1:T(8,128)(2,1)}) %all-gather.45.cloned.1.call-update) | async-done | bytes 1310736 | tf_op jit(solution)/shard_map/all_gather | solution.py:177
  868.8 16.0 fusion.5
  919.5 52.7 %reduce-scatter.44.cloned.1.call-done = bf16[128,320]{1,0:T(8,128)(2,1)} async-done(((bf16[2048,320]{1,0:T(8,128)(2,1)}), bf16[128,320]{1,0:T(8,128)(2,1)}) %reduce-scatter.44.cloned.1.call-update) | async-done | bytes 81936
  978.7 70.3 %reduce-scatter.46.cloned.1.call-done = bf16[128,320]{1,0:T(8,128)(2,1)} async-done(((bf16[2048,320]{1,0:T(8,128)(2,1)}), bf16[128,320]{1,0:T(8,128)(2,1)}) %reduce-scatter.46.cloned.1.call-update) | async-done | bytes 81936
  1059.1 35.6 %all-gather.47.cloned.1.call-done = bf16[2048,320]{0,1:T(8,128)(2,1)} async-done(((bf16[128,320]{0,1:T(8,128)(2,1)}), bf16[2048,320]{0,1:T(8,128)(2,1)}) %all-gather.47.cloned.1.call-update) | async-done | bytes 1310736 | tf_op jit(solution)/shard_map/all_gather | solution.py:176
  1119.6 21.0 %all-gather.49.cloned.1.call-done = bf16[2048,320]{0,1:T(8,128)(2,1)} async-done(((bf16[128,320]{0,1:T(8,128)(2,1)}), bf16[2048,320]{0,1:T(8,128)(2,1)}) %all-gather.49.cloned.1.call-update) | async-done | bytes 1310736 | tf_op jit(solution)/shard_map/all_gather | solution.py:177
  1140.6 16.0 fusion
  1183.3 34.0 %reduce-scatter.50.cloned.1.call-done = bf16[128,320]{1,0:T(8,128)(2,1)} async-done(((bf16[2048,320]{1,0:T(8,128)(2,1)}), bf16[128,320]{1,0:T(8,128)(2,1)}) %reduce-scatter.50.cloned.1.call-update) | async-done | bytes 81936
  1224.8 69.3 %reduce-scatter.48.cloned.1.call-done = bf16[128,320]{1,0:T(8,128)(2,1)} async-done(((bf16[2048,320]{1,0:T(8,128)(2,1)}), bf16[128,320]{1,0:T(8,128)(2,1)}) %reduce-scatter.48.cloned.1.call-update) | async-done | bytes 81936
  1360.7 58.5 %reduce-scatter.56.cloned.1.call-done = bf16[640,960]{1,0:T(8,128)(2,1)} async-done(((bf16[2560,960]{1,0:T(8,128)(2,1)}), bf16[640,960]{1,0:T(8,128)(2,1)}) %reduce-scatter.56.cloned.1.call-update) | async-done | bytes 1228816
  1421.7 37.9 %reduce-scatter.34.cloned.1.call-done = bf16[240,960]{1,0:T(8,128)(2,1)} async-done(((bf16[960,960]{1,0:T(8,128)(2,1)}), bf16[240,960]{1,0:T(8,128)(2,1)}) %reduce-scatter.34.cloned.1.call-update) | async-done | bytes 460816 | tf_op jit(solution)/shard_map/reduce_scatter | solution.py:380
  1459.5 40.2 %reduce-scatter.32.cloned.1.call-done = bf16[240,960]{1,0:T(8,128)(2,1)} async-done(((bf16[960,960]{1,0:T(8,128)(2,1)}), bf16[240,960]{1,0:T(8,128)(2,1)}) %reduce-scatter.32.cloned.1.call-update) | async-done | bytes 460816 | tf_op jit(solution)/shard_map/reduce_scatter | solution.py:380
  1499.8 58.5 %reduce-scatter.38.cloned.1.call-done = bf16[240,2560]{1,0:T(8,128)(2,1)} async-done(((bf16[960,2560]{1,0:T(8,128)(2,1)}), bf16[240,2560]{1,0:T(8,128)(2,1)}) %reduce-scatter.38.cloned.1.call-update) | async-done | bytes 1228816 | tf_op jit(solution)/shard_map/reduce_scatter | solution.py:380
  1558.2 58.1 %reduce-scatter.36.cloned.1.call-done = bf16[240,2560]{1,0:T(8,128)(2,1)} async-done(((bf16[960,2560]{1,0:T(8,128)(2,1)}), bf16[240,2560]{1,0:T(8,128)(2,1)}) %reduce-scatter.36.cloned.1.call-update) | async-done | bytes 1228816 | tf_op jit(solution)/shard_map/reduce_scatter | solution.py:380
  1633.3 41.4 %all-reduce.16 = (bf16[1,240]{1,0:T(2,128)(2,1)S(1)}, bf16[1,240]{1,0:T(2,128)(2,1)S(1)}) all-reduce(bf16[1,240]{1,0:T(2,128)(2,1)S(1)} %broadcast_in_dim.228, bf16[1,240]{1,0:T(2,128)(2,1)S(1)} %broadcast_in_dim.238), channel_id=1, replica_groups=mesh['section'=2,'blk'=16,'wshard'=4] {'blk'}, use_global_device_ids=true, to_apply=%region_39.40 | all-reduce | flops 480 | bytes 1920 | tf_op jit(solution)/shard_map/psum | solution.py:383
  1679.1 55.6 %all-reduce.22.cloned.1.call-done = (bf16[1,240,960]{2,1,0:T(8,128)(2,1)}, bf16[1,240,320]{1,2,0:T(8,128)(2,1)}, bf16[1,240,320]{1,2,0:T(8,128)(2,1)}, bf16[1,24...) async-done(((bf16[1,240,960]{2,1,0:T(8,128)(2,1)}, bf16[1,240,320]{1,2,0:T(8,128)(2,1)}, ...) | async-done | bytes 4915216 | tf_op jit(solution)/shard_map/psum | solution.py:383
  (630 shorter events, 508.8 us)
Async XLA Ops:
  7.9 87.3 %all-gather.29.cloned.1.call-start = ((), (), s32[]{:S(2)}) async-start(), calls=%async_computation.14 | async-start | bytes 1392640 | tf_op jit(solution)/shard_map/all_gather | solution.py:115
  50.5 90.6 %all-gather.27.cloned.1.call-start = ((), (), s32[]{:S(2)}) async-start(), calls=%async_computation.13 | async-start | bytes 1392640 | tf_op jit(solution)/shard_map/all_gather | solution.py:116
  70.4 97.4 %all-gather.53.cloned.1.call-start = ((), (), s32[]{:S(2)}) async-start(), calls=%async_computation.30 | async-start | bytes 2457600 | tf_op jit(solution)/shard_map/all_gather | solution.py:307
  71.0 140.4 %all-gather.55.cloned.1.call-start = ((), (), s32[]{:S(2)}) async-start(), calls=%async_computation.31 | async-start | bytes 6144000 | tf_op jit(solution)/shard_map/all_gather | solution.py:309
  71.6 183.4 %all-gather.57.cloned.1.call-start = ((), (), s32[]{:S(2)}) async-start(), calls=%async_computation.32 | async-start | bytes 6144000 | tf_op jit(solution)/shard_map/all_gather | solution.py:310
  72.2 226.5 %all-gather.59.cloned.1.call-start = ((), (), s32[]{:S(2)}) async-start(), calls=%async_computation.33 | async-start | bytes 6144000 | tf_op jit(solution)/shard_map/all_gather | solution.py:311
  72.9 286.2 %all-gather.33.cloned.1.call-start = ((), (), s32[]{:S(2)}) async-start(), calls=%async_computation.16 | async-start | bytes 1392640 | tf_op jit(solution)/shard_map/all_gather | solution.py:115
  313.2 91.8 %all-gather.31.cloned.1.call-start = ((), (), s32[]{:S(2)}) async-start(), calls=%async_computation.15 | async-start | bytes 1392640 | tf_op jit(solution)/shard_map/all_gather | solution.py:116
  314.3 136.5 %all-gather.39.cloned.1.call-start = ((), (), s32[]{:S(2)}) async-start(), calls=%async_computation.19 | async-start | bytes 1392640 | tf_op jit(solution)/shard_map/all_gather | solution.py:176
  314.9 182.3 %all-gather.41.cloned.1.call-start = ((), (), s32[]{:S(2)}) async-start(), calls=%async_computation.20 | async-start | bytes 1392640 | tf_op jit(solution)/shard_map/all_gather | solution.py:177
  318.3 282.4 %reduce-scatter.40.cloned.1.call-start = ((), (), s32[]{:S(2)}) async-start(), calls=%async_computation.34 | async-start | bytes 1671168
  527.5 149.9 %reduce-scatter.42.cloned.1.call-start = ((), (), s32[]{:S(2)}) async-start(), calls=%async_computation.35 | async-start | bytes 1671168
  540.9 190.7 %all-gather.37.cloned.1.call-start = ((), (), s32[]{:S(2)}) async-start(), calls=%async_computation.18 | async-start | bytes 1392640 | tf_op jit(solution)/shard_map/all_gather | solution.py:115
  545.8 134.6 %collective-permute-start.1 = (bf16[128,960]{0,1:T(8,128)(2,1)}, bf16[128,960]{0,1:T(8,128)(2,1)}, u32[]{:S(2)}, u32[]{:S(2)}) collective-permute-start(bf16[128,960]{0,1:T(8,128)(2,1)} %fusion.177), channel_id=1, source_target_pairs={{0,64},{1,65},{2,66},{3,67},{4,68},{5,69},{6,70},{7,71},{8,72},{9,... | collective-permute-start | bytes 737288 | tf_op jit(solution)/shard_map/ppermute | solution.py:18
  687.7 89.6 %all-gather.35.cloned.1.call-start = ((), (), s32[]{:S(2)}) async-start(), calls=%async_computation.17 | async-start | bytes 1392640 | tf_op jit(solution)/shard_map/all_gather | solution.py:116
  689.9 133.1 %all-gather.43.cloned.1.call-start = ((), (), s32[]{:S(2)}) async-start(), calls=%async_computation.21 | async-start | bytes 1392640 | tf_op jit(solution)/shard_map/all_gather | solution.py:176
  691.5 177.3 %all-gather.45.cloned.1.call-start = ((), (), s32[]{:S(2)}) async-start(), calls=%async_computation.22 | async-start | bytes 1392640 | tf_op jit(solution)/shard_map/all_gather | solution.py:177
  694.1 99.0 %collective-permute-start.2 = (bf16[128,960]{0,1:T(8,128)(2,1)}, bf16[128,960]{0,1:T(8,128)(2,1)}, u32[]{:S(2)}, u32[]{:S(2)}) collective-permute-start(bf16[128,960]{0,1:T(8,128)(2,1)} %get-tuple-element.99), channel_id=1, source_target_pairs={{64,0},{65,1},{66,2},{67,3},{68,4},{69,5},{70,6},{71,7},{72,8},{73... | collective-permute-start | bytes 737288 | tf_op jit(solution)/shard_map/ppermute | solution.py:18
  699.0 273.3 %reduce-scatter.44.cloned.1.call-start = ((), (), s32[]{:S(2)}) async-start(), calls=%async_computation.36 | async-start | bytes 1671168
  899.1 149.9 %reduce-scatter.46.cloned.1.call-start = ((), (), s32[]{:S(2)}) async-start(), calls=%async_computation.37 | async-start | bytes 1671168
  912.3 182.4 %all-gather.47.cloned.1.call-start = ((), (), s32[]{:S(2)}) async-start(), calls=%async_computation.23 | async-start | bytes 1392640 | tf_op jit(solution)/shard_map/all_gather | solution.py:176
  912.9 227.7 %all-gather.49.cloned.1.call-start = ((), (), s32[]{:S(2)}) async-start(), calls=%async_computation.24 | async-start | bytes 1392640 | tf_op jit(solution)/shard_map/all_gather | solution.py:177
  913.6 303.7 %reduce-scatter.50.cloned.1.call-start = ((), (), s32[]{:S(2)}) async-start(), calls=%async_computation.39 | async-start | bytes 1671168
  1119.4 174.7 %reduce-scatter.48.cloned.1.call-start = ((), (), s32[]{:S(2)}) async-start(), calls=%async_computation.38 | async-start | bytes 1671168
  1174.6 173.6 %reduce-scatter.54.cloned.1.call-start = ((), (), s32[]{:S(2)}) async-start(), calls=%async_computation.41 | async-start | bytes 921600
  1221.8 137.2 %reduce-scatter.52.cloned.1.call-start = ((), (), s32[]{:S(2)}) async-start(), calls=%async_computation.40 | async-start | bytes 921600
  1300.0 119.3 %reduce-scatter.56.cloned.1.call-start = ((), (), s32[]{:S(2)}) async-start(), calls=%async_computation.42 | async-start | bytes 6553600
  1318.5 141.0 %reduce-scatter.34.cloned.1.call-start = ((), (), s32[]{:S(2)}) async-start(), calls=%async_computation.26 | async-start | bytes 2457600 | tf_op jit(solution)/shard_map/reduce_scatter | solution.py:380
  1323.1 176.7 %reduce-scatter.32.cloned.1.call-start = ((), (), s32[]{:S(2)}) async-start(), calls=%async_computation.25 | async-start | bytes 2457600 | tf_op jit(solution)/shard_map/reduce_scatter | solution.py:380
  1331.6 226.6 %reduce-scatter.38.cloned.1.call-start = ((), (), s32[]{:S(2)}) async-start(), calls=%async_computation.28 | async-start | bytes 6144000 | tf_op jit(solution)/shard_map/reduce_scatter | solution.py:380
  1339.4 277.0 %reduce-scatter.36.cloned.1.call-start = ((), (), s32[]{:S(2)}) async-start(), calls=%async_computation.27 | async-start | bytes 6144000 | tf_op jit(solution)/shard_map/reduce_scatter | solution.py:380
  1348.1 386.6 %all-reduce.22.cloned.1.call-start = ((), (), s32[]{:S(2)}) async-start(), calls=%async_computation.43 | async-start | bytes 9994240 | tf_op jit(solution)/shard_map/psum | solution.py:383
  (168 other events, 5014.4 us)
Sparse Core Ops, SparseCore 0:
  9.7 36.1 all-gather.50
  50.6 44.5 all-gather.28
  97.3 43.7 all-gather.26
  142.7 25.1 all-gather.52
  169.4 42.0 all-gather.54
  213.0 42.0 all-gather.56
  256.7 41.9 all-gather.58
  313.3 45.7 all-gather.32
  361.2 43.7 all-gather.30
  407.0 43.7 all-gather.38
  453.4 43.7 all-gather.40
  527.6 73.0 reduce-scatter.39
  604.5 72.8 reduce-scatter.41
  687.8 43.6 all-gather.36
  733.5 43.7 all-gather.34
  779.3 43.7 all-gather.42
  825.0 43.7 all-gather.44
  899.2 72.9 reduce-scatter.43
  976.0 72.9 reduce-scatter.45
  1051.0 43.6 all-gather.46
  1096.8 43.7 all-gather.48
  1144.4 72.8 reduce-scatter.49
  1221.1 72.9 reduce-scatter.47
  1297.2 29.0 reduce-scatter.53
  1329.7 29.2 reduce-scatter.51
  1361.5 57.6 reduce-scatter.55
  1422.6 36.9 reduce-scatter.33
  1462.8 36.9 reduce-scatter.31
  1502.7 55.5 reduce-scatter.37
  1560.8 55.5 reduce-scatter.35
  1622.6 112.0 all-reduce.21
where the time goes:
time: 1760 us; the launch traced here: 1750 us
  waiting for transfers between devices  1150 us (65%)
  matrix products  318 us (18%)
  other arithmetic  99.1 us (6%)
  blocking collectives  95 us (5%)
  local copies, waits for them, and re-layouts  60.3 us (3%)
  between operations  18.7 us (1%)
    unnamed x40, waiting for transfers between devices  417 us
    reduce_scatter x4, waiting for transfers between devices, body(): lax.psum_scatter(for_sending(grad_sum), 'wshard', scatter_dimension=0, ti...  195 us
    all_gather x3, waiting for transfers between devices, layer_backward(): lax.all_gather(value_own, 'blk', axis=0, tiled=True)  95 us
    all_gather x3, waiting for transfers between devices, layer_forward(): lax.all_gather(key_own, 'blk', axis=0, tiled=True)  86.2 us
    all_gather x3, waiting for transfers between devices, layer_forward(): lax.all_gather(value_own, 'blk', axis=0, tiled=True)  82.3 us
    all_gather x3, waiting for transfers between devices, layer_backward(): lax.all_gather(key_own, 'blk', axis=0, tiled=True)  78.3 us
    psum x1, waiting for transfers between devices, body(): lax.psum(for_sending(partial_sums), 'blk')  55.6 us
    dot_general x6, matrix products, attention_scores(): jnp.einsum('qkgd,skd->kgqs', grouped, whole_keys.reshape(-1, KV, HD), pre...  49.6 us
  transfers between devices with their start and end apart: 35, of which 30 were waited for; matrix products, arithmetic and copies ran while one was open for 22% of the time, Pallas kernels for 0%

commit v1 on v0

v1 whole, which is shorter than its diff:
```python
import functools

import jax
import jax.numpy as jnp
from jax import lax
from jax.experimental import pallas as pl
from jax.experimental.pallas import tpu as pltpu
from jax.sharding import PartitionSpec as P

D = 960
H = 15
KV = 5
HD = 64
FF = 2560
ROWS = 128
NB = 16
LEN = ROWS * NB
QKV = H * HD + 2 * KV * HD
UNITS = FF // 8
SHARE = D // 4
PIECE = 16
QKV_PART = QKV // 8
OUT_PART = D // 8
OUT_AT = 256
ATT_WIDTH = 384
DOWN_ROWS = 30
FF_ROWS = 96
TILE = 256

EIGHT = ("section", "wshard")
eps_norm = 1e-05
rope_base = 10000.0
BF = jnp.bfloat16
F32 = jnp.float32
VMEM_BYTES = 56 * 1024 * 1024


def place_of(y, core):
    return (y % 2) * 4 + (y // 2) * 2 + core


def ring_pairs(step, flip):
    return [
        (place_of(y, c), place_of((y + step) % 4, c ^ flip)) for y in range(4) for c in range(2)
    ]


def hop(array, step, flip=0):
    return lax.ppermute(array, EIGHT, ring_pairs(step, flip))


def swap_section(array):
    return lax.ppermute(array, "section", [(0, 1), (1, 0)])


def gather_eight(block):
    half = block.shape[0] // 2
    beside = hop(block, 0, 1)
    before = hop(block, 1)
    after = hop(block, -1)
    far = jnp.concatenate([hop(before[:half], 1), hop(after[half:], -1)], axis=0)
    return [
        [block, beside],
        [after, hop(after, 0, 1)],
        [far, hop(far, 0, 1)],
        [before, hop(before, 0, 1)],
    ]


def scatter_eight(parts):
    half = parts[0][0].shape[0] // 2
    total = [None] * 4
    for step in (2, 1, 3, 0):
        arrived = hop(parts[step][1].astype(BF), 0, 1)
        total[step] = parts[step][0].astype(F32) + arrived.astype(F32)
    far = total[2].astype(BF)
    low = hop(far[:half], 1).astype(F32)
    high = hop(far[half:], -1).astype(F32)
    forth = jnp.concatenate([total[1][:half] + low, total[1][half:]], axis=0).astype(BF)
    back = jnp.concatenate([total[3][:half], total[3][half:] + high], axis=0).astype(BF)
    return total[0] + hop(forth, 1).astype(F32) + hop(back, -1).astype(F32)


def norm_factor(values):
    return lax.rsqrt(jnp.mean(values * values, axis=-1, keepdims=True) + eps_norm)


def norm_backward(values, gain, grad):
    factor = norm_factor(values)
    scaled = grad * gain
    inner = jnp.mean(values * scaled, axis=-1, keepdims=True)
    grad_values = factor * scaled - values * (factor * factor * factor * inner)
    grad_gain = jnp.sum(grad * values * factor, axis=0, keepdims=True)
    return grad_values, grad_gain


def dot(left, right):
    return jnp.dot(left, right, preferred_element_type=F32)


def against(left, right):
    return lax.dot_general(left, right, (((1,), (1,)), ((), ())), preferred_element_type=F32)


def across(left, right):
    return lax.dot_general(left, right, (((0,), (0,)), ((), ())), preferred_element_type=F32)


def rotate(values, cosine, sine):
    half = HD // 2
    turned = jnp.concatenate([-values[:, half:], values[:, :half]], axis=1)
    return values * cosine + turned * sine


def rotate_back(grad, cosine, sine):
    half = HD // 2
    part = grad * sine
    return grad * cosine + jnp.concatenate([part[:, half:], -part[:, :half]], axis=1)


def fold(rows):
    half = rows.shape[0] // 2
    return jnp.concatenate([rows[:half], rows[half:]], axis=1)


def unfold(block):
    return jnp.concatenate([block[:, :HD], block[:, HD:]], axis=0)


def load_blocks(table_ref, layer, blocks, weight_ref, gain_ref, sems):
    def copies(number):
        place = table_ref[2 * number + 1]
        block = blocks[number]
        return (
            pltpu.make_async_copy(
                block.at[pl.ds(0, SHARE)],
                weight_ref.at[pl.ds(pl.multiple_of(place * SHARE, 16), SHARE)],
                sems.at[0, number],
            ),
            pltpu.make_async_copy(
                block.at[pl.ds(SHARE, 16), pl.ds(0, 256)], gain_ref.at[place], sems.at[1, number]
            ),
        )

    for number in range(8):

        @pl.when(table_ref[2 * number] == layer)
        def _():
            for copy in copies(number):
                copy.start()

    for number in range(8):

        @pl.when(table_ref[2 * number] == layer)
        def _():
            for copy in copies(number):
                copy.wait()

    return jnp.concatenate([gain_ref[w, 0:1, :SHARE] for w in range(4)], axis=1).astype(F32)


def project_kernel(layer, table_ref, x_ref, cos_ref, sin_ref, *refs):
    blocks, (h_ref, out_ref, w_ref, gain_ref, sems) = refs[:8], refs[8:]
    gain = load_blocks(table_ref, layer, blocks, w_ref, gain_ref, sems)
    x = x_ref[...]
    h = (x * norm_factor(x) * gain).astype(BF)
    h_ref[...] = h
    cosine, sine = cos_ref[...], sin_ref[...]
    lin = dot(h, w_ref[...])

    def head(at):
        return lin[:, at * HD : (at + 1) * HD]

    for group in range(KV):
        key = rotate(head(H + group), cosine, sine).astype(BF)
        pair = jnp.concatenate([key, head(H + KV + group).astype(BF)], axis=1)
        for member in range(H // KV):
            index = group * (H // KV) + member
            out_ref[index, 0:ROWS, :] = pair
            query = rotate(head(index), cosine, sine).astype(BF)
            out_ref[index, ROWS:, :] = fold(query)
    out_ref[NB - 1] = jnp.zeros((ROWS + ROWS // 2, 2 * HD), BF)


def diagonal_mask(size, keys_first):
    rows = lax.broadcasted_iota(jnp.int32, (size, size), 0)
    columns = lax.broadcasted_iota(jnp.int32, (size, size), 1)
    return rows <= columns if keys_first else columns <= rows


def attend_kernel(place_ref, in_ref, out_ref, lse_ref, q_ref, k_ref, v_ref):
    for p in range(NB):
        block = in_ref[place_ref[p]]
        at = slice(p * ROWS, (p + 1) * ROWS)
        k_ref[at, :] = block[:ROWS, :HD]
        v_ref[at, :] = block[:ROWS, HD:]
        q_ref[at, :] = unfold(block[ROWS:])
    mask = diagonal_mask(TILE, False)
    for tile in range(LEN // TILE):
        at = slice(tile * TILE, (tile + 1) * TILE)
        seen = (tile + 1) * TILE
        scores = against(q_ref[at, :], k_ref[:seen, :]) * HD ** (-0.5)
        last = jnp.where(mask, scores[:, seen - TILE :], -jnp.inf)
        if tile:
            scores = jnp.concatenate([scores[:, : seen - TILE], last], axis=1)
        else:
            scores = last
        peak = jnp.max(scores, axis=-1, keepdims=True)
        terms = jnp.exp(scores - peak)
        total = jnp.sum(terms, axis=-1, keepdims=True)
        attend = (terms * (1.0 / total)).astype(BF)
        mixed = dot(attend, v_ref[:seen, :]).astype(BF)
        lse = peak + jnp.log(total)
        lse_ref[:, at] = jnp.transpose(jnp.broadcast_to(lse, (TILE, 128)))[:8, :]
        for part in range(TILE // ROWS):
            index = place_ref[tile * (TILE // ROWS) + part]
            out_ref[index] = fold(mixed[part * ROWS : (part + 1) * ROWS])


def attend_back_kernel(
    place_ref, in_ref, do_ref, lse_ref, out_ref, q_ref, k_ref, v_ref, g_ref, kt_ref, dq_ref, dk_ref, dv_ref
):
    for p in range(NB):
        block = in_ref[place_ref[p]]
        at = slice(p * ROWS, (p + 1) * ROWS)
        k_ref[at, :] = block[:ROWS, :HD]
        v_ref[at, :] = block[:ROWS, HD:]
        q_ref[at, :] = unfold(block[ROWS:])
        g_ref[at, :] = unfold(do_ref[place_ref[p]])
    kt_ref[...] = jnp.transpose(k_ref[...].astype(F32)).astype(BF)
    dk_ref[...] = jnp.zeros((LEN, HD), F32)
    dv_ref[...] = jnp.zeros((LEN, HD), F32)
    mask = diagonal_mask(TILE, True)
    for tile in range(LEN // TILE):
        at = slice(tile * TILE, (tile + 1) * TILE)
        seen = (tile + 1) * TILE
        query = q_ref[at, :]
        grad = g_ref[at, :]
        scores = against(k_ref[:seen, :], query) * HD ** (-0.5)
        last = jnp.where(mask, scores[seen - TILE :], -jnp.inf)
        if tile:
            scores = jnp.concatenate([scores[: seen - TILE], last], axis=0)
        else:
            scores = last
        full = jnp.exp(scores - lse_ref[0:1, at])
        attend_grad = against(v_ref[:seen, :], grad)
        inner = jnp.sum(full * attend_grad, axis=0, keepdims=True)
        score_grad = (full * (attend_grad - inner)).astype(BF)
        dv_ref[:seen, :] += dot(full.astype(BF), grad)
        dk_ref[:seen, :] += dot(score_grad, query)
        dq_ref[at, :] = jnp.transpose(dot(kt_ref[:, :seen], score_grad))
    for p in range(NB):
        index = place_ref[p]
        at = slice(p * ROWS, (p + 1) * ROWS)
        key_grad = (dk_ref[at, :] * HD ** (-0.5)).astype(BF)
        query_grad = (dq_ref[at, :] * HD ** (-0.5)).astype(BF)
        out_ref[index, 0:ROWS, :] = jnp.concatenate([key_grad, dv_ref[at, :].astype(BF)], axis=1)
        out_ref[index, ROWS:, :] = fold(query_grad)


def mix_kernel(layer, table_ref, in_ref, x_ref, *refs):
    blocks, (o_ref, x2_ref, h_ref, w_ref, gain_ref, sems) = refs[:8], refs[8:]
    gain = load_blocks(table_ref, layer, blocks, w_ref, gain_ref, sems)
    mixed = jnp.concatenate([unfold(in_ref[index]) for index in range(H)], axis=1)
    o_ref[...] = mixed
    x2 = x_ref[...] + dot(mixed, w_ref[...])
    x2_ref[...] = x2
    h_ref[...] = (x2 * norm_factor(x2) * gain).astype(BF)


def mix_back_kernel(layer, table_ref, dy_ref, dh_ref, x2_ref, *refs):
    blocks, (dx2_ref, out_ref, e_ref, gg_ref, w_ref, gain_ref, sems) = refs[:8], refs[8:]
    gain = load_blocks(table_ref, layer, blocks, w_ref, gain_ref, sems)
    part, grad_gain = norm_backward(x2_ref[...], gain, dh_ref[...])
    dx2 = dy_ref[...] + part
    dx2_ref[...] = dx2
    gg_ref[...] = grad_gain
    low = dx2.astype(BF)
    for index in range(8):
        e_ref[index, :, 0:OUT_PART] = low[:, index * OUT_PART : (index + 1) * OUT_PART]
        e_ref[index, :, OUT_PART:] = jnp.zeros((ROWS, 128 - OUT_PART), BF)
    mixed_grad = against(low, w_ref[...]).astype(BF)
    for index in range(H):
        out_ref[index] = fold(mixed_grad[:, index * HD : (index + 1) * HD])
    out_ref[NB - 1] = jnp.zeros((ROWS // 2, 2 * HD), BF)


def project_back_kernel(layer, table_ref, in_ref, dx2_ref, x_ref, cos_ref, sin_ref, gg_ref, *refs):
    blocks, (dx_ref, lin_ref, w_ref, gain_ref, sems) = refs[:8], refs[8:]
    gain = load_blocks(table_ref, layer, blocks, w_ref, gain_ref, sems)
    cosine, sine = cos_ref[...], sin_ref[...]
    queries, keys, values = [], [], []
    for group in range(KV):
        pair = None
        for member in range(H // KV):
            index = group * (H // KV) + member
            own = in_ref[index, 0:ROWS, :].astype(F32)
            pair = own if pair is None else pair + own
            query = unfold(in_ref[index, ROWS:, :].astype(F32))
            queries.append(rotate_back(query, cosine, sine).astype(BF))
        keys.append(rotate_back(pair[:, :HD], cosine, sine).astype(BF))
        values.append(pair[:, HD:].astype(BF))
    lin_grad = jnp.concatenate(queries + keys + values, axis=1)
    part, grad_gain = norm_backward(x_ref[...], gain, against(lin_grad, w_ref[...]))
    dx_ref[...] = dx2_ref[...] + part
    gains = jnp.concatenate([grad_gain, gg_ref[...], jnp.zeros((14, D), F32)], axis=0).astype(BF)
    for index in range(8):
        lin_ref[index, 0:ROWS, 0:QKV_PART] = lin_grad[:, index * QKV_PART : (index + 1) * QKV_PART]
        lin_ref[index, 0:ROWS, QKV_PART:] = jnp.zeros((ROWS, 256 - QKV_PART), BF)
        lin_ref[index, ROWS:, 0:OUT_PART] = gains[:, index * OUT_PART : (index + 1) * OUT_PART]
        lin_ref[index, ROWS:, OUT_PART:] = jnp.zeros((16, 256 - OUT_PART), BF)


def feed_kernel(count, *refs):
    normed = jnp.concatenate([ref[...] for ref in refs[:count]], axis=0)
    wgu_ref, wd_ref, lin_ref, hidden_ref = refs[count : count + 4]
    lin = dot(normed, wgu_ref[...])
    lin_ref[...] = lin
    gate, up = lin[:, :UNITS], lin[:, UNITS:]
    hidden = (gate * jax.nn.sigmoid(gate) * up).astype(BF)
    hidden_ref[...] = hidden
    part = dot(hidden, wd_ref[...]).astype(BF)
    for index, ref in enumerate(refs[count + 4 :]):
        ref[...] = part[index * ROWS : (index + 1) * ROWS]


def feed_back_kernel(count, *refs):
    branch = jnp.concatenate([ref[...] for ref in refs[:count]], axis=0)
    lin_ref, wgu_ref, wd_ref, grad_ref = refs[count : count + 4]
    hidden_grad = against(branch, wd_ref[...])
    gate, up = lin_ref[:, :UNITS], lin_ref[:, UNITS:]
    sig = jax.nn.sigmoid(gate)
    up_grad = hidden_grad * (gate * sig)
    gate_grad = hidden_grad * up * (sig + gate * sig * (1.0 - sig))
    lin_grad = jnp.concatenate([gate_grad, up_grad], axis=1).astype(BF)
    grad_ref[...] = lin_grad
    part = against(lin_grad, wgu_ref[...]).astype(BF)
    for index, ref in enumerate(refs[count + 4 :]):
        ref[...] = part[index * ROWS : (index + 1) * ROWS]


def feed_grads_kernel(*refs):
    normed = jnp.concatenate([ref[...] for ref in refs[:8]], axis=0)
    branch = jnp.concatenate([ref[...] for ref in refs[8:16]], axis=0)
    lin_grad = jnp.concatenate([ref[...] for ref in refs[16:19]], axis=0)
    hidden = jnp.concatenate([ref[...] for ref in refs[19:22]], axis=0)
    out_ref = refs[22]
    gate_up = across(normed, lin_grad).astype(BF)
    for piece in range(NB - 1):
        for w in range(4):
            at = w * SHARE + piece * PIECE
            out_ref[piece, w * PIECE : (w + 1) * PIECE, :] = gate_up[at : at + PIECE]
    out_ref[NB - 1, 0 : 4 * PIECE, :] = jnp.zeros((4 * PIECE, 2 * UNITS), BF)
    down = across(hidden, branch)
    each = UNITS // NB
    for piece in range(NB):
        rows = down[piece * each : (piece + 1) * each]
        tail = rows[:, 2 * UNITS :]
        tail = jnp.concatenate([tail[: each // 2], tail[each // 2 :]], axis=1)
        rest = jnp.zeros((FF_ROWS - 4 * PIECE - DOWN_ROWS, 2 * UNITS), F32)
        out_ref[piece, 4 * PIECE :, :] = jnp.concatenate(
            [rows[:, : 2 * UNITS], tail, rest], axis=0
        ).astype(BF)


def attend_grads_kernel(index_ref, rows_ref, lin_ref, e_ref, out_ref):
    normed = jnp.concatenate([rows_ref[t, 0:ROWS, :] for t in range(8)], axis=0)
    mixed = jnp.concatenate([rows_ref[t, ROWS:, :] for t in range(8)], axis=0)
    lin_grad = jnp.concatenate([lin_ref[t, 0:ROWS, :] for t in range(8)], axis=0)
    branch = jnp.concatenate([e_ref[t] for t in range(8)], axis=0)
    weight = across(normed, lin_grad).astype(BF)
    out_weight = across(mixed, branch).astype(BF)
    for piece in range(NB - 1):
        for w in range(4):
            at = w * SHARE + piece * PIECE
            to = slice(w * PIECE, (w + 1) * PIECE)
            out_ref[piece, to, 0:OUT_AT] = weight[at : at + PIECE]
            out_ref[piece, to, OUT_AT:] = out_weight[at : at + PIECE]
    gains = lin_ref[0, ROWS:, :].astype(F32)
    for t in range(1, 8):
        gains = gains + lin_ref[t, ROWS:, :].astype(F32)
    out_ref[NB - 1] = jnp.zeros((4 * PIECE, ATT_WIDTH), BF)
    at = pl.multiple_of(index_ref[0] * PIECE, PIECE)
    out_ref[NB - 1, pl.ds(at, PIECE), 0:OUT_AT] = gains.astype(BF)


def finish_feed_kernel(in_ref, gate_ref, up_ref, down_ref):
    for piece in range(NB - 1):
        at = slice(piece * PIECE, (piece + 1) * PIECE)
        parts = []
        for w in range(4):
            for s in range(2):
                source = 4 * s + w
                parts.append(in_ref[piece, source * PIECE : (source + 1) * PIECE, :].astype(F32))
        gate_ref[at, :] = jnp.concatenate([part[:, :UNITS] for part in parts], axis=1)
        up_ref[at, :] = jnp.concatenate([part[:, UNITS:] for part in parts], axis=1)
    each = UNITS // NB
    for piece in range(NB):
        for s in range(2):
            at = 8 * PIECE + s * (FF_ROWS - 4 * PIECE)
            rows = in_ref[piece, at : at + FF_ROWS - 4 * PIECE, :].astype(F32)
            tail = rows[each:DOWN_ROWS]
            tail = jnp.concatenate([tail[:, :UNITS], tail[:, UNITS:]], axis=0)
            to = s * UNITS + piece * each
            down_ref[to : to + each, :] = jnp.concatenate([rows[:each], tail], axis=1)


def finish_attend_kernel(in_ref, q_ref, k_ref, v_ref, o_ref, gain_ref):
    for piece in range(NB - 1):
        at = slice(piece * PIECE, (piece + 1) * PIECE)
        parts = [in_ref[piece, t * PIECE : (t + 1) * PIECE, :].astype(F32) for t in range(8)]
        lin = jnp.concatenate([part[:, :QKV_PART] for part in parts], axis=1)
        q_ref[at, :] = lin[:, : H * HD]
        k_ref[at, :] = lin[:, H * HD : (H + KV) * HD]
        v_ref[at, :] = lin[:, (H + KV) * HD :]
        o_ref[at, :] = jnp.concatenate(
            [part[:, OUT_AT : OUT_AT + OUT_PART] for part in parts], axis=1
        )
    sides = []
    for side in range(2):
        total = None
        for w in range(4):
            t = 2 * w + side
            own = in_ref[NB - 1, t * PIECE : (t + 1) * PIECE, 0:OUT_PART].astype(F32)[:8]
            total = own if total is None else total + own
        sides.append(total)
    gain_ref[...] = jnp.concatenate(sides, axis=1)


def whole(shape):
    return pl.BlockSpec(shape, lambda i: (0,) * len(shape))


def layer_of(layer, shape):
    return pl.BlockSpec((None,) + shape, lambda i: (layer,) + (0,) * len(shape))


def call(kernel, in_specs, outs, args, scratch=(), flops=0, moved=8_000_000, exps=0):
    return pl.pallas_call(
        kernel,
        grid=(1,),
        in_specs=in_specs,
        out_specs=[whole(shape) for shape, _ in outs],
        out_shape=[jax.ShapeDtypeStruct(shape, dtype) for shape, dtype in outs],
        scratch_shapes=list(scratch),
        compiler_params=pltpu.CompilerParams(vmem_limit_bytes=VMEM_BYTES),
        cost_estimate=pl.CostEstimate(flops=flops, bytes_accessed=moved, transcendentals=exps),
    )(*args)


SMEM = pl.BlockSpec(memory_space=pltpu.SMEM)
HBM = pl.BlockSpec(memory_space=pl.ANY)
PACK = (NB, ROWS + ROWS // 2, 2 * HD)
HEADS = (NB, ROWS // 2, 2 * HD)
GROUPS = ((0,), (1, 3), (2,))


def exchange(array):
    return lax.all_to_all(array, "blk", 0, 0, tiled=True)


def exchange_eight(array):
    return lax.all_to_all(array, EIGHT, 0, 0, tiled=True)


def sum_over_blocks(pieces):
    return jnp.sum(exchange(pieces).astype(F32), axis=0).astype(BF)


def weight_scratch(width):
    return [
        pltpu.VMEM((D, width), BF),
        pltpu.VMEM((4, 16, 256), BF),
        pltpu.SemaphoreType.DMA((2, 8)),
    ]


def body(
    tokens,
    cotangent,
    span_order,
    norm_one,
    w_query,
    w_key,
    w_value,
    w_out,
    norm_two,
    w_gate,
    w_up,
    w_down,
):
    section = lax.axis_index("section")
    shard = lax.axis_index("wshard")
    core = shard % 2
    y = 2 * (shard // 2) + section

    owners = []
    for step in range(4):
        there = (y + step) % 4
        for flip in range(2):
            owners += [there % 2, 2 * (there // 2) + (core ^ flip)]
    table = jnp.stack(owners).astype(jnp.int32)

    def with_gain(weight, gain):
        row = jnp.pad(gain[None], ((0, 15), (0, weight.shape[1] - SHARE)))
        return jnp.concatenate([weight, row], axis=0)

    first = jnp.concatenate([w_query[0], w_key[0], w_value[0]], axis=1)
    wqkv = sum(gather_eight(with_gain(first, norm_one[0])), [])
    out_block, gate_block, up_block, down_block = lax.optimization_barrier(
        (w_out[0], w_gate[0], w_up[0], w_down[0], wqkv[4])
    )[:4]
    wout = sum(gather_eight(with_gain(out_block, norm_two[0])), [])

    pieces = jnp.concatenate(
        [gate_block.reshape(SHARE, 4, 2, UNITS), up_block.reshape(SHARE, 4, 2, UNITS)], axis=3
    ).transpose(2, 1, 0, 3)
    wgu = exchange_eight(pieces.reshape(8, SHARE, 2 * UNITS)).reshape(2, D, 2 * UNITS)
    halves = down_block.reshape(2, UNITS, D)
    kept = lax.dynamic_index_in_dim(halves, section, 0, keepdims=False)
    sent = lax.dynamic_index_in_dim(halves, 1 - section, 0, keepdims=False)
    other = swap_section(sent)
    wdown = jnp.where(section == 0, jnp.stack([kept, other]), jnp.stack([other, kept]))

    block_index = lax.axis_index("blk")
    own_block = lax.dynamic_index_in_dim(span_order, block_index, 0, keepdims=False)
    positions = own_block * ROWS + jnp.arange(ROWS, dtype=jnp.int32)
    exponent = jnp.arange(HD // 2, dtype=F32) * (2.0 / HD)
    angles = positions.astype(F32)[:, None] * (rope_base ** (-exponent))[None, :]
    angles = jnp.concatenate([angles, angles], axis=-1)
    cosine, sine = jnp.cos(angles), jnp.sin(angles)
    slots = jnp.arange(NB, dtype=jnp.int32)
    place = jnp.sum(
        jnp.where(span_order[None, :] == slots[:, None], slots[None, :], 0), axis=1
    ).astype(jnp.int32)

    angle = whole((ROWS, HD))
    rows = whole((ROWS, D))
    row_scratch = pltpu.VMEM((LEN, HD), BF)
    weights = [HBM] * 8
    feed_weights = [(D, 2 * UNITS), (UNITS, D)]

    def forward(layer, x):
        h1, packed = call(
            functools.partial(project_kernel, layer),
            [SMEM, rows, angle, angle] + weights,
            [((ROWS, D), BF), (PACK, BF)],
            (table, x, cosine, sine, *wqkv),
            weight_scratch(QKV),
        )
        packed = exchange(packed)
        heads, lse = call(
            attend_kernel,
            [SMEM, whole(PACK)],
            [(HEADS, BF), ((8, LEN), F32)],
            (place, packed),
            [row_scratch] * 3,
            flops=1_000_000_000,
        )
        heads = exchange(heads)
        mixed, x2, h2 = call(
            functools.partial(mix_kernel, layer),
            [SMEM, whole(HEADS), rows] + weights,
            [((ROWS, D), BF), ((ROWS, D), F32), ((ROWS, D), BF)],
            (table, heads, x, *wout),
            weight_scratch(D),
        )
        found = gather_eight(h2)
        kept_ff, parts = [], [None] * 4
        for group in GROUPS:
            blocks = sum([found[step] for step in group], [])
            count = len(blocks)
            lin, hidden, *part = call(
                functools.partial(feed_kernel, count),
                [rows] * count + [layer_of(layer, shape) for shape in feed_weights],
                [((count * ROWS, 2 * UNITS), F32), ((count * ROWS, UNITS), BF)]
                + [((ROWS, D), BF)] * count,
                (*blocks, wgu, wdown),
                flops=500_000_000,
            )
            kept_ff.append((blocks, lin, hidden))
            for number, step in enumerate(group):
                parts[step] = part[2 * number : 2 * number + 2]
        y_out = x2 + scatter_eight(parts)
        both = lax.all_gather(jnp.concatenate([h1, mixed], axis=0), EIGHT, axis=0)
        return y_out, (x, both, packed, lse, x2, kept_ff)

    def backward(layer, dy, kept_state):
        x, both, packed, lse, x2, kept_ff = kept_state
        found = gather_eight(dy.astype(BF))
        parts, branches, lin_grads = [None] * 4, [], []
        for group, (_, lin, _) in zip(GROUPS, kept_ff):
            blocks = sum([found[step] for step in group], [])
            count = len(blocks)
            lin_grad, *part = call(
                functools.partial(feed_back_kernel, count),
                [rows] * count
                + [whole((count * ROWS, 2 * UNITS))]
                + [layer_of(layer, shape) for shape in feed_weights],
                [((count * ROWS, 2 * UNITS), BF)] + [((ROWS, D), BF)] * count,
                (*blocks, lin, wgu, wdown),
                flops=500_000_000,
            )
            branches += blocks
            lin_grads.append(lin_grad)
            for number, step in enumerate(group):
                parts[step] = part[2 * number : 2 * number + 2]
        dh2 = scatter_eight(parts)
        normed = sum([item[0] for item in kept_ff], [])
        sizes = [len(item[0]) * ROWS for item in kept_ff]
        grad_ff = call(
            feed_grads_kernel,
            [rows] * 16
            + [whole((size, 2 * UNITS)) for size in sizes]
            + [whole((size, UNITS)) for size in sizes],
            [((NB, FF_ROWS, 2 * UNITS), BF)],
            (*normed, *branches, *lin_grads, *[item[2] for item in kept_ff]),
            flops=2_000_000_000,
        )[0]
        dx2, heads_grad, e_parts, grad_gain_two = call(
            functools.partial(mix_back_kernel, layer),
            [SMEM, rows, rows, rows] + weights,
            [((ROWS, D), F32), (HEADS, BF), ((8, ROWS, 128), BF), ((1, D), F32)],
            (table, dy, dh2, x2, *wout),
            weight_scratch(D),
        )
        heads_grad = exchange(heads_grad)
        e_all = exchange_eight(e_parts)
        packed_grad = call(
            attend_back_kernel,
            [SMEM, whole(PACK), whole(HEADS), whole((8, LEN))],
            [(PACK, BF)],
            (place, packed, heads_grad, lse),
            [row_scratch] * 4
            + [pltpu.VMEM((HD, LEN), BF)]
            + [pltpu.VMEM((LEN, HD), F32)] * 3,
            flops=3_000_000_000,
        )[0]
        packed_grad = exchange(packed_grad)
        dx, lin_parts = call(
            functools.partial(project_back_kernel, layer),
            [SMEM, whole(PACK), rows, rows, angle, angle, whole((1, D))] + weights,
            [((ROWS, D), F32), ((8, ROWS + 16, 256), BF)],
            (table, packed_grad, dx2, x, cosine, sine, grad_gain_two, *wqkv),
            weight_scratch(QKV),
        )
        lin_all = exchange_eight(lin_parts)
        grad_att = call(
            attend_grads_kernel,
            [
                SMEM,
                whole((8, 2 * ROWS, D)),
                whole((8, ROWS + 16, 256)),
                whole((8, ROWS, 128)),
            ],
            [((NB, 4 * PIECE, ATT_WIDTH), BF)],
            (gain_owner, both, lin_all, e_all),
            flops=1_000_000_000,
        )[0]
        return dx, sum_over_blocks(grad_ff), sum_over_blocks(grad_att)

    gain_owner = ((4 * section + shard) // 2).astype(jnp.int32).reshape(1)
    x0 = lax.dynamic_index_in_dim(tokens[:, 0], section, 0, keepdims=False).astype(F32)
    cot = lax.dynamic_index_in_dim(cotangent[:, 0], section, 0, keepdims=False).astype(F32)
    y0, kept0 = forward(0, x0)
    y0 = y0.astype(BF)
    y1, kept1 = forward(1, y0.astype(F32))
    y1 = y1.astype(BF)
    dx1, ff1, att1 = backward(1, cot, kept1)
    dx0, ff0, att0 = backward(0, dx1.astype(BF).astype(F32), kept0)

    def by_section(of_first, of_second):
        own = jnp.where(section == 0, of_first, of_second)
        other = swap_section(jnp.where(section == 0, of_second, of_first))
        return jnp.where(section == 0, jnp.stack([own, other]), jnp.stack([other, own]))

    layer_outputs = by_section(y0, y1)
    input_grads = by_section(dx0, dx1)

    upper = 4 * PIECE
    spread = jnp.stack([ff0[:upper], ff1[:upper]]).reshape(8, PIECE, 2 * UNITS)
    spread = exchange_eight(spread).reshape(8 * PIECE, 2 * UNITS)
    lower = by_section(ff0[upper:], ff1[upper:]).reshape(-1, 2 * UNITS)
    found = lax.all_gather(jnp.concatenate([spread, lower], axis=0), "blk", axis=0)
    grad_gate, grad_up, grad_down = call(
        finish_feed_kernel,
        [whole(found.shape)],
        [((SHARE, FF), F32), ((SHARE, FF), F32), ((FF // 4, D), F32)],
        (found,),
    )
    spread = jnp.stack([att0, att1]).reshape(8, PIECE, ATT_WIDTH)
    spread = exchange_eight(spread).reshape(1, 8 * PIECE, ATT_WIDTH)
    found = exchange(jnp.broadcast_to(spread, (NB, 8 * PIECE, ATT_WIDTH)))
    grad_query, grad_key, grad_value, grad_out, gain_grads = call(
        finish_attend_kernel,
        [whole(found.shape)],
        [
            ((SHARE, H * HD), F32),
            ((SHARE, KV * HD), F32),
            ((SHARE, KV * HD), F32),
            ((SHARE, D), F32),
            ((8, SHARE), F32),
        ],
        (found,),
    )
    return (
        layer_outputs[None, :, None],
        input_grads[None, :, None],
        gain_grads[0][None],
        grad_query[None],
        grad_key[None],
        grad_value[None],
        grad_out[None],
        gain_grads[1][None],
        grad_gate[None],
        grad_up[None],
        grad_down[None],
    )


def solution(mesh):
    return jax.shard_map(
        body,
        mesh=mesh,
        in_specs=(
            P(None, "wshard", "blk", None),
            P(None, "wshard", "blk", None),
            P(),
            P("section", "wshard"),
            P("section", "wshard", None),
            P("section", "wshard", None),
            P("section", "wshard", None),
            P("section", "wshard", None),
            P("section", "wshard"),
            P("section", "wshard", None),
            P("section", "wshard", None),
            P("section", "wshard", None),
        ),
        out_specs=(
            P("section", None, "wshard", "blk", None),
            P("section", None, "wshard", "blk", None),
            P("section", "wshard"),
            P("section", "wshard", None),
            P("section", "wshard", None),
            P("section", "wshard", None),
            P("section", "wshard", None),
            P("section", "wshard"),
            P("section", "wshard", None),
            P("section", "wshard", None),
            P("section", "wshard", None),
        ),
        check_vma=False,
    )
```

time: 1760 us -> 741 us (0.42)
  waiting for transfers between devices: 1150 us -> 239 us
  matrix products: 318 us -> 0 us
  Pallas kernels: 0 us -> 160 us
  starting transfers between devices: 12.4 us -> 146 us
  other arithmetic: 99.1 us -> 32.3 us
    all_gather x17 -> x3, waiting for transfers between devices: 477 us -> 0.01 us  [the longest x2 0.01 us: forward(): both = lax.all_gather(jnp.concatenate([h1, mixed], axis=0), EIGHT, axis=0)]
    unnamed x40 -> x3, waiting for transfers between devices: 417 us -> 0.05 us
    dot_general x84 -> x0, matrix products: 318 us -> none  [the longest x6 49.6 us: attention_scores(): jnp.einsum('qkgd,skd->kgqs', grouped, whole_keys.reshape(-1, KV, HD), pre...]
    reduce_scatter x4 -> x0, waiting for transfers between devices: 195 us -> none  [body(): lax.psum_scatter(for_sending(grad_sum), 'wshard', scatter_dimension=0, ti...]
    pallas_call x0 -> x30, Pallas kernels: none -> 160 us  [call(): pl.pallas_call(kernel, grid=(1,), in_specs=in_specs, out_specs=[whole(sha...]
    ppermute x4 -> x84, waiting for transfers between devices: 5.6 us -> 164 us  [the longest x80 147 us: hop(): return lax.ppermute(array, EIGHT, ring_pairs(step, flip))]
    all_to_all x0 -> x5, blocking collectives: none -> 80.4 us  [the longest x4 65 us: exchange(): return lax.all_to_all(array, 'blk', 0, 0, tiled=True)]
    all_to_all x0 -> x15, waiting for transfers between devices: none -> 74.8 us  [the longest x9 63.2 us: exchange(): return lax.all_to_all(array, 'blk', 0, 0, tiled=True)]
  transfers between devices with their start and end apart: 35 -> 102, of which waited for: 30 -> 41; matrix products, arithmetic and copies ran while one was open for 22% -> 9% of each run, Pallas kernels for 0% -> 20%
where the time goes in v1:
time: 741 us; the launch traced here: 730 us
  waiting for transfers between devices  239 us (32%)
  Pallas kernels  160 us (22%)
  starting transfers between devices  146 us (20%)
  blocking collectives  80.4 us (11%)
  local copies, waits for them, and re-layouts  56.3 us (8%)
  other arithmetic  32.3 us (4%)
  between operations  16.3 us (2%)
    pallas_call x30, Pallas kernels, call(): pl.pallas_call(kernel, grid=(1,), in_specs=in_specs, out_specs=[whole(sha...  160 us
    ppermute x80, waiting for transfers between devices, hop(): return lax.ppermute(array, EIGHT, ring_pairs(step, flip))  147 us
    ppermute x80, starting transfers between devices, hop(): return lax.ppermute(array, EIGHT, ring_pairs(step, flip))  73.8 us
    all_to_all x4, blocking collectives, exchange(): return lax.all_to_all(array, 'blk', 0, 0, tiled=True)  65 us
    all_to_all x9, waiting for transfers between devices, exchange(): return lax.all_to_all(array, 'blk', 0, 0, tiled=True)  63.2 us
    all_to_all x9, starting transfers between devices, exchange(): return lax.all_to_all(array, 'blk', 0, 0, tiled=True)  41.3 us
    unnamed x168, local copies, waits for them, and re-layouts  27.4 us
    all_to_all x6, starting transfers between devices, exchange_eight(): return lax.all_to_all(array, EIGHT, 0, 0, tiled=True)  25.7 us
  transfers between devices with their start and end apart: 102, of which 41 were waited for; matrix products, arithmetic and copies ran while one was open for 9% of the time, Pallas kernels for 20%

profile of v1, /device:TPU:0, one launch (start us, length us, event | category | flops | bytes accessed | tf_op | source)
XLA Modules:
  0.0 729.9 jit_solution(6877409663298275161)
XLA Ops:
  15.2 18.4 %collective-permute-done.3 = bf16[256,1600]{0,1:T(8,128)(2,1)} collective-permute-done((bf16[256,1600]{0,1:T(8,128)(2,1)}, bf16[256,1600]{0,1:T(8,128)(2,1)}, u32[]{:S(2)}, u32[]{:S(2)}) %collective-permute-start.3) | collective-permute-done | bytes 819232 | tf_op jit(solution)/shard_map/ppermute | solution.py:49
  49.4 6.3 collective-permute-done.5
  72.6 6.0 shard_map.203
  78.5 7.9 %all-to-all-start = ((bf16[16,192,128]{2,1,0:T(8,128)(2,1)}), bf16[16,192,128]{2,1,0:T(8,128)(2,1)}, u32[]{:S(2)}, u32[]{:S(2)}) async-start(bf16[16,192,128]{2,1,0:T(8,128)(2,1)} %get-tuple-element.99), calls=%async_computation | async-start | bytes 1572864 | tf_op jit(solution)/shard_map/all_to_all | solution.py:459
  90.5 5.5 collective-permute-done.12
  101.3 8.1 %shard_map.204 = (bf16[16,64,128]{2,1,0:T(8,128)(2,1)}, f32[8,2048]{1,0:T(8,128)}) custom-call(s32[16]{0:T(128)} %select_reduce_fusion.place_ref, bf16[16,192,128]{2,1,0:T(8,128)(2,1)} %all-to-all-done.in_ref), custom_call_target="tpu_custom_call" | custom-call | flops 1000000000 | bytes 8000000 | tf_op jit(solution)/shard_map/pallas_call | solution.py:439
  113.0 8.5 %all-to-all-done.1.in_ref = bf16[16,64,128]{2,1,0:T(8,128)(2,1)S(1)} async-done(((bf16[16,64,128]{2,1,0:T(8,128)(2,1)}), bf16[16,64,128]{2,1,0:T(8,128)(2,1)S(1)}, u32[]{:S(2)}, u32[]{:S(2)}) %all-to-all-start.1) | async-done | bytes 262176 | tf_op jit(solution)/shard_map/all_to_all | solution.py:459
  147.4 48.5 %collective-permute-done.21.refs_2_.refs_4_ = bf16[128,960]{1,0:T(8,128)(2,1)S(1)} collective-permute-done((bf16[128,960]{1,0:T(8,128)(2,1)}, bf16[128,960]{1,0:T(8,128)(2,1)S(1)}, u32[]{:S(2)}, u32[]{:S(2)}) %collective-permute-start.21) | collective-permute-done | bytes 245792 | tf_op jit(solution)/shard_map/ppermute | solution.py:49
  244.9 6.0 shard_map.209
  250.9 19.3 %all_to_all.100.in_ref = bf16[16,192,128]{2,1,0:T(8,128)(2,1)} all-to-all(bf16[16,192,128]{2,1,0:T(8,128)(2,1)} %get-tuple-element.115), channel_id=1, replica_groups=mesh['section'=2,'blk'=16,'wshard'=4] {'blk'}, dimensions={0} | all-to-all | bytes 1572864 | tf_op jit(solution)/shard_map/all_to_all | solution.py:459
  270.2 8.1 %shard_map.210 = (bf16[16,64,128]{2,1,0:T(8,128)(2,1)}, f32[8,2048]{1,0:T(8,128)}) custom-call(s32[16]{0:T(128)} %select_reduce_fusion.place_ref, bf16[16,192,128]{2,1,0:T(8,128)(2,1)} %all_to_all.100.in_ref), custom_call_target="tpu_custom_call" | custom-call | flops 1000000000 | bytes 8000000 | tf_op jit(solution)/shard_map/pallas_call | solution.py:439
  285.5 5.1 all-to-all-done.4.in_ref
  344.7 7.1 collective-permute-done.64
  356.6 11.3 %collective-permute-done.65 = bf16[128,960]{1,0:T(8,128)(2,1)S(1)} collective-permute-done((bf16[128,960]{1,0:T(8,128)(2,1)S(1)}, bf16[128,960]{1,0:T(8,128)(2,1)S(1)}, u32[]{:S(2)}, u32[]{:S(2)}) %collective-permute-start.65) | collective-permute-done | bytes 245792 | tf_op jit(solution)/shard_map/ppermute | solution.py:49
  377.4 13.3 %all_to_all.101.do_ref = bf16[16,64,128]{2,1,0:T(8,128)(2,1)} all-to-all(bf16[16,64,128]{2,1,0:T(8,128)(2,1)} %get-tuple-element.138), channel_id=1, replica_groups=mesh['section'=2,'blk'=16,'wshard'=4] {'blk'}, dimensions={0} | all-to-all | bytes 524288 | tf_op jit(solution)/shard_map/all_to_all | solution.py:459
  390.7 10.4 %shard_map.219 = bf16[16,192,128]{2,1,0:T(8,128)(2,1)} custom-call(s32[16]{0:T(128)} %select_reduce_fusion.place_ref, bf16[16,192,128]{2,1,0:T(8,128)(2,1)} %all_to_all.100.in_ref, bf16[16,64,128]{2,1,0:T(8,128)(2,1)} %all_to_all.101.do_ref, f32[8,2048]{1,0:T(8,128)} %get-tuple-element.139.lse_ref), custom_call_target="tpu_custom_call" | custom-call | flops 3000000000 | bytes 8000000 | tf_op jit(solution)/shard_map/pallas_call | solution.py:439
  404.7 6.6 shard_map.231
  421.1 6.6 shard_map.220
  458.4 6.5 shard_map.230
  464.9 7.7 %all-to-all-start.17 = ((bf16[16,96,640]{2,1,0:T(8,128)(2,1)}), bf16[16,96,640]{2,1,0:T(8,128)(2,1)}, u32[]{:S(2)}, u32[]{:S(2)}) async-start(bf16[16,96,640]{2,1,0:T(8,128)(2,1)} %shard_map.230), calls=%async_computation.17 | async-start | bytes 3932160 | tf_op jit(solution)/shard_map/all_to_all | solution.py:459
  475.9 29.1 %all-to-all-done.17 = bf16[16,96,640]{2,1,0:T(8,128)(2,1)} async-done(((bf16[16,96,640]{2,1,0:T(8,128)(2,1)}), bf16[16,96,640]{2,1,0:T(8,128)(2,1)}, u32[]{:S(2)}, u32[]{:S(2)}) %all-to-all-start.17) | async-done | bytes 1966112 | tf_op jit(solution)/shard_map/all_to_all | solution.py:459
  507.9 6.1 all-to-all-start.19
  524.4 5.4 collective-permute-done.81
  538.7 12.9 %all_to_all.102.do_ref = bf16[16,64,128]{2,1,0:T(8,128)(2,1)} all-to-all(bf16[16,64,128]{2,1,0:T(8,128)(2,1)} %get-tuple-element.154), channel_id=1, replica_groups=mesh['section'=2,'blk'=16,'wshard'=4] {'blk'}, dimensions={0} | all-to-all | bytes 524288 | tf_op jit(solution)/shard_map/all_to_all | solution.py:459
  555.0 10.4 %shard_map.225 = bf16[16,192,128]{2,1,0:T(8,128)(2,1)} custom-call(s32[16]{0:T(128)} %select_reduce_fusion.place_ref, bf16[16,192,128]{2,1,0:T(8,128)(2,1)} %all-to-all-done.in_ref, bf16[16,64,128]{2,1,0:T(8,128)(2,1)} %all_to_all.102.do_ref, f32[8,2048]{1,0:T(8,128)} %get-tuple-element.155.lse_ref), custom_call_target="tpu_custom_call" | custom-call | flops 3000000000 | bytes 8000000 | tf_op jit(solution)/shard_map/pallas_call | solution.py:439
  565.4 19.5 %all_to_all.103.in_ref = bf16[16,192,128]{2,1,0:T(8,128)(2,1)} all-to-all(bf16[16,192,128]{2,1,0:T(8,128)(2,1)} %shard_map.225), channel_id=1, replica_groups=mesh['section'=2,'blk'=16,'wshard'=4] {'blk'}, dimensions={0} | all-to-all | bytes 1572864 | tf_op jit(solution)/shard_map/all_to_all | solution.py:459
  589.8 6.6 shard_map.226
  597.0 15.4 %all_to_all.104.lin_ref = bf16[8,144,256]{2,1,0:T(8,128)(2,1)} all-to-all(bf16[8,144,256]{2,1,0:T(8,128)(2,1)} %get-tuple-element.161), channel_id=1, replica_groups=mesh['section'=2,'blk'=16,'wshard'=4] {'section','wshard'}, dimensions={0} | all-to-all | bytes 1179648 | tf_op jit(solution)/shard_map/all_to_all | solution.py:463
  638.2 5.8 all-to-all-done.11
  655.4 5.3 all-to-all-done.14
  681.7 17.0 %collective-permute-done.49 = bf16[128,960]{1,0:T(8,128)(2,1)S(1)} collective-permute-done((bf16[128,960]{1,0:T(8,128)(2,1)S(1)}, bf16[128,960]{1,0:T(8,128)(2,1)S(1)}, u32[]{:S(2)}, u32[]{:S(2)}) %collective-permute-start.49) | collective-permute-done | bytes 245792 | tf_op jit(solution)/shard_map/ppermute | solution.py:53
  713.9 6.0 shard_map.232
  (488 shorter events, 356.6 us)
Async XLA Ops:
  12.0 21.7 %collective-permute-start.3 = (bf16[256,1600]{0,1:T(8,128)(2,1)}, bf16[256,1600]{0,1:T(8,128)(2,1)}, u32[]{:S(2)}, u32[]{:S(2)}) collective-permute-start(bf16[256,1600]{0,1:T(8,128)(2,1)} %copy.105), channel_id=1, source_target_pairs={{0,64},{1,65},{64,2},{65,3},{2,66},{3,67},{66,0},{67,1},{4,68},{5,... | collective-permute-start | bytes 2457608 | tf_op jit(solution)/shard_map/ppermute | solution.py:49
  13.7 27.7 %collective-permute-start.1 = (bf16[256,1600]{0,1:T(8,128)(2,1)}, bf16[256,1600]{0,1:T(8,128)(2,1)}, u32[]{:S(2)}, u32[]{:S(2)}) collective-permute-start(bf16[256,1600]{0,1:T(8,128)(2,1)} %copy.105), channel_id=1, source_target_pairs={{0,66},{1,67},{64,0},{65,1},{2,64},{3,65},{66,2},{67,3},{4,70},{5,... | collective-permute-start | bytes 2457608 | tf_op jit(solution)/shard_map/ppermute | solution.py:49
  36.3 22.1 %collective-permute-start = (bf16[256,1600]{0,1:T(8,128)(2,1)}, bf16[256,1600]{0,1:T(8,128)(2,1)}, u32[]{:S(2)}, u32[]{:S(2)}) collective-permute-start(bf16[256,1600]{0,1:T(8,128)(2,1)} %copy.105), channel_id=1, source_target_pairs={{0,1},{1,0},{64,65},{65,64},{2,3},{3,2},{66,67},{67,66},{4,5},{5,4... | collective-permute-start | bytes 2457608 | tf_op jit(solution)/shard_map/ppermute | solution.py:49
  46.0 19.9 %collective-permute-start.2 = (bf16[256,1600]{0,1:T(8,128)(2,1)}, bf16[256,1600]{0,1:T(8,128)(2,1)}, u32[]{:S(2)}, u32[]{:S(2)}) collective-permute-start(bf16[256,1600]{0,1:T(8,128)(2,1)} %collective-permute-done.1), channel_id=1, source_target_pairs={{0,1},{1,0},{64,65},{65,64},{2,3},{3,2},{66,67},{67,66},{4,5},{5,4... | collective-permute-start | bytes 2457608 | tf_op jit(solution)/shard_map/ppermute | solution.py:49
  46.3 21.8 %collective-permute-start.7 = (bf16[256,1600]{0,1:T(8,128)(2,1)}, bf16[256,1600]{0,1:T(8,128)(2,1)}, u32[]{:S(2)}, u32[]{:S(2)}) collective-permute-start(bf16[256,1600]{0,1:T(8,128)(2,1)} %collective-permute-done.3), channel_id=1, source_target_pairs={{0,1},{1,0},{64,65},{65,64},{2,3},{3,2},{66,67},{67,66},{4,5},{5,4... | collective-permute-start | bytes 2457608 | tf_op jit(solution)/shard_map/ppermute | solution.py:49
  57.2 29.3 %collective-permute-start.11 = (bf16[256,960]{1,0:T(8,128)(2,1)S(1)}, bf16[256,960]{1,0:T(8,128)(2,1)S(1)}, u32[]{:S(2)}, u32[]{:S(2)}) collective-permute-start(bf16[256,960]{1,0:T(8,128)(2,1)S(1)} %fusion.3.refs_0_), channel_id=1, source_target_pairs={{0,64},{1,65},{64,2},{65,3},{2,66},{3,67},{66,0},{67,1},{4,68},{5,... | collective-permute-start | bytes 1474568 | tf_op jit(solution)/shard_map/ppermute | solution.py:49
  58.4 28.2 %collective-permute-start.9 = (bf16[256,960]{1,0:T(8,128)(2,1)S(1)}, bf16[256,960]{1,0:T(8,128)(2,1)S(1)}, u32[]{:S(2)}, u32[]{:S(2)}) collective-permute-start(bf16[256,960]{1,0:T(8,128)(2,1)S(1)} %fusion.3.refs_0_), channel_id=1, source_target_pairs={{0,66},{1,67},{64,0},{65,1},{2,64},{3,65},{66,2},{67,3},{4,70},{5,... | collective-permute-start | bytes 1474568 | tf_op jit(solution)/shard_map/ppermute | solution.py:49
  78.5 22.7 %all-to-all-start = ((bf16[16,192,128]{2,1,0:T(8,128)(2,1)}), bf16[16,192,128]{2,1,0:T(8,128)(2,1)}, u32[]{:S(2)}, u32[]{:S(2)}) async-start(bf16[16,192,128]{2,1,0:T(8,128)(2,1)} %get-tuple-element.99), calls=%async_computation | async-start | bytes 1572864 | tf_op jit(solution)/shard_map/all_to_all | solution.py:459
  89.9 23.1 %collective-permute-start.8 = (bf16[256,960]{1,0:T(8,128)(2,1)S(1)}, bf16[256,960]{1,0:T(8,128)(2,1)S(1)}, u32[]{:S(2)}, u32[]{:S(2)}) collective-permute-start(bf16[256,960]{1,0:T(8,128)(2,1)S(1)} %fusion.3.refs_0_), channel_id=1, source_target_pairs={{0,1},{1,0},{64,65},{65,64},{2,3},{3,2},{66,67},{67,66},{4,5},{5,4... | collective-permute-start | bytes 1474568 | tf_op jit(solution)/shard_map/ppermute | solution.py:49
  89.9 23.1 %collective-permute-start.10 = (bf16[256,960]{1,0:T(8,128)(2,1)S(1)}, bf16[256,960]{1,0:T(8,128)(2,1)}, u32[]{:S(2)}, u32[]{:S(2)}) collective-permute-start(bf16[256,960]{1,0:T(8,128)(2,1)S(1)} %collective-permute-done.9.refs_2_), channel_id=1, source_target_pairs={{0,1},{1,0},{64,65},{65,64},{2,3},{3,2},{66,67},{67,66},{4,5},{5,4... | collective-permute-start | bytes 1474568 | tf_op jit(solution)/shard_map/ppermute | solution.py:49
  90.4 22.6 %collective-permute-start.15 = (bf16[256,960]{1,0:T(8,128)(2,1)S(1)}, bf16[256,960]{1,0:T(8,128)(2,1)}, u32[]{:S(2)}, u32[]{:S(2)}) collective-permute-start(bf16[256,960]{1,0:T(8,128)(2,1)S(1)} %collective-permute-done.11.refs_6_), channel_id=1, source_target_pairs={{0,1},{1,0},{64,65},{65,64},{2,3},{3,2},{66,67},{67,66},{4,5},{5,4... | collective-permute-start | bytes 1474568 | tf_op jit(solution)/shard_map/ppermute | solution.py:49
  96.0 17.0 %collective-permute-start.14 = (bf16[256,960]{1,0:T(8,128)(2,1)S(1)}, bf16[256,960]{1,0:T(8,128)(2,1)}, u32[]{:S(2)}, u32[]{:S(2)}) collective-permute-start(bf16[256,960]{1,0:T(8,128)(2,1)S(1)} %constant_dynamic-update-slice_fusion.2.refs_4_), channel_id=1, source_target_pairs={{0,1},{1,0},{64,65},{65,64},{2,3},{3,2},{66,67},{67,66},{4,5},{5,4... | collective-permute-start | bytes 1474568 | tf_op jit(solution)/shard_map/ppermute | solution.py:49
  112.9 504.2 %all-gather.7.cloned.1.call-start = ((), (), s32[]{:S(2)}) async-start(), calls=%async_computation.20 | async-start | bytes 4718592 | tf_op jit(solution)/shard_map/all_gather | solution.py:585
  133.1 76.3 %all-to-all-start.2 = ((bf16[8,240,640]{2,1,0:T(8,128)(2,1)}), bf16[8,240,640]{2,1,0:T(8,128)(2,1)S(1)}, u32[]{:S(2)}, u32[]{:S(2)}) async-start(bf16[8,240,640]{2,1,0:T(8,128)(2,1)} %bitcast.78), calls=%async_computation.2 | async-start | bytes 4915200 | tf_op jit(solution)/shard_map/all_to_all | solution.py:463
  142.1 60.4 %collective-permute-start.17 = (bf16[320,960]{1,0:T(8,128)(2,1)}, bf16[320,960]{1,0:T(8,128)(2,1)}, u32[]{:S(2)}, u32[]{:S(2)}) collective-permute-start(bf16[320,960]{1,0:T(8,128)(2,1)} %get-tuple-element.249), channel_id=1, source_target_pairs={{0,64},{64,0},{1,65},{65,1},{2,66},{66,2},{3,67},{67,3},{4,68},{68... | collective-permute-start | bytes 1843208 | tf_op jit(solution)/shard_map/ppermute | solution.py:53
  144.1 51.7 %collective-permute-start.21 = (bf16[128,960]{1,0:T(8,128)(2,1)}, bf16[128,960]{1,0:T(8,128)(2,1)S(1)}, u32[]{:S(2)}, u32[]{:S(2)}) collective-permute-start(bf16[128,960]{1,0:T(8,128)(2,1)} %get-tuple-element.103.refs_0_), channel_id=1, source_target_pairs={{0,64},{1,65},{64,2},{65,3},{2,66},{3,67},{66,0},{67,1},{4,68},{5,... | collective-permute-start | bytes 737288 | tf_op jit(solution)/shard_map/ppermute | solution.py:49
  144.2 55.4 %collective-permute-start.19 = (bf16[128,960]{1,0:T(8,128)(2,1)}, bf16[128,960]{1,0:T(8,128)(2,1)S(1)}, u32[]{:S(2)}, u32[]{:S(2)}) collective-permute-start(bf16[128,960]{1,0:T(8,128)(2,1)} %get-tuple-element.103.refs_0_), channel_id=1, source_target_pairs={{0,66},{1,67},{64,0},{65,1},{2,64},{3,65},{66,2},{67,3},{4,70},{5,... | collective-permute-start | bytes 737288 | tf_op jit(solution)/shard_map/ppermute | solution.py:49
  281.9 351.7 %all-gather.9.cloned.1.call-start = ((), (), s32[]{:S(2)}) async-start(), calls=%async_computation.21 | async-start | bytes 4718592 | tf_op jit(solution)/shard_map/all_gather | solution.py:585
  282.3 16.8 %collective-permute-start.52 = (bf16[128,960]{1,0:T(8,128)(2,1)S(1)}, bf16[128,960]{1,0:T(8,128)(2,1)S(1)}, u32[]{:S(2)}, u32[]{:S(2)}) collective-permute-start(bf16[128,960]{1,0:T(8,128)(2,1)S(1)} %bitcast.83), channel_id=1, source_target_pairs={{0,66},{1,67},{64,0},{65,1},{2,64},{3,65},{66,2},{67,3},{4,70},{5,... | collective-permute-start | bytes 737288 | tf_op jit(solution)/shard_map/ppermute | solution.py:49
  310.9 24.1 %collective-permute-start.59 = (bf16[128,960]{1,0:T(8,128)(2,1)S(1)}, bf16[128,960]{1,0:T(8,128)(2,1)}, u32[]{:S(2)}, u32[]{:S(2)}) collective-permute-start(bf16[128,960]{1,0:T(8,128)(2,1)S(1)} %constant_dynamic-update-slice_fusion.8.refs_0_.refs_14_), channel_id=1, source_target_pairs={{0,1},{1,0},{64,65},{65,64},{2,3},{3,2},{66,67},{67,66},{4,5},{5,4... | collective-permute-start | bytes 737288 | tf_op jit(solution)/shard_map/ppermute | solution.py:49
  330.4 26.2 %collective-permute-start.51 = (bf16[128,960]{1,0:T(8,128)(2,1)}, bf16[128,960]{1,0:T(8,128)(2,1)S(1)}, u32[]{:S(2)}, u32[]{:S(2)}) collective-permute-start(bf16[128,960]{1,0:T(8,128)(2,1)} %get-tuple-element.129), channel_id=1, source_target_pairs={{0,1},{1,0},{64,65},{65,64},{2,3},{3,2},{66,67},{67,66},{4,5},{5,4... | collective-permute-start | bytes 737288 | tf_op jit(solution)/shard_map/ppermute | solution.py:49
  417.2 47.7 %all-to-all-start.18 = ((bf16[16,96,640]{2,1,0:T(8,128)(2,1)}), bf16[16,96,640]{2,1,0:T(8,128)(2,1)S(1)}, u32[]{:S(2)}, u32[]{:S(2)}) async-start(bf16[16,96,640]{2,1,0:T(8,128)(2,1)} %shard_map.231), calls=%async_computation.18 | async-start | bytes 3932160 | tf_op jit(solution)/shard_map/all_to_all | solution.py:459
  464.9 40.1 %all-to-all-start.17 = ((bf16[16,96,640]{2,1,0:T(8,128)(2,1)}), bf16[16,96,640]{2,1,0:T(8,128)(2,1)}, u32[]{:S(2)}, u32[]{:S(2)}) async-start(bf16[16,96,640]{2,1,0:T(8,128)(2,1)} %shard_map.230), calls=%async_computation.17 | async-start | bytes 3932160 | tf_op jit(solution)/shard_map/all_to_all | solution.py:459
  473.3 51.1 %collective-permute-start.67 = (bf16[128,960]{1,0:T(8,128)(2,1)}, bf16[128,960]{1,0:T(8,128)(2,1)S(1)}, u32[]{:S(2)}, u32[]{:S(2)}) collective-permute-start(bf16[128,960]{1,0:T(8,128)(2,1)} %get-tuple-element.145), channel_id=1, source_target_pairs={{0,1},{1,0},{64,65},{65,64},{2,3},{3,2},{66,67},{67,66},{4,5},{5,4... | collective-permute-start | bytes 737288 | tf_op jit(solution)/shard_map/ppermute | solution.py:49
  514.1 199.9 %all-gather.11.cloned.1.call-start = ((), (), s32[]{:S(2)}) async-start(), calls=%async_computation.22 | async-start | bytes 4177920 | tf_op jit(solution)/shard_map/all_gather | solution.py:684
  616.4 59.8 %collective-permute-start.34 = (bf16[128,960]{1,0:T(8,128)(2,1)}, bf16[128,960]{1,0:T(8,128)(2,1)}, u32[]{:S(2)}, u32[]{:S(2)}) collective-permute-start(bf16[128,960]{1,0:T(8,128)(2,1)} %get-tuple-element.120), channel_id=1, source_target_pairs={{0,1},{1,0},{64,65},{65,64},{2,3},{3,2},{66,67},{67,66},{4,5},{5,4... | collective-permute-start | bytes 737288 | tf_op jit(solution)/shard_map/ppermute | solution.py:49
  616.6 31.1 %collective-permute-start.39 = (bf16[128,960]{1,0:T(8,128)(2,1)}, bf16[128,960]{1,0:T(8,128)(2,1)}, u32[]{:S(2)}, u32[]{:S(2)}) collective-permute-start(bf16[128,960]{1,0:T(8,128)(2,1)} %get-tuple-element.122), channel_id=1, source_target_pairs={{0,1},{1,0},{64,65},{65,64},{2,3},{3,2},{66,67},{67,66},{4,5},{5,4... | collective-permute-start | bytes 737288 | tf_op jit(solution)/shard_map/ppermute | solution.py:49
  626.7 17.4 %all-to-all-start.11 = ((bf16[16,64,384]{2,1,0:T(8,128)(2,1)}), bf16[16,64,384]{2,1,0:T(8,128)(2,1)S(1)}, u32[]{:S(2)}, u32[]{:S(2)}) async-start(bf16[16,64,384]{2,1,0:T(8,128)(2,1)} %shard_map.227), calls=%async_computation.11 | async-start | bytes 1572864 | tf_op jit(solution)/shard_map/all_to_all | solution.py:459
  650.7 25.5 %collective-permute-start.48 = (bf16[128,960]{1,0:T(8,128)(2,1)}, bf16[128,960]{1,0:T(8,128)(2,1)S(1)}, u32[]{:S(2)}, u32[]{:S(2)}) collective-permute-start(bf16[128,960]{1,0:T(8,128)(2,1)} %pad_maximum_fusion.5), channel_id=1, source_target_pairs={{0,66},{1,67},{64,0},{65,1},{2,64},{3,65},{66,2},{67,3},{4,70},{5,... | collective-permute-start | bytes 737288 | tf_op jit(solution)/shard_map/ppermute | solution.py:49
  672.3 31.2 %all-to-all-start.16 = ((bf16[16,128,384]{2,1,0:T(8,128)(2,1)}), bf16[16,128,384]{2,1,0:T(8,128)(2,1)S(1)}, u32[]{:S(2)}, u32[]{:S(2)}) async-start(bf16[16,128,384]{2,1,0:T(8,128)(2,1)} %broadcast_in_dim.50), calls=%async_computation.16 | async-start | bytes 3145728 | tf_op jit(solution)/shard_map/all_to_all | solution.py:459
  679.4 20.3 %collective-permute-start.82 = (f32[128,960]{1,0:T(8,128)}, f32[128,960]{1,0:T(8,128)S(1)}, u32[]{:S(2)}, u32[]{:S(2)}) collective-permute-start(f32[128,960]{1,0:T(8,128)} %get-tuple-element.251), channel_id=1, source_target_pairs={{0,64},{64,0},{1,65},{65,1},{2,66},{66,2},{3,67},{67,3},{4,68},{68... | collective-permute-start | bytes 1474568 | tf_op jit(solution)/shard_map/ppermute | solution.py:53
  679.8 18.9 %collective-permute-start.49 = (bf16[128,960]{1,0:T(8,128)(2,1)S(1)}, bf16[128,960]{1,0:T(8,128)(2,1)S(1)}, u32[]{:S(2)}, u32[]{:S(2)}) collective-permute-start(bf16[128,960]{1,0:T(8,128)(2,1)S(1)} %broadcast_select_fusion.1), channel_id=1, source_target_pairs={{0,64},{64,0},{1,65},{65,1},{2,66},{66,2},{3,67},{67,3},{4,68},{68... | collective-permute-start | bytes 737288 | tf_op jit(solution)/shard_map/ppermute | solution.py:53
  (146 other events, 1403.6 us)
Sparse Core Ops, SparseCore 0:
  128.5 83.5 all-gather.6
  323.5 58.7 all-gather.8
  521.2 47.2 all-gather.10

commit v2 on v1

--- a/solution.py
+++ b/solution.py
@@ -17,14 +17,14 @@
 LEN = ROWS * NB
 QKV = H * HD + 2 * KV * HD
 UNITS = FF // 8
+WIDE = 1664
 SHARE = D // 4
 PIECE = 16
 QKV_PART = QKV // 8
 OUT_PART = D // 8
 OUT_AT = 256
 ATT_WIDTH = 384
-DOWN_ROWS = 30
-FF_ROWS = 96
+FF_WIDTH = D
 TILE = 256
 
 EIGHT = ("section", "wshard")
@@ -125,6 +125,36 @@
 
 def unfold(block):
     return jnp.concatenate([block[:, :HD], block[:, HD:]], axis=0)
+
+
+def pack_attend_kernel(q_ref, k_ref, v_ref, o_ref, one_ref, two_ref, first_ref, second_ref):
+    gap = jnp.zeros((SHARE, WIDE - QKV), BF)
+    keys, values = jnp.transpose(k_ref[...]), jnp.transpose(v_ref[...])
+    first_ref[0:SHARE, :] = jnp.concatenate([q_ref[...], keys, values, gap], axis=1)
+    second_ref[0:SHARE, :] = o_ref[...]
+    for ref, gain in ((first_ref, one_ref), (second_ref, two_ref)):
+        row = jnp.concatenate([gain[...], jnp.zeros((15, SHARE), BF)], axis=0)
+        width = ref.shape[1]
+        ref[SHARE:, :] = jnp.concatenate([row, jnp.zeros((16, width - SHARE), BF)], axis=1)
+
+
+def pack_feed_kernel(table_ref, gate_ref, up_ref, down_ref, pieces_ref, kept_ref, sent_ref):
+    for s in range(2):
+        for w in range(4):
+            at = 2 * w + s
+            at = slice(at * UNITS, (at + 1) * UNITS)
+            pieces_ref[4 * s + w] = jnp.concatenate([gate_ref[:, at], up_ref[:, at]], axis=1)
+    first, second = down_ref[:, :UNITS], down_ref[:, UNITS:]
+
+    @pl.when(table_ref[0] == 0)
+    def _():
+        kept_ref[...] = first
+        sent_ref[...] = second
+
+    @pl.when(table_ref[0] == 1)
+    def _():
+        kept_ref[...] = second
+        sent_ref[...] = first
 
 
 def load_blocks(table_ref, layer, blocks, weight_ref, gain_ref, sems):
@@ -166,7 +196,7 @@
     h = (x * norm_factor(x) * gain).astype(BF)
     h_ref[...] = h
     cosine, sine = cos_ref[...], sin_ref[...]
-    lin = dot(h, w_ref[...])
+    lin = dot(h, w_ref[:, :QKV])
 
     def head(at):
         return lin[:, at * HD : (at + 1) * HD]
@@ -301,7 +331,7 @@
         keys.append(rotate_back(pair[:, :HD], cosine, sine).astype(BF))
         values.append(pair[:, HD:].astype(BF))
     lin_grad = jnp.concatenate(queries + keys + values, axis=1)
-    part, grad_gain = norm_backward(x_ref[...], gain, against(lin_grad, w_ref[...]))
+    part, grad_gain = norm_backward(x_ref[...], gain, against(lin_grad, w_ref[:, :QKV]))
     dx_ref[...] = dx2_ref[...] + part
     gains = jnp.concatenate([grad_gain, gg_ref[...], jnp.zeros((14, D), F32)], axis=0).astype(BF)
     for index in range(8):
@@ -311,23 +341,25 @@
         lin_ref[index, ROWS:, OUT_PART:] = jnp.zeros((16, 256 - OUT_PART), BF)
 
 
-def feed_kernel(count, *refs):
+def feed_kernel(count, layer, table_ref, *refs):
     normed = jnp.concatenate([ref[...] for ref in refs[:count]], axis=0)
-    wgu_ref, wd_ref, lin_ref, hidden_ref = refs[count : count + 4]
+    wgu_ref, kept_ref, other_ref, lin_ref, hidden_ref = refs[count : count + 5]
     lin = dot(normed, wgu_ref[...])
     lin_ref[...] = lin
     gate, up = lin[:, :UNITS], lin[:, UNITS:]
     hidden = (gate * jax.nn.sigmoid(gate) * up).astype(BF)
     hidden_ref[...] = hidden
-    part = dot(hidden, wd_ref[...]).astype(BF)
-    for index, ref in enumerate(refs[count + 4 :]):
+    down = jnp.where(table_ref[0] == layer, kept_ref[...], other_ref[...])
+    part = against(hidden, down).astype(BF)
+    for index, ref in enumerate(refs[count + 5 :]):
         ref[...] = part[index * ROWS : (index + 1) * ROWS]
 
 
-def feed_back_kernel(count, *refs):
+def feed_back_kernel(count, layer, table_ref, *refs):
     branch = jnp.concatenate([ref[...] for ref in refs[:count]], axis=0)
-    lin_ref, wgu_ref, wd_ref, grad_ref = refs[count : count + 4]
-    hidden_grad = against(branch, wd_ref[...])
+    lin_ref, wgu_ref, kept_ref, other_ref, grad_ref = refs[count : count + 5]
+    down = jnp.where(table_ref[0] == layer, kept_ref[...], other_ref[...])
+    hidden_grad = dot(branch, down)
     gate, up = lin_ref[:, :UNITS], lin_ref[:, UNITS:]
     sig = jax.nn.sigmoid(gate)
     up_grad = hidden_grad * (gate * sig)
@@ -335,7 +367,7 @@
     lin_grad = jnp.concatenate([gate_grad, up_grad], axis=1).astype(BF)
     grad_ref[...] = lin_grad
     part = against(lin_grad, wgu_ref[...]).astype(BF)
-    for index, ref in enumerate(refs[count + 4 :]):
+    for index, ref in enumerate(refs[count + 5 :]):
         ref[...] = part[index * ROWS : (index + 1) * ROWS]
 
 
@@ -346,28 +378,23 @@
     hidden = jnp.concatenate([ref[...] for ref in refs[19:22]], axis=0)
     out_ref = refs[22]
     gate_up = across(normed, lin_grad).astype(BF)
+    down = across(branch, hidden).astype(BF)
     for piece in range(NB - 1):
-        for w in range(4):
-            at = w * SHARE + piece * PIECE
-            out_ref[piece, w * PIECE : (w + 1) * PIECE, :] = gate_up[at : at + PIECE]
-    out_ref[NB - 1, 0 : 4 * PIECE, :] = jnp.zeros((4 * PIECE, 2 * UNITS), BF)
-    down = across(hidden, branch)
-    each = UNITS // NB
-    for piece in range(NB):
-        rows = down[piece * each : (piece + 1) * each]
-        tail = rows[:, 2 * UNITS :]
-        tail = jnp.concatenate([tail[: each // 2], tail[each // 2 :]], axis=1)
-        rest = jnp.zeros((FF_ROWS - 4 * PIECE - DOWN_ROWS, 2 * UNITS), F32)
-        out_ref[piece, 4 * PIECE :, :] = jnp.concatenate(
-            [rows[:, : 2 * UNITS], tail, rest], axis=0
-        ).astype(BF)
-
-
-def attend_grads_kernel(index_ref, rows_ref, lin_ref, e_ref, out_ref):
-    normed = jnp.concatenate([rows_ref[t, 0:ROWS, :] for t in range(8)], axis=0)
-    mixed = jnp.concatenate([rows_ref[t, ROWS:, :] for t in range(8)], axis=0)
-    lin_grad = jnp.concatenate([lin_ref[t, 0:ROWS, :] for t in range(8)], axis=0)
-    branch = jnp.concatenate([e_ref[t] for t in range(8)], axis=0)
+        rows = [
+            gate_up[w * SHARE + piece * PIECE : w * SHARE + (piece + 1) * PIECE] for w in range(4)
+        ]
+        lower = down[4 * piece * PIECE : 4 * (piece + 1) * PIECE]
+        out_ref[piece] = jnp.concatenate([jnp.concatenate(rows, axis=0), lower], axis=1)
+    out_ref[NB - 1] = jnp.zeros((4 * PIECE, FF_WIDTH), BF)
+
+
+def attend_grads_kernel(index_ref, table_ref, *refs):
+    blocks, (lin_ref, e_ref, out_ref) = refs[:8], refs[8:]
+    sources = [4 * table_ref[2 * k] + table_ref[2 * k + 1] for k in range(8)]
+    normed = jnp.concatenate([ref[0:ROWS, :] for ref in blocks], axis=0)
+    mixed = jnp.concatenate([ref[ROWS:, :] for ref in blocks], axis=0)
+    lin_grad = jnp.concatenate([lin_ref[t, 0:ROWS, :] for t in sources], axis=0)
+    branch = jnp.concatenate([e_ref[t] for t in sources], axis=0)
     weight = across(normed, lin_grad).astype(BF)
     out_weight = across(mixed, branch).astype(BF)
     for piece in range(NB - 1):
@@ -390,32 +417,29 @@
         parts = []
         for w in range(4):
             for s in range(2):
-                source = 4 * s + w
-                parts.append(in_ref[piece, source * PIECE : (source + 1) * PIECE, :].astype(F32))
+                at_row = (4 * s + w) * PIECE
+                parts.append(in_ref[piece, at_row : at_row + PIECE, :].astype(F32))
         gate_ref[at, :] = jnp.concatenate([part[:, :UNITS] for part in parts], axis=1)
         up_ref[at, :] = jnp.concatenate([part[:, UNITS:] for part in parts], axis=1)
-    each = UNITS // NB
-    for piece in range(NB):
-        for s in range(2):
-            at = 8 * PIECE + s * (FF_ROWS - 4 * PIECE)
-            rows = in_ref[piece, at : at + FF_ROWS - 4 * PIECE, :].astype(F32)
-            tail = rows[each:DOWN_ROWS]
-            tail = jnp.concatenate([tail[:, :UNITS], tail[:, UNITS:]], axis=0)
-            to = s * UNITS + piece * each
-            down_ref[to : to + each, :] = jnp.concatenate([rows[:each], tail], axis=1)
+        rows = in_ref[piece, 8 * PIECE :, :].astype(F32)
+        to = slice(4 * piece * PIECE, 4 * (piece + 1) * PIECE)
+        down_ref[to, :] = rows
 
 
 def finish_attend_kernel(in_ref, q_ref, k_ref, v_ref, o_ref, gain_ref):
+    keys, values = [], []
     for piece in range(NB - 1):
         at = slice(piece * PIECE, (piece + 1) * PIECE)
         parts = [in_ref[piece, t * PIECE : (t + 1) * PIECE, :].astype(F32) for t in range(8)]
         lin = jnp.concatenate([part[:, :QKV_PART] for part in parts], axis=1)
         q_ref[at, :] = lin[:, : H * HD]
-        k_ref[at, :] = lin[:, H * HD : (H + KV) * HD]
-        v_ref[at, :] = lin[:, (H + KV) * HD :]
+        keys.append(lin[:, H * HD : (H + KV) * HD])
+        values.append(lin[:, (H + KV) * HD :])
         o_ref[at, :] = jnp.concatenate(
             [part[:, OUT_AT : OUT_AT + OUT_PART] for part in parts], axis=1
         )
+    k_ref[...] = jnp.transpose(jnp.concatenate(keys, axis=0))
+    v_ref[...] = jnp.transpose(jnp.concatenate(values, axis=0))
     sides = []
     for side in range(2):
         total = None
@@ -435,7 +459,7 @@
     return pl.BlockSpec((None,) + shape, lambda i: (layer,) + (0,) * len(shape))
 
 
-def call(kernel, in_specs, outs, args, scratch=(), flops=0, moved=8_000_000, exps=0):
+def call(kernel, in_specs, outs, args, scratch=()):
     return pl.pallas_call(
         kernel,
         grid=(1,),
@@ -444,7 +468,7 @@
         out_shape=[jax.ShapeDtypeStruct(shape, dtype) for shape, dtype in outs],
         scratch_shapes=list(scratch),
         compiler_params=pltpu.CompilerParams(vmem_limit_bytes=VMEM_BYTES),
-        cost_estimate=pl.CostEstimate(flops=flops, bytes_accessed=moved, transcendentals=exps),
+        cost_estimate=pl.CostEstimate(flops=1, bytes_accessed=1, transcendentals=0),
     )(*args)
 
 
@@ -501,26 +525,32 @@
             owners += [there % 2, 2 * (there // 2) + (core ^ flip)]
     table = jnp.stack(owners).astype(jnp.int32)
 
-    def with_gain(weight, gain):
-        row = jnp.pad(gain[None], ((0, 15), (0, weight.shape[1] - SHARE)))
-        return jnp.concatenate([weight, row], axis=0)
-
-    first = jnp.concatenate([w_query[0], w_key[0], w_value[0]], axis=1)
-    wqkv = sum(gather_eight(with_gain(first, norm_one[0])), [])
-    out_block, gate_block, up_block, down_block = lax.optimization_barrier(
-        (w_out[0], w_gate[0], w_up[0], w_down[0], wqkv[4])
-    )[:4]
-    wout = sum(gather_eight(with_gain(out_block, norm_two[0])), [])
-
-    pieces = jnp.concatenate(
-        [gate_block.reshape(SHARE, 4, 2, UNITS), up_block.reshape(SHARE, 4, 2, UNITS)], axis=3
-    ).transpose(2, 1, 0, 3)
-    wgu = exchange_eight(pieces.reshape(8, SHARE, 2 * UNITS)).reshape(2, D, 2 * UNITS)
-    halves = down_block.reshape(2, UNITS, D)
-    kept = lax.dynamic_index_in_dim(halves, section, 0, keepdims=False)
-    sent = lax.dynamic_index_in_dim(halves, 1 - section, 0, keepdims=False)
+    x0 = lax.dynamic_index_in_dim(tokens[:, 0], section, 0, keepdims=False).astype(F32)
+    cot = lax.dynamic_index_in_dim(cotangent[:, 0], section, 0, keepdims=False).astype(F32)
+    first, second = call(
+        pack_attend_kernel,
+        [
+            whole((SHARE, D)),
+            whole((KV * HD, SHARE)),
+            whole((KV * HD, SHARE)),
+            whole((SHARE, D)),
+            whole((1, SHARE)),
+            whole((1, SHARE)),
+        ],
+        [((SHARE + 16, WIDE), BF), ((SHARE + 16, D), BF)],
+        (w_query[0], w_key[0].T, w_value[0].T, w_out[0], norm_one, norm_two),
+    )
+    pieces, kept, sent = call(
+        pack_feed_kernel,
+        [SMEM, whole((SHARE, FF)), whole((SHARE, FF)), whole((D, FF // 4))],
+        [((8, SHARE, 2 * UNITS), BF), ((D, UNITS), BF), ((D, UNITS), BF)],
+        (table, w_gate[0], w_up[0], w_down[0].T),
+    )
+    wqkv = sum(gather_eight(first), [])
+    wqkv[4], second, pieces, sent = lax.optimization_barrier((wqkv[4], second, pieces, sent))
+    wout = sum(gather_eight(second), [])
+    wgu = exchange_eight(pieces).reshape(2, D, 2 * UNITS)
     other = swap_section(sent)
-    wdown = jnp.where(section == 0, jnp.stack([kept, other]), jnp.stack([other, kept]))
 
     block_index = lax.axis_index("blk")
     own_block = lax.dynamic_index_in_dim(span_order, block_index, 0, keepdims=False)
@@ -538,16 +568,17 @@
     rows = whole((ROWS, D))
     row_scratch = pltpu.VMEM((LEN, HD), BF)
     weights = [HBM] * 8
-    feed_weights = [(D, 2 * UNITS), (UNITS, D)]
-
-    def forward(layer, x):
+    half_down = whole((D, UNITS))
+
+    def forward(layer, x, meanwhile):
         h1, packed = call(
             functools.partial(project_kernel, layer),
             [SMEM, rows, angle, angle] + weights,
             [((ROWS, D), BF), (PACK, BF)],
             (table, x, cosine, sine, *wqkv),
-            weight_scratch(QKV),
+            weight_scratch(WIDE),
         )
+        beside = meanwhile(packed)
         packed = exchange(packed)
         heads, lse = call(
             attend_kernel,
@@ -555,9 +586,9 @@
             [(HEADS, BF), ((8, LEN), F32)],
             (place, packed),
             [row_scratch] * 3,
-            flops=1_000_000_000,
         )
         heads = exchange(heads)
+        heads, beside = lax.optimization_barrier((heads, beside))
         mixed, x2, h2 = call(
             functools.partial(mix_kernel, layer),
             [SMEM, whole(HEADS), rows] + weights,
@@ -571,35 +602,32 @@
             blocks = sum([found[step] for step in group], [])
             count = len(blocks)
             lin, hidden, *part = call(
-                functools.partial(feed_kernel, count),
-                [rows] * count + [layer_of(layer, shape) for shape in feed_weights],
+                functools.partial(feed_kernel, count, layer),
+                [SMEM] + [rows] * count + [layer_of(layer, (D, 2 * UNITS)), half_down, half_down],
                 [((count * ROWS, 2 * UNITS), F32), ((count * ROWS, UNITS), BF)]
                 + [((ROWS, D), BF)] * count,
-                (*blocks, wgu, wdown),
-                flops=500_000_000,
+                (table, *blocks, wgu, kept, other),
             )
             kept_ff.append((blocks, lin, hidden))
             for number, step in enumerate(group):
                 parts[step] = part[2 * number : 2 * number + 2]
-        y_out = x2 + scatter_eight(parts)
-        both = lax.all_gather(jnp.concatenate([h1, mixed], axis=0), EIGHT, axis=0)
-        return y_out, (x, both, packed, lse, x2, kept_ff)
-
-    def backward(layer, dy, kept_state):
-        x, both, packed, lse, x2, kept_ff = kept_state
-        found = gather_eight(dy.astype(BF))
+        both = jnp.concatenate([h1, mixed], axis=0)
+        return parts, beside, (x, both, packed, lse, x2, kept_ff)
+
+    def backward(layer, dy, found, kept_state, beside_feed, beside_attend):
+        x, _, packed, lse, x2, kept_ff = kept_state
         parts, branches, lin_grads = [None] * 4, [], []
         for group, (_, lin, _) in zip(GROUPS, kept_ff):
             blocks = sum([found[step] for step in group], [])
             count = len(blocks)
             lin_grad, *part = call(
-                functools.partial(feed_back_kernel, count),
-                [rows] * count
+                functools.partial(feed_back_kernel, count, layer),
+                [SMEM]
+                + [rows] * count
                 + [whole((count * ROWS, 2 * UNITS))]
-                + [layer_of(layer, shape) for shape in feed_weights],
+                + [layer_of(layer, (D, 2 * UNITS)), half_down, half_down],
                 [((count * ROWS, 2 * UNITS), BF)] + [((ROWS, D), BF)] * count,
-                (*blocks, lin, wgu, wdown),
-                flops=500_000_000,
+                (table, *blocks, lin, wgu, kept, other),
             )
             branches += blocks
             lin_grads.append(lin_grad)
@@ -613,10 +641,10 @@
             [rows] * 16
             + [whole((size, 2 * UNITS)) for size in sizes]
             + [whole((size, UNITS)) for size in sizes],
-            [((NB, FF_ROWS, 2 * UNITS), BF)],
+            [((NB, 4 * PIECE, FF_WIDTH), BF)],
             (*normed, *branches, *lin_grads, *[item[2] for item in kept_ff]),
-            flops=2_000_000_000,
         )[0]
+        dh2, fed = lax.optimization_barrier((dh2, beside_feed))
         dx2, heads_grad, e_parts, grad_gain_two = call(
             functools.partial(mix_back_kernel, layer),
             [SMEM, rows, rows, rows] + weights,
@@ -624,8 +652,9 @@
             (table, dy, dh2, x2, *wout),
             weight_scratch(D),
         )
+        attended = beside_attend(dx2, grad_ff)
+        e_all = exchange_eight(e_parts)
         heads_grad = exchange(heads_grad)
-        e_all = exchange_eight(e_parts)
         packed_grad = call(
             attend_back_kernel,
             [SMEM, whole(PACK), whole(HEADS), whole((8, LEN))],
@@ -634,58 +663,74 @@
             [row_scratch] * 4
             + [pltpu.VMEM((HD, LEN), BF)]
             + [pltpu.VMEM((LEN, HD), F32)] * 3,
-            flops=3_000_000_000,
         )[0]
         packed_grad = exchange(packed_grad)
+        packed_grad, e_all, attended = lax.optimization_barrier((packed_grad, e_all, attended))
         dx, lin_parts = call(
             functools.partial(project_back_kernel, layer),
             [SMEM, whole(PACK), rows, rows, angle, angle, whole((1, D))] + weights,
             [((ROWS, D), F32), ((8, ROWS + 16, 256), BF)],
             (table, packed_grad, dx2, x, cosine, sine, grad_gain_two, *wqkv),
-            weight_scratch(QKV),
+            weight_scratch(WIDE),
         )
-        lin_all = exchange_eight(lin_parts)
-        grad_att = call(
+        return dx, lin_parts, e_all, grad_ff, fed, attended
+
+    def attend_grads(blocks, lin_all, e_all):
+        return call(
             attend_grads_kernel,
-            [
-                SMEM,
-                whole((8, 2 * ROWS, D)),
-                whole((8, ROWS + 16, 256)),
-                whole((8, ROWS, 128)),
-            ],
+            [SMEM, SMEM]
+            + [whole((2 * ROWS, D))] * 8
+            + [whole((8, ROWS + 16, 256)), whole((8, ROWS, 128))],
             [((NB, 4 * PIECE, ATT_WIDTH), BF)],
-            (gain_owner, both, lin_all, e_all),
-            flops=1_000_000_000,
+            (gain_owner, table, *blocks, lin_all, e_all),
         )[0]
-        return dx, sum_over_blocks(grad_ff), sum_over_blocks(grad_att)
-
-    gain_owner = ((4 * section + shard) // 2).astype(jnp.int32).reshape(1)
-    x0 = lax.dynamic_index_in_dim(tokens[:, 0], section, 0, keepdims=False).astype(F32)
-    cot = lax.dynamic_index_in_dim(cotangent[:, 0], section, 0, keepdims=False).astype(F32)
-    y0, kept0 = forward(0, x0)
-    y0 = y0.astype(BF)
-    y1, kept1 = forward(1, y0.astype(F32))
-    y1 = y1.astype(BF)
-    dx1, ff1, att1 = backward(1, cot, kept1)
-    dx0, ff0, att0 = backward(0, dx1.astype(BF).astype(F32), kept0)
+
+    def after(value, *others):
+        return lax.optimization_barrier((value, *others))[0]
 
     def by_section(of_first, of_second):
         own = jnp.where(section == 0, of_first, of_second)
         other = swap_section(jnp.where(section == 0, of_second, of_first))
         return jnp.where(section == 0, jnp.stack([own, other]), jnp.stack([other, own]))
 
-    layer_outputs = by_section(y0, y1)
+    gain_owner = ((4 * section + shard) // 2).astype(jnp.int32).reshape(1)
+    parts, (wgu, other), kept0 = forward(0, x0, lambda packed: (wgu, other))
+    y0 = (kept0[4] + scatter_eight(parts)).astype(BF)
+    parts1, (found, both0), kept1 = forward(
+        1,
+        y0.astype(F32),
+        lambda packed: (gather_eight(after(cot.astype(BF), packed)), gather_eight(after(kept0[1], packed))),
+    )
+    dx1, lin1, e1, grad_ff1, _, both1 = backward(
+        1, cot, found, kept1, (), lambda dx2, grad_ff: gather_eight(after(kept1[1], dx2))
+    )
+    dy0 = dx1.astype(BF)
+    ff1 = sum_over_blocks(after(grad_ff1, dx1))
+
+    def beside_last(dx2, grad_ff):
+        parts = after(parts1, dx2)
+        y1 = (kept1[4] + scatter_eight(parts)).astype(BF)
+        outputs = by_section(y0, y1)
+        return exchange_eight(after(lin1, dx2)), outputs
+
+    dx0, lin0, e0, grad_ff0, ff1, (lin1, layer_outputs) = backward(
+        0, dy0.astype(F32), gather_eight(dy0), kept0, ff1, beside_last
+    )
+    ff0 = sum_over_blocks(grad_ff0)
+    upper = 2 * UNITS
+    spread = jnp.stack([ff0[:, :upper], ff1[:, :upper]]).reshape(8, PIECE, upper)
+    spread = exchange_eight(spread).reshape(8 * PIECE, upper)
+    lower = by_section(ff0[:, upper:], ff1[:, upper:])
+    lower = jnp.concatenate([lower[0], lower[1]], axis=1)
+    found = lax.all_gather(jnp.concatenate([spread, lower], axis=0), "blk", axis=0)
+    att1 = sum_over_blocks(attend_grads(sum(both1, []), lin1, e1))
+    att0 = attend_grads(sum(both0, []), exchange_eight(lin0), e0)
     input_grads = by_section(dx0, dx1)
-
-    upper = 4 * PIECE
-    spread = jnp.stack([ff0[:upper], ff1[:upper]]).reshape(8, PIECE, 2 * UNITS)
-    spread = exchange_eight(spread).reshape(8 * PIECE, 2 * UNITS)
-    lower = by_section(ff0[upper:], ff1[upper:]).reshape(-1, 2 * UNITS)
-    found = lax.all_gather(jnp.concatenate([spread, lower], axis=0), "blk", axis=0)
+    att0 = sum_over_blocks(att0)
     grad_gate, grad_up, grad_down = call(
         finish_feed_kernel,
         [whole(found.shape)],
-        [((SHARE, FF), F32), ((SHARE, FF), F32), ((FF // 4, D), F32)],
+        [((SHARE, FF), F32), ((SHARE, FF), F32), ((D, FF // 4), F32)],
         (found,),
     )
     spread = jnp.stack([att0, att1]).reshape(8, PIECE, ATT_WIDTH)
@@ -696,8 +741,8 @@
         [whole(found.shape)],
         [
             ((SHARE, H * HD), F32),
-            ((SHARE, KV * HD), F32),
-            ((SHARE, KV * HD), F32),
+            ((KV * HD, SHARE), F32),
+            ((KV * HD, SHARE), F32),
             ((SHARE, D), F32),
             ((8, SHARE), F32),
         ],
@@ -708,13 +753,13 @@
         input_grads[None, :, None],
         gain_grads[0][None],
         grad_query[None],
-        grad_key[None],
-        grad_value[None],
+        grad_key.T[None],
+        grad_value.T[None],
         grad_out[None],
         gain_grads[1][None],
         grad_gate[None],
         grad_up[None],
-        grad_down[None],
+        grad_down.T[None],
     )
 
 

time: 741 us -> 719 us (0.970)
  blocking collectives: 80.4 us -> 22.1 us
  waiting for transfers between devices: 239 us -> 267 us
  starting transfers between devices: 146 us -> 170 us
  local copies, waits for them, and re-layouts: 56.3 us -> 41.6 us
  Pallas kernels: 160 us -> 171 us
  other arithmetic: 32.3 us -> 22.7 us
    all_to_all x4 -> x1, blocking collectives: 65 us -> 12.9 us  [exchange(): return lax.all_to_all(array, 'blk', 0, 0, tiled=True)]
    all_to_all x9 -> x12, waiting for transfers between devices: 63.2 us -> 84 us  [exchange(): return lax.all_to_all(array, 'blk', 0, 0, tiled=True)]
    ppermute x80 -> x96, starting transfers between devices: 73.8 us -> 92.6 us  [hop(): return lax.ppermute(array, EIGHT, ring_pairs(step, flip))]
    ppermute x4, waiting for transfers between devices: 17 us -> 30.9 us  [swap_section(): return lax.ppermute(array, 'section', [(0, 1), (1, 0)])]
    pallas_call x30 -> x32, Pallas kernels: 160 us -> 171 us  [call(): pl.pallas_call(kernel, grid=(1,), in_specs=in_specs, out_specs=[whole(sha...]
    all_to_all x9 -> x12, starting transfers between devices: 41.3 us -> 51.3 us  [exchange(): return lax.all_to_all(array, 'blk', 0, 0, tiled=True)]
    ppermute x6 -> x1, local copies, waits for them, and re-layouts: 11.8 us -> 2.24 us  [swap_section(): return lax.ppermute(array, 'section', [(0, 1), (1, 0)])]
    ppermute x80 -> x96, waiting for transfers between devices: 147 us -> 138 us  [hop(): return lax.ppermute(array, EIGHT, ring_pairs(step, flip))]
  transfers between devices with their start and end apart: 102 -> 119, of which waited for: 41 -> 46; matrix products, arithmetic and copies ran while one was open for 9% -> 6% of each run, Pallas kernels for 20% -> 17%
where the time goes in v2:
time: 719 us; the launch traced here: 711 us
  waiting for transfers between devices  267 us (37%)
  Pallas kernels  171 us (24%)
  starting transfers between devices  170 us (24%)
  local copies, waits for them, and re-layouts  41.6 us (6%)
  other arithmetic  22.7 us (3%)
  blocking collectives  22.1 us (3%)
  between operations  16.8 us (2%)
    pallas_call x32, Pallas kernels, call(): pl.pallas_call(kernel, grid=(1,), in_specs=in_specs, out_specs=[whole(sha...  171 us
    ppermute x96, waiting for transfers between devices, hop(): return lax.ppermute(array, EIGHT, ring_pairs(step, flip))  138 us
    ppermute x96, starting transfers between devices, hop(): return lax.ppermute(array, EIGHT, ring_pairs(step, flip))  92.6 us
    all_to_all x12, waiting for transfers between devices, exchange(): return lax.all_to_all(array, 'blk', 0, 0, tiled=True)  84 us
    all_to_all x12, starting transfers between devices, exchange(): return lax.all_to_all(array, 'blk', 0, 0, tiled=True)  51.3 us
    ppermute x4, waiting for transfers between devices, swap_section(): return lax.ppermute(array, 'section', [(0, 1), (1, 0)])  30.9 us
    all_to_all x6, starting transfers between devices, exchange_eight(): return lax.all_to_all(array, EIGHT, 0, 0, tiled=True)  25.4 us
    unnamed x179, local copies, waits for them, and re-layouts  20.8 us
  transfers between devices with their start and end apart: 119, of which 46 were waited for; matrix products, arithmetic and copies ran while one was open for 6% of the time, Pallas kernels for 17%

profile of v2, /device:TPU:0, one launch (start us, length us, event | category | flops | bytes accessed | tf_op | source)
XLA Modules:
  0.0 710.6 jit_solution(1896593802428041142)
XLA Ops:
  13.0 19.0 %collective-permute-done.3.refs_6_ = bf16[256,1664]{1,0:T(8,128)(2,1)S(1)} collective-permute-done((bf16[256,1664]{1,0:T(8,128)(2,1)}, bf16[256,1664]{1,0:T(8,128)(2,1)S(1)}, u32[]{:S(2)}, u32[]{:S(2)}) %collective-permute-start.3) | collective-permute-done | bytes 852000 | tf_op jit(solution)/shard_map/ppermute | solution.py:49
  36.7 7.5 %collective-permute-done.4 = bf16[128,1664]{1,0:T(8,128)(2,1)S(1)} collective-permute-done((bf16[128,1664]{1,0:T(8,128)(2,1)S(1)}, bf16[128,1664]{1,0:T(8,128)(2,1)S(1)}, u32[]{:S(2)}, u32[]{:S(2)}) %collective-permute-start.4) | collective-permute-done | bytes 426016 | tf_op jit(solution)/shard_map/ppermute | solution.py:49
  55.8 6.0 shard_map.205
  61.8 8.0 %all-to-all-start = ((bf16[16,192,128]{2,1,0:T(8,128)(2,1)}), bf16[16,192,128]{2,1,0:T(8,128)(2,1)S(1)}, u32[]{:S(2)}, u32[]{:S(2)}) async-start(bf16[16,192,128]{2,1,0:T(8,128)(2,1)} %get-tuple-element.158), calls=%async_computation | async-start | bytes 1572864 | tf_op jit(solution)/shard_map/all_to_all | solution.py:483
  70.4 14.2 %all-to-all-done.in_ref = bf16[16,192,128]{2,1,0:T(8,128)(2,1)S(1)} async-done(((bf16[16,192,128]{2,1,0:T(8,128)(2,1)}), bf16[16,192,128]{2,1,0:T(8,128)(2,1)S(1)}, u32[]{:S(2)}, u32[]{:S(2)}) %all-to-all-start) | async-done | bytes 786464 | tf_op jit(solution)/shard_map/all_to_all | solution.py:483
  85.5 8.1 %shard_map.206 = (bf16[16,64,128]{2,1,0:T(8,128)(2,1)}, f32[8,2048]{1,0:T(8,128)}) custom-call(s32[16]{0:T(128)} %select_reduce_fusion.place_ref, bf16[16,192,128]{2,1,0:T(8,128)(2,1)} %copy-done.6), custom_call_target="tpu_custom_call" | custom-call | flops 1 | bytes 1 | tf_op jit(solution)/shard_map/pallas_call | solution.py:463
  93.6 12.9 %all_to_all.100.in_ref = bf16[16,64,128]{2,1,0:T(8,128)(2,1)} all-to-all(bf16[16,64,128]{2,1,0:T(8,128)(2,1)} %get-tuple-element.159), channel_id=1, replica_groups=mesh['section'=2,'blk'=16,'wshard'=4] {'blk'}, dimensions={0} | all-to-all | bytes 524288 | tf_op jit(solution)/shard_map/all_to_all | solution.py:483
  114.6 38.7 %collective-permute-done.12.refs_6_ = bf16[256,960]{1,0:T(8,128)(2,1)S(1)} collective-permute-done((bf16[256,960]{1,0:T(8,128)(2,1)}, bf16[256,960]{1,0:T(8,128)(2,1)S(1)}, u32[]{:S(2)}, u32[]{:S(2)}) %collective-permute-start.12) | collective-permute-done | bytes 491552 | tf_op jit(solution)/shard_map/ppermute | solution.py:49
  167.3 10.4 %collective-permute-done.8 = bf16[960,320]{0,1:T(8,128)(2,1)} collective-permute-done((bf16[960,320]{0,1:T(8,128)(2,1)}, bf16[960,320]{0,1:T(8,128)(2,1)}, u32[]{:S(2)}, u32[]{:S(2)}) %collective-permute-start.8) | collective-permute-done | bytes 614432 | tf_op jit(solution)/shard_map/ppermute | solution.py:53
  186.0 6.1 collective-permute-done.21.refs_2_.refs_4_
  235.8 6.0 shard_map.211
  273.5 8.1 %shard_map.212 = (bf16[16,64,128]{2,1,0:T(8,128)(2,1)}, f32[8,2048]{1,0:T(8,128)}) custom-call(s32[16]{0:T(128)} %select_reduce_fusion.place_ref, bf16[16,192,128]{2,1,0:T(8,128)(2,1)} %copy-done.7), custom_call_target="tpu_custom_call" | custom-call | flops 1 | bytes 1 | tf_op jit(solution)/shard_map/pallas_call | solution.py:463
  285.2 9.5 %all-to-all-done.4.in_ref = bf16[16,64,128]{2,1,0:T(8,128)(2,1)S(1)} async-done(((bf16[16,64,128]{2,1,0:T(8,128)(2,1)}), bf16[16,64,128]{2,1,0:T(8,128)(2,1)S(1)}, u32[]{:S(2)}, u32[]{:S(2)}) %all-to-all-start.4) | async-done | bytes 262176 | tf_op jit(solution)/shard_map/all_to_all | solution.py:483
  303.1 5.8 collective-permute-done.53.refs_2_.refs_4_
  377.3 7.0 collective-permute-done.68.refs_6_
  393.7 10.4 %shard_map.221 = bf16[16,192,128]{2,1,0:T(8,128)(2,1)} custom-call(s32[16]{0:T(128)} %select_reduce_fusion.place_ref, bf16[16,192,128]{2,1,0:T(8,128)(2,1)} %copy-done.7, bf16[16,64,128]{2,1,0:T(8,128)(2,1)} %copy-done.53, f32[8,2048]{1,0:T(8,128)} %get-tuple-element.206.lse_ref), custom_call_target="tpu_custom_call" | custom-call | flops 1 | bytes 1 | tf_op jit(solution)/shard_map/pallas_call | solution.py:463
  410.8 6.9 shard_map.226
  424.0 6.6 shard_map.222
  467.5 6.9 shard_map.233
  474.6 7.0 all-to-all-start.18
  501.2 14.6 %all-to-all-done.18 = bf16[16,64,960]{2,1,0:T(8,128)(2,1)} async-done(((bf16[16,64,960]{2,1,0:T(8,128)(2,1)}), bf16[16,64,960]{2,1,0:T(8,128)(2,1)}, u32[]{:S(2)}, u32[]{:S(2)}) %all-to-all-start.18) | async-done | bytes 1966112 | tf_op jit(solution)/shard_map/all_to_all | solution.py:483
  518.6 6.4 all-to-all-start.19
  525.1 6.2 all-to-all-done.19
  552.7 7.9 %all-to-all-done.9.do_ref = bf16[16,64,128]{2,1,0:T(8,128)(2,1)S(1)} async-done(((bf16[16,64,128]{2,1,0:T(8,128)(2,1)}), bf16[16,64,128]{2,1,0:T(8,128)(2,1)S(1)}, u32[]{:S(2)}, u32[]{:S(2)}) %all-to-all-start.9) | async-done | bytes 262176 | tf_op jit(solution)/shard_map/all_to_all | solution.py:483
  568.5 10.4 %shard_map.228 = bf16[16,192,128]{2,1,0:T(8,128)(2,1)} custom-call(s32[16]{0:T(128)} %select_reduce_fusion.place_ref, bf16[16,192,128]{2,1,0:T(8,128)(2,1)} %copy-done.6, bf16[16,64,128]{2,1,0:T(8,128)(2,1)} %copy-done.52, f32[8,2048]{1,0:T(8,128)} %get-tuple-element.235.lse_ref), custom_call_target="tpu_custom_call" | custom-call | flops 1 | bytes 1 | tf_op jit(solution)/shard_map/pallas_call | solution.py:463
  583.9 8.1 %collective-permute-done.97 = bf16[128,960]{1,0:T(8,128)(2,1)S(1)} collective-permute-done((bf16[128,960]{1,0:T(8,128)(2,1)S(1)}, bf16[128,960]{1,0:T(8,128)(2,1)S(1)}, u32[]{:S(2)}, u32[]{:S(2)}) %collective-permute-start.97) | collective-permute-done | bytes 245792 | tf_op jit(solution)/shard_map/ppermute | solution.py:53
  598.1 6.6 shard_map.229
  613.0 6.1 all-to-all-done.13.refs_8_
  627.3 9.1 %all-to-all-done.15 = bf16[16,64,384]{2,1,0:T(8,128)(2,1)S(1)} async-done(((bf16[16,64,384]{2,1,0:T(8,128)(2,1)}), bf16[16,64,384]{2,1,0:T(8,128)(2,1)S(1)}, u32[]{:S(2)}, u32[]{:S(2)}) %all-to-all-start.15) | async-done | bytes 786464 | tf_op jit(solution)/shard_map/all_to_all | solution.py:483
  640.2 12.9 %all-to-all-done.14 = bf16[16,64,384]{2,1,0:T(8,128)(2,1)S(1)} async-done(((bf16[16,64,384]{2,1,0:T(8,128)(2,1)}), bf16[16,64,384]{2,1,0:T(8,128)(2,1)S(1)}, u32[]{:S(2)}, u32[]{:S(2)}) %all-to-all-start.14) | async-done | bytes 786464 | tf_op jit(solution)/shard_map/all_to_all | solution.py:483
  653.2 9.2 %all_to_all.101 = bf16[8,16,384]{2,1,0:T(8,128)(2,1)S(1)} all-to-all(bf16[8,16,384]{2,1,0:T(8,128)(2,1)S(1)} %bitcast.97), channel_id=1, replica_groups=mesh['section'=2,'blk'=16,'wshard'=4] {'section','wshard'}, dimensions={0} | all-to-all | bytes 196608 | tf_op jit(solution)/shard_map/all_to_all | solution.py:487
  670.8 12.3 %collective-permute-done.98 = f32[128,960]{1,0:T(8,128)S(1)} collective-permute-done((f32[128,960]{1,0:T(8,128)}, f32[128,960]{1,0:T(8,128)S(1)}, u32[]{:S(2)}, u32[]{:S(2)}) %collective-permute-start.98) | collective-permute-done | bytes 491552 | tf_op jit(solution)/shard_map/ppermute | solution.py:53
  (523 shorter events, 378.9 us)
Async XLA Ops:
  9.8 22.3 %collective-permute-start.3 = (bf16[256,1664]{1,0:T(8,128)(2,1)}, bf16[256,1664]{1,0:T(8,128)(2,1)S(1)}, u32[]{:S(2)}, u32[]{:S(2)}) collective-permute-start(bf16[256,1664]{1,0:T(8,128)(2,1)} %get-tuple-element.153.refs_0_), channel_id=1, source_target_pairs={{0,64},{1,65},{64,2},{65,3},{2,66},{3,67},{66,0},{67,1},{4,68},{5,... | collective-permute-start | bytes 2555912 | tf_op jit(solution)/shard_map/ppermute | solution.py:49
  11.4 21.0 %collective-permute-start.1 = (bf16[256,1664]{1,0:T(8,128)(2,1)}, bf16[256,1664]{1,0:T(8,128)(2,1)S(1)}, u32[]{:S(2)}, u32[]{:S(2)}) collective-permute-start(bf16[256,1664]{1,0:T(8,128)(2,1)} %get-tuple-element.153.refs_0_), channel_id=1, source_target_pairs={{0,66},{1,67},{64,0},{65,1},{2,64},{3,65},{66,2},{67,3},{4,70},{5,... | collective-permute-start | bytes 2555912 | tf_op jit(solution)/shard_map/ppermute | solution.py:49
  36.2 19.6 %collective-permute-start = (bf16[256,1664]{1,0:T(8,128)(2,1)}, bf16[256,1664]{1,0:T(8,128)(2,1)}, u32[]{:S(2)}, u32[]{:S(2)}) collective-permute-start(bf16[256,1664]{1,0:T(8,128)(2,1)} %get-tuple-element.153.refs_0_), channel_id=1, source_target_pairs={{0,1},{1,0},{64,65},{65,64},{2,3},{3,2},{66,67},{67,66},{4,5},{5,4... | collective-permute-start | bytes 2555912 | tf_op jit(solution)/shard_map/ppermute | solution.py:49
  36.2 19.6 %collective-permute-start.7 = (bf16[256,1664]{1,0:T(8,128)(2,1)S(1)}, bf16[256,1664]{1,0:T(8,128)(2,1)}, u32[]{:S(2)}, u32[]{:S(2)}) collective-permute-start(bf16[256,1664]{1,0:T(8,128)(2,1)S(1)} %collective-permute-done.3.refs_6_), channel_id=1, source_target_pairs={{0,1},{1,0},{64,65},{65,64},{2,3},{3,2},{66,67},{67,66},{4,5},{5,4... | collective-permute-start | bytes 2555912 | tf_op jit(solution)/shard_map/ppermute | solution.py:49
  36.7 19.1 %collective-permute-start.2 = (bf16[256,1664]{1,0:T(8,128)(2,1)S(1)}, bf16[256,1664]{1,0:T(8,128)(2,1)}, u32[]{:S(2)}, u32[]{:S(2)}) collective-permute-start(bf16[256,1664]{1,0:T(8,128)(2,1)S(1)} %collective-permute-done.1.refs_2_), channel_id=1, source_target_pairs={{0,1},{1,0},{64,65},{65,64},{2,3},{3,2},{66,67},{67,66},{4,5},{5,4... | collective-permute-start | bytes 2555912 | tf_op jit(solution)/shard_map/ppermute | solution.py:49
  61.8 22.8 %all-to-all-start = ((bf16[16,192,128]{2,1,0:T(8,128)(2,1)}), bf16[16,192,128]{2,1,0:T(8,128)(2,1)S(1)}, u32[]{:S(2)}, u32[]{:S(2)}) async-start(bf16[16,192,128]{2,1,0:T(8,128)(2,1)} %get-tuple-element.158), calls=%async_computation | async-start | bytes 1572864 | tf_op jit(solution)/shard_map/all_to_all | solution.py:483
  106.5 71.3 %all-to-all-start.2 = ((bf16[8,240,640]{2,1,0:T(8,128)(2,1)}), bf16[8,240,640]{2,1,0:T(8,128)(2,1)S(1)}, u32[]{:S(2)}, u32[]{:S(2)}) async-start(bf16[8,240,640]{2,1,0:T(8,128)(2,1)} %get-tuple-element.160), calls=%async_computation.2 | async-start | bytes 4915200 | tf_op jit(solution)/shard_map/all_to_all | solution.py:487
  111.3 42.0 %collective-permute-start.12 = (bf16[256,960]{1,0:T(8,128)(2,1)}, bf16[256,960]{1,0:T(8,128)(2,1)S(1)}, u32[]{:S(2)}, u32[]{:S(2)}) collective-permute-start(bf16[256,960]{1,0:T(8,128)(2,1)} %get-tuple-element.163.refs_0_), channel_id=1, source_target_pairs={{0,64},{1,65},{64,2},{65,3},{2,66},{3,67},{66,0},{67,1},{4,68},{5,... | collective-permute-start | bytes 1474568 | tf_op jit(solution)/shard_map/ppermute | solution.py:49
  113.3 40.8 %collective-permute-start.10 = (bf16[256,960]{1,0:T(8,128)(2,1)}, bf16[256,960]{1,0:T(8,128)(2,1)S(1)}, u32[]{:S(2)}, u32[]{:S(2)}) collective-permute-start(bf16[256,960]{1,0:T(8,128)(2,1)} %get-tuple-element.163.refs_0_), channel_id=1, source_target_pairs={{0,66},{1,67},{64,0},{65,1},{2,64},{3,65},{66,2},{67,3},{4,70},{5,... | collective-permute-start | bytes 1474568 | tf_op jit(solution)/shard_map/ppermute | solution.py:49
  158.1 19.7 %collective-permute-start.9 = (bf16[256,960]{1,0:T(8,128)(2,1)}, bf16[256,960]{1,0:T(8,128)(2,1)}, u32[]{:S(2)}, u32[]{:S(2)}) collective-permute-start(bf16[256,960]{1,0:T(8,128)(2,1)} %get-tuple-element.163.refs_0_), channel_id=1, source_target_pairs={{0,1},{1,0},{64,65},{65,64},{2,3},{3,2},{66,67},{67,66},{4,5},{5,4... | collective-permute-start | bytes 1474568 | tf_op jit(solution)/shard_map/ppermute | solution.py:49
  210.4 18.8 %collective-permute-start.18 = (bf16[128,960]{1,0:T(8,128)(2,1)}, bf16[128,960]{1,0:T(8,128)(2,1)S(1)}, u32[]{:S(2)}, u32[]{:S(2)}) collective-permute-start(bf16[128,960]{1,0:T(8,128)(2,1)} %get-tuple-element.168), channel_id=1, source_target_pairs={{0,1},{1,0},{64,65},{65,64},{2,3},{3,2},{66,67},{67,66},{4,5},{5,4... | collective-permute-start | bytes 737288 | tf_op jit(solution)/shard_map/ppermute | solution.py:49
  245.2 27.4 %all-to-all-start.3 = ((bf16[16,192,128]{2,1,0:T(8,128)(2,1)}), bf16[16,192,128]{2,1,0:T(8,128)(2,1)S(1)}, u32[]{:S(2)}, u32[]{:S(2)}) async-start(bf16[16,192,128]{2,1,0:T(8,128)(2,1)} %get-tuple-element.175), calls=%async_computation.3 | async-start | bytes 1572864 | tf_op jit(solution)/shard_map/all_to_all | solution.py:483
  271.0 23.7 %collective-permute-start.48 = (bf16[256,960]{1,0:T(8,128)(2,1)S(1)}, bf16[256,960]{1,0:T(8,128)(2,1)}, u32[]{:S(2)}, u32[]{:S(2)}) collective-permute-start(bf16[256,960]{1,0:T(8,128)(2,1)S(1)} %collective-permute-done.44.refs_6_), channel_id=1, source_target_pairs={{0,1},{1,0},{64,65},{65,64},{2,3},{3,2},{66,67},{67,66},{4,5},{5,4... | collective-permute-start | bytes 1474568 | tf_op jit(solution)/shard_map/ppermute | solution.py:49
  271.9 22.8 %collective-permute-start.43 = (bf16[256,960]{1,0:T(8,128)(2,1)}, bf16[256,960]{1,0:T(8,128)(2,1)}, u32[]{:S(2)}, u32[]{:S(2)}) collective-permute-start(bf16[256,960]{1,0:T(8,128)(2,1)} %collective-permute-done.42.refs_2_), channel_id=1, source_target_pairs={{0,1},{1,0},{64,65},{65,64},{2,3},{3,2},{66,67},{67,66},{4,5},{5,4... | collective-permute-start | bytes 1474568 | tf_op jit(solution)/shard_map/ppermute | solution.py:49
  271.9 22.8 %collective-permute-start.47 = (bf16[256,960]{1,0:T(8,128)(2,1)}, bf16[256,960]{1,0:T(8,128)(2,1)}, u32[]{:S(2)}, u32[]{:S(2)}) collective-permute-start(bf16[256,960]{1,0:T(8,128)(2,1)} %constant_dynamic-update-slice_fusion.8.refs_4_), channel_id=1, source_target_pairs={{0,1},{1,0},{64,65},{65,64},{2,3},{3,2},{66,67},{67,66},{4,5},{5,4... | collective-permute-start | bytes 1474568 | tf_op jit(solution)/shard_map/ppermute | solution.py:49
  315.8 21.0 %collective-permute-start.58 = (bf16[128,960]{1,0:T(8,128)(2,1)S(1)}, bf16[128,960]{1,0:T(8,128)(2,1)S(1)}, u32[]{:S(2)}, u32[]{:S(2)}) collective-permute-start(bf16[128,960]{1,0:T(8,128)(2,1)S(1)} %constant_dynamic-update-slice_fusion.10.refs_0_.refs_6_), channel_id=1, source_target_pairs={{0,1},{1,0},{64,65},{65,64},{2,3},{3,2},{66,67},{67,66},{4,5},{5,4... | collective-permute-start | bytes 737288 | tf_op jit(solution)/shard_map/ppermute | solution.py:49
  336.3 23.5 %collective-permute-start.50 = (bf16[128,960]{1,0:T(8,128)(2,1)}, bf16[128,960]{1,0:T(8,128)(2,1)S(1)}, u32[]{:S(2)}, u32[]{:S(2)}) collective-permute-start(bf16[128,960]{1,0:T(8,128)(2,1)} %get-tuple-element.189), channel_id=1, source_target_pairs={{0,1},{1,0},{64,65},{65,64},{2,3},{3,2},{66,67},{67,66},{4,5},{5,4... | collective-permute-start | bytes 737288 | tf_op jit(solution)/shard_map/ppermute | solution.py:49
  370.5 18.8 %collective-permute-start.66 = (bf16[256,960]{1,0:T(8,128)(2,1)S(1)}, bf16[256,960]{1,0:T(8,128)(2,1)S(1)}, u32[]{:S(2)}, u32[]{:S(2)}) collective-permute-start(bf16[256,960]{1,0:T(8,128)(2,1)S(1)} %pad_maximum_fusion.1.refs_0_), channel_id=1, source_target_pairs={{0,66},{1,67},{64,0},{65,1},{2,64},{3,65},{66,2},{67,3},{4,70},{5,... | collective-permute-start | bytes 1474568 | tf_op jit(solution)/shard_map/ppermute | solution.py:49
  384.3 24.8 %collective-permute-start.69 = (bf16[128,960]{1,0:T(8,128)(2,1)S(1)}, bf16[128,960]{1,0:T(8,128)(2,1)S(1)}, u32[]{:S(2)}, u32[]{:S(2)}) collective-permute-start(bf16[128,960]{1,0:T(8,128)(2,1)S(1)} %slice.224), channel_id=1, source_target_pairs={{0,64},{1,65},{64,2},{65,3},{2,66},{3,67},{66,0},{67,1},{4,68},{5,... | collective-permute-start | bytes 737288 | tf_op jit(solution)/shard_map/ppermute | solution.py:49
  390.1 19.0 %collective-permute-start.70 = (bf16[128,960]{1,0:T(8,128)(2,1)}, bf16[128,960]{1,0:T(8,128)(2,1)}, u32[]{:S(2)}, u32[]{:S(2)}) collective-permute-start(bf16[128,960]{1,0:T(8,128)(2,1)} %slice.225), channel_id=1, source_target_pairs={{0,66},{1,67},{64,0},{65,1},{2,64},{3,65},{66,2},{67,3},{4,70},{5,... | collective-permute-start | bytes 737288 | tf_op jit(solution)/shard_map/ppermute | solution.py:49
  404.8 18.2 %all-to-all-start.6 = ((bf16[16,192,128]{2,1,0:T(8,128)(2,1)}), bf16[16,192,128]{2,1,0:T(8,128)(2,1)S(1)}, u32[]{:S(2)}, u32[]{:S(2)}) async-start(bf16[16,192,128]{2,1,0:T(8,128)(2,1)} %shard_map.221), calls=%async_computation.6 | async-start | bytes 1572864 | tf_op jit(solution)/shard_map/all_to_all | solution.py:483
  430.6 44.0 %all-to-all-start.8 = ((bf16[16,64,960]{2,1,0:T(8,128)(2,1)}), bf16[16,64,960]{2,1,0:T(8,128)(2,1)S(1)}, u32[]{:S(2)}, u32[]{:S(2)}) async-start(bf16[16,64,960]{2,1,0:T(8,128)(2,1)} %shard_map.226), calls=%async_computation.8 | async-start | bytes 4194304 | tf_op jit(solution)/shard_map/all_to_all | solution.py:483
  462.3 31.3 %collective-permute-start.74 = (bf16[128,960]{1,0:T(8,128)(2,1)}, bf16[128,960]{1,0:T(8,128)(2,1)}, u32[]{:S(2)}, u32[]{:S(2)}) collective-permute-start(bf16[128,960]{1,0:T(8,128)(2,1)} %get-tuple-element.217), channel_id=1, source_target_pairs={{0,1},{1,0},{64,65},{65,64},{2,3},{3,2},{66,67},{67,66},{4,5},{5,4... | collective-permute-start | bytes 737288 | tf_op jit(solution)/shard_map/ppermute | solution.py:49
  462.3 19.4 %collective-permute-start.86 = (bf16[128,960]{1,0:T(8,128)(2,1)}, bf16[128,960]{1,0:T(8,128)(2,1)}, u32[]{:S(2)}, u32[]{:S(2)}) collective-permute-start(bf16[128,960]{1,0:T(8,128)(2,1)} %get-tuple-element.225), channel_id=1, source_target_pairs={{0,1},{1,0},{64,65},{65,64},{2,3},{3,2},{66,67},{67,66},{4,5},{5,4... | collective-permute-start | bytes 737288 | tf_op jit(solution)/shard_map/ppermute | solution.py:49
  474.6 41.2 %all-to-all-start.18 = ((bf16[16,64,960]{2,1,0:T(8,128)(2,1)}), bf16[16,64,960]{2,1,0:T(8,128)(2,1)}, u32[]{:S(2)}, u32[]{:S(2)}) async-start(bf16[16,64,960]{2,1,0:T(8,128)(2,1)} %shard_map.233), calls=%async_computation.18 | async-start | bytes 4194304 | tf_op jit(solution)/shard_map/all_to_all | solution.py:483
  525.0 172.9 %all-gather.3.cloned.1.call-start = ((), (), s32[]{:S(2)}) async-start(), calls=%async_computation.20 | async-start | bytes 4177920 | tf_op jit(solution)/shard_map/all_gather | solution.py:725
  540.6 41.9 %collective-permute-start.89 = (bf16[128,960]{1,0:T(8,128)(2,1)}, bf16[128,960]{1,0:T(8,128)(2,1)S(1)}, u32[]{:S(2)}, u32[]{:S(2)}) collective-permute-start(bf16[128,960]{1,0:T(8,128)(2,1)} %get-tuple-element.249), channel_id=1, source_target_pairs={{0,1},{1,0},{64,65},{65,64},{2,3},{3,2},{66,67},{67,66},{4,5},{5,4... | collective-permute-start | bytes 737288 | tf_op jit(solution)/shard_map/ppermute | solution.py:49
  544.9 19.3 %collective-permute-start.95 = (bf16[64,960]{1,0:T(8,128)(2,1)S(1)}, bf16[64,960]{1,0:T(8,128)(2,1)S(1)}, u32[]{:S(2)}, u32[]{:S(2)}) collective-permute-start(bf16[64,960]{1,0:T(8,128)(2,1)S(1)} %get-tuple-element.339), channel_id=1, source_target_pairs={{0,66},{1,67},{64,0},{65,1},{2,64},{3,65},{66,2},{67,3},{4,70},{5,... | collective-permute-start | bytes 368648 | tf_op jit(solution)/shard_map/ppermute | solution.py:49
  552.7 29.9 %collective-permute-start.93 = (bf16[128,960]{1,0:T(8,128)(2,1)}, bf16[128,960]{1,0:T(8,128)(2,1)}, u32[]{:S(2)}, u32[]{:S(2)}) collective-permute-start(bf16[128,960]{1,0:T(8,128)(2,1)} %pad_maximum_fusion.8), channel_id=1, source_target_pairs={{0,64},{1,65},{64,2},{65,3},{2,66},{3,67},{66,0},{67,1},{4,68},{5,... | collective-permute-start | bytes 737288 | tf_op jit(solution)/shard_map/ppermute | solution.py:49
  560.6 18.3 %all-to-all-start.12 = ((bf16[8,144,256]{2,1,0:T(8,128)(2,1)}), bf16[8,144,256]{2,1,0:T(8,128)(2,1)S(1)}, u32[]{:S(2)}, u32[]{:S(2)}) async-start(bf16[8,144,256]{2,1,0:T(8,128)(2,1)} %get-tuple-element.239), calls=%async_computation.12 | async-start | bytes 1179648 | tf_op jit(solution)/shard_map/all_to_all | solution.py:487
  578.9 18.3 %all-to-all-start.10 = ((bf16[16,192,128]{2,1,0:T(8,128)(2,1)}), bf16[16,192,128]{2,1,0:T(8,128)(2,1)S(1)}, u32[]{:S(2)}, u32[]{:S(2)}) async-start(bf16[16,192,128]{2,1,0:T(8,128)(2,1)} %shard_map.228), calls=%async_computation.10 | async-start | bytes 1572864 | tf_op jit(solution)/shard_map/all_to_all | solution.py:483
  663.7 28.4 %all-to-all-start.17 = ((bf16[16,128,384]{2,1,0:T(8,128)(2,1)}), bf16[16,128,384]{2,1,0:T(8,128)(2,1)S(1)}, u32[]{:S(2)}, u32[]{:S(2)}) async-start(bf16[16,128,384]{2,1,0:T(8,128)(2,1)} %broadcast_in_dim.53), calls=%async_computation.17 | async-start | bytes 3145728 | tf_op jit(solution)/shard_map/all_to_all | solution.py:483
  (171 other events, 1765.4 us)
Sparse Core Ops, SparseCore 0:
  532.2 46.9 all-gather.2

commit v3 on v2

--- a/solution.py
+++ b/solution.py
@@ -53,26 +53,44 @@
     return lax.ppermute(array, "section", [(0, 1), (1, 0)])
 
 
+def after(values, *others):
+    return lax.optimization_barrier((values, others))[0]
+
+
+def gather_near(block):
+    before = hop(block, 1)
+    after_it = hop(block, -1)
+    return block, hop(block, 0, 1), after_it, before
+
+
+def gather_far(near):
+    half = near[0].shape[0] // 2
+    low, high = hop(near[3][:half], 1), hop(near[2][half:], -1)
+    beside = [hop(near[2], 0, 1), hop(near[3], 0, 1)]
+    return low, high, hop(low, 0, 1), hop(high, 0, 1), *beside
+
+
+def arranged(near, far):
+    return [[near[0], near[1]], [near[2], far[4]], list(far[:4]), [near[3], far[5]]]
+
+
 def gather_eight(block):
-    half = block.shape[0] // 2
-    beside = hop(block, 0, 1)
-    before = hop(block, 1)
-    after = hop(block, -1)
-    far = jnp.concatenate([hop(before[:half], 1), hop(after[half:], -1)], axis=0)
-    return [
-        [block, beside],
-        [after, hop(after, 0, 1)],
-        [far, hop(far, 0, 1)],
-        [before, hop(before, 0, 1)],
-    ]
+    near = gather_near(block)
+    return arranged(near, gather_far(near))
+
+
+def exchange_eight(parts):
+    found = [parts[0]] + [None] * 7
+    for step, flip in ((0, 1), (1, 0), (3, 0), (1, 1), (3, 1), (2, 0), (2, 1)):
+        found[2 * ((4 - step) % 4) + flip] = hop(parts[2 * step + flip], step, flip)
+    return found
 
 
 def scatter_eight(parts):
     half = parts[0][0].shape[0] // 2
     total = [None] * 4
     for step in (2, 1, 3, 0):
-        arrived = hop(parts[step][1].astype(BF), 0, 1)
-        total[step] = parts[step][0].astype(F32) + arrived.astype(F32)
+        total[step] = parts[step][0].astype(F32) + hop(parts[step][1], 0, 1).astype(F32)
     far = total[2].astype(BF)
     low = hop(far[:half], 1).astype(F32)
     high = hop(far[half:], -1).astype(F32)
@@ -138,12 +156,15 @@
         ref[SHARE:, :] = jnp.concatenate([row, jnp.zeros((16, width - SHARE), BF)], axis=1)
 
 
-def pack_feed_kernel(table_ref, gate_ref, up_ref, down_ref, pieces_ref, kept_ref, sent_ref):
+def pack_feed_kernel(table_ref, gate_ref, up_ref, down_ref, *refs):
+    pieces, (kept_ref, sent_ref, held_ref) = refs[:8], refs[8:]
     for s in range(2):
         for w in range(4):
             at = 2 * w + s
             at = slice(at * UNITS, (at + 1) * UNITS)
-            pieces_ref[4 * s + w] = jnp.concatenate([gate_ref[:, at], up_ref[:, at]], axis=1)
+            held_ref[4 * s + w] = jnp.concatenate([gate_ref[:, at], up_ref[:, at]], axis=1)
+    for number in range(8):
+        pieces[number][...] = held_ref[4 * table_ref[2 * number] + table_ref[2 * number + 1]]
     first, second = down_ref[:, :UNITS], down_ref[:, UNITS:]
 
     @pl.when(table_ref[0] == 0)
@@ -157,20 +178,23 @@
         sent_ref[...] = first
 
 
-def load_blocks(table_ref, layer, blocks, weight_ref, gain_ref, sems):
+def load_blocks(table_ref, layer, blocks, weight_ref, sems, gain_ref=None):
     def copies(number):
         place = table_ref[2 * number + 1]
-        block = blocks[number]
-        return (
-            pltpu.make_async_copy(
-                block.at[pl.ds(0, SHARE)],
-                weight_ref.at[pl.ds(pl.multiple_of(place * SHARE, 16), SHARE)],
-                sems.at[0, number],
-            ),
-            pltpu.make_async_copy(
-                block.at[pl.ds(SHARE, 16), pl.ds(0, 256)], gain_ref.at[place], sems.at[1, number]
-            ),
-        )
+        done = 0
+        for part, block in enumerate(blocks[number]):
+            rows = min(block.shape[0], SHARE - done)
+            yield pltpu.make_async_copy(
+                block.at[pl.ds(0, rows)],
+                weight_ref.at[pl.ds(pl.multiple_of(place * SHARE + done, 16), rows)],
+                sems.at[part, number],
+            )
+            done += rows
+        if gain_ref is not None:
+            last = block.shape[0] - 16
+            yield pltpu.make_async_copy(
+                block.at[pl.ds(last, 16), pl.ds(0, 256)], gain_ref.at[place], sems.at[2, number]
+            )
 
     for number in range(8):
 
@@ -186,12 +210,17 @@
             for copy in copies(number):
                 copy.wait()
 
-    return jnp.concatenate([gain_ref[w, 0:1, :SHARE] for w in range(4)], axis=1).astype(F32)
+    if gain_ref is not None:
+        return jnp.concatenate([gain_ref[w, 0:1, :SHARE] for w in range(4)], axis=1).astype(F32)
+
+
+def by_block(refs):
+    return [refs[0:1], refs[1:2], refs[2:3], refs[3:4], refs[4:6], refs[6:8], refs[8:9], refs[9:10]]
 
 
 def project_kernel(layer, table_ref, x_ref, cos_ref, sin_ref, *refs):
-    blocks, (h_ref, out_ref, w_ref, gain_ref, sems) = refs[:8], refs[8:]
-    gain = load_blocks(table_ref, layer, blocks, w_ref, gain_ref, sems)
+    blocks, (h_ref, out_ref, w_ref, gain_ref, sems) = by_block(refs), refs[10:]
+    gain = load_blocks(table_ref, layer, blocks, w_ref, sems, gain_ref)
     x = x_ref[...]
     h = (x * norm_factor(x) * gain).astype(BF)
     h_ref[...] = h
@@ -289,8 +318,8 @@
 
 
 def mix_kernel(layer, table_ref, in_ref, x_ref, *refs):
-    blocks, (o_ref, x2_ref, h_ref, w_ref, gain_ref, sems) = refs[:8], refs[8:]
-    gain = load_blocks(table_ref, layer, blocks, w_ref, gain_ref, sems)
+    blocks, (o_ref, x2_ref, h_ref, w_ref, gain_ref, sems) = by_block(refs), refs[10:]
+    gain = load_blocks(table_ref, layer, blocks, w_ref, sems, gain_ref)
     mixed = jnp.concatenate([unfold(in_ref[index]) for index in range(H)], axis=1)
     o_ref[...] = mixed
     x2 = x_ref[...] + dot(mixed, w_ref[...])
@@ -299,16 +328,13 @@
 
 
 def mix_back_kernel(layer, table_ref, dy_ref, dh_ref, x2_ref, *refs):
-    blocks, (dx2_ref, out_ref, e_ref, gg_ref, w_ref, gain_ref, sems) = refs[:8], refs[8:]
-    gain = load_blocks(table_ref, layer, blocks, w_ref, gain_ref, sems)
+    blocks, (dx2_ref, out_ref, gg_ref, w_ref, gain_ref, sems) = by_block(refs), refs[10:]
+    gain = load_blocks(table_ref, layer, blocks, w_ref, sems, gain_ref)
     part, grad_gain = norm_backward(x2_ref[...], gain, dh_ref[...])
     dx2 = dy_ref[...] + part
     dx2_ref[...] = dx2
     gg_ref[...] = grad_gain
     low = dx2.astype(BF)
-    for index in range(8):
-        e_ref[index, :, 0:OUT_PART] = low[:, index * OUT_PART : (index + 1) * OUT_PART]
-        e_ref[index, :, OUT_PART:] = jnp.zeros((ROWS, 128 - OUT_PART), BF)
     mixed_grad = against(low, w_ref[...]).astype(BF)
     for index in range(H):
         out_ref[index] = fold(mixed_grad[:, index * HD : (index + 1) * HD])
@@ -316,8 +342,9 @@
 
 
 def project_back_kernel(layer, table_ref, in_ref, dx2_ref, x_ref, cos_ref, sin_ref, gg_ref, *refs):
-    blocks, (dx_ref, lin_ref, w_ref, gain_ref, sems) = refs[:8], refs[8:]
-    gain = load_blocks(table_ref, layer, blocks, w_ref, gain_ref, sems)
+    blocks, parts, refs = by_block(refs), refs[11:19], refs[10:11] + refs[19:]
+    dx_ref, held_ref, w_ref, gain_ref, sems = refs
+    gain = load_blocks(table_ref, layer, blocks, w_ref, sems, gain_ref)
     cosine, sine = cos_ref[...], sin_ref[...]
     queries, keys, values = [], [], []
     for group in range(KV):
@@ -334,16 +361,31 @@
     part, grad_gain = norm_backward(x_ref[...], gain, against(lin_grad, w_ref[:, :QKV]))
     dx_ref[...] = dx2_ref[...] + part
     gains = jnp.concatenate([grad_gain, gg_ref[...], jnp.zeros((14, D), F32)], axis=0).astype(BF)
+    low = dx2_ref[...].astype(BF)
     for index in range(8):
-        lin_ref[index, 0:ROWS, 0:QKV_PART] = lin_grad[:, index * QKV_PART : (index + 1) * QKV_PART]
-        lin_ref[index, 0:ROWS, QKV_PART:] = jnp.zeros((ROWS, 256 - QKV_PART), BF)
-        lin_ref[index, ROWS:, 0:OUT_PART] = gains[:, index * OUT_PART : (index + 1) * OUT_PART]
-        lin_ref[index, ROWS:, OUT_PART:] = jnp.zeros((16, 256 - OUT_PART), BF)
+        at = slice(index * OUT_PART, (index + 1) * OUT_PART)
+        lin = lin_grad[:, index * QKV_PART : (index + 1) * QKV_PART]
+        held_ref[index, 0:ROWS, :] = jnp.concatenate(
+            [
+                lin,
+                jnp.zeros((ROWS, OUT_AT - QKV_PART), BF),
+                low[:, at],
+                jnp.zeros((ROWS, ATT_WIDTH - OUT_AT - OUT_PART), BF),
+            ],
+            axis=1,
+        )
+        held_ref[index, ROWS:, 0:OUT_PART] = gains[:, at]
+        held_ref[index, ROWS:, OUT_PART:] = jnp.zeros((16, ATT_WIDTH - OUT_PART), BF)
+    for number in range(8):
+        parts[number][...] = held_ref[4 * table_ref[2 * number] + table_ref[2 * number + 1]]
 
 
 def feed_kernel(count, layer, table_ref, *refs):
     normed = jnp.concatenate([ref[...] for ref in refs[:count]], axis=0)
-    wgu_ref, kept_ref, other_ref, lin_ref, hidden_ref = refs[count : count + 5]
+    refs = refs[count:]
+    kept_ref, other_ref, lin_ref, hidden_ref = refs[8:12]
+    wgu_ref, sems = refs[-2:]
+    load_blocks(table_ref, layer, [refs[k : k + 1] for k in range(8)], wgu_ref, sems)
     lin = dot(normed, wgu_ref[...])
     lin_ref[...] = lin
     gate, up = lin[:, :UNITS], lin[:, UNITS:]
@@ -351,13 +393,16 @@
     hidden_ref[...] = hidden
     down = jnp.where(table_ref[0] == layer, kept_ref[...], other_ref[...])
     part = against(hidden, down).astype(BF)
-    for index, ref in enumerate(refs[count + 5 :]):
+    for index, ref in enumerate(refs[12:-2]):
         ref[...] = part[index * ROWS : (index + 1) * ROWS]
 
 
 def feed_back_kernel(count, layer, table_ref, *refs):
     branch = jnp.concatenate([ref[...] for ref in refs[:count]], axis=0)
-    lin_ref, wgu_ref, kept_ref, other_ref, grad_ref = refs[count : count + 5]
+    refs = refs[count:]
+    kept_ref, other_ref, lin_ref, grad_ref = refs[8:12]
+    wgu_ref, sems = refs[-2:]
+    load_blocks(table_ref, layer, [refs[k : k + 1] for k in range(8)], wgu_ref, sems)
     down = jnp.where(table_ref[0] == layer, kept_ref[...], other_ref[...])
     hidden_grad = dot(branch, down)
     gate, up = lin_ref[:, :UNITS], lin_ref[:, UNITS:]
@@ -367,16 +412,16 @@
     lin_grad = jnp.concatenate([gate_grad, up_grad], axis=1).astype(BF)
     grad_ref[...] = lin_grad
     part = against(lin_grad, wgu_ref[...]).astype(BF)
-    for index, ref in enumerate(refs[count + 5 :]):
+    for index, ref in enumerate(refs[12:-2]):
         ref[...] = part[index * ROWS : (index + 1) * ROWS]
 
 
 def feed_grads_kernel(*refs):
-    normed = jnp.concatenate([ref[...] for ref in refs[:8]], axis=0)
-    branch = jnp.concatenate([ref[...] for ref in refs[8:16]], axis=0)
-    lin_grad = jnp.concatenate([ref[...] for ref in refs[16:19]], axis=0)
-    hidden = jnp.concatenate([ref[...] for ref in refs[19:22]], axis=0)
-    out_ref = refs[22]
+    normed = jnp.concatenate([ref[...] for ref in refs[:10]], axis=0)
+    branch = jnp.concatenate([ref[...] for ref in refs[10:20]], axis=0)
+    lin_grad = jnp.concatenate([ref[...] for ref in refs[20:23]], axis=0)
+    hidden = jnp.concatenate([ref[...] for ref in refs[23:26]], axis=0)
+    out_ref = refs[26]
     gate_up = across(normed, lin_grad).astype(BF)
     down = across(branch, hidden).astype(BF)
     for piece in range(NB - 1):
@@ -388,13 +433,19 @@
     out_ref[NB - 1] = jnp.zeros((4 * PIECE, FF_WIDTH), BF)
 
 
-def attend_grads_kernel(index_ref, table_ref, *refs):
-    blocks, (lin_ref, e_ref, out_ref) = refs[:8], refs[8:]
-    sources = [4 * table_ref[2 * k] + table_ref[2 * k + 1] for k in range(8)]
-    normed = jnp.concatenate([ref[0:ROWS, :] for ref in blocks], axis=0)
-    mixed = jnp.concatenate([ref[ROWS:, :] for ref in blocks], axis=0)
-    lin_grad = jnp.concatenate([lin_ref[t, 0:ROWS, :] for t in sources], axis=0)
-    branch = jnp.concatenate([e_ref[t] for t in sources], axis=0)
+def attend_grads_kernel(index_ref, *refs):
+    found, parts, out_ref = by_block(refs), refs[10:18], refs[18]
+    normed, mixed = [], []
+    for block in found:
+        if len(block) == 2:
+            normed.append(block[0][...])
+            mixed.append(block[1][...])
+        else:
+            normed.append(block[0][0:ROWS, :])
+            mixed.append(block[0][ROWS:, :])
+    normed, mixed = jnp.concatenate(normed, axis=0), jnp.concatenate(mixed, axis=0)
+    lin_grad = jnp.concatenate([ref[0:ROWS, 0:OUT_AT] for ref in parts], axis=0)
+    branch = jnp.concatenate([ref[0:ROWS, OUT_AT:] for ref in parts], axis=0)
     weight = across(normed, lin_grad).astype(BF)
     out_weight = across(mixed, branch).astype(BF)
     for piece in range(NB - 1):
@@ -403,9 +454,9 @@
             to = slice(w * PIECE, (w + 1) * PIECE)
             out_ref[piece, to, 0:OUT_AT] = weight[at : at + PIECE]
             out_ref[piece, to, OUT_AT:] = out_weight[at : at + PIECE]
-    gains = lin_ref[0, ROWS:, :].astype(F32)
-    for t in range(1, 8):
-        gains = gains + lin_ref[t, ROWS:, :].astype(F32)
+    gains = parts[0][ROWS:, 0:OUT_AT].astype(F32)
+    for ref in parts[1:]:
+        gains = gains + ref[ROWS:, 0:OUT_AT].astype(F32)
     out_ref[NB - 1] = jnp.zeros((4 * PIECE, ATT_WIDTH), BF)
     at = pl.multiple_of(index_ref[0] * PIECE, PIECE)
     out_ref[NB - 1, pl.ds(at, PIECE), 0:OUT_AT] = gains.astype(BF)
@@ -483,10 +534,6 @@
     return lax.all_to_all(array, "blk", 0, 0, tiled=True)
 
 
-def exchange_eight(array):
-    return lax.all_to_all(array, EIGHT, 0, 0, tiled=True)
-
-
 def sum_over_blocks(pieces):
     return jnp.sum(exchange(pieces).astype(F32), axis=0).astype(BF)
 
@@ -495,7 +542,7 @@
     return [
         pltpu.VMEM((D, width), BF),
         pltpu.VMEM((4, 16, 256), BF),
-        pltpu.SemaphoreType.DMA((2, 8)),
+        pltpu.SemaphoreType.DMA((3, 8)),
     ]
 
 
@@ -540,17 +587,19 @@
         [((SHARE + 16, WIDE), BF), ((SHARE + 16, D), BF)],
         (w_query[0], w_key[0].T, w_value[0].T, w_out[0], norm_one, norm_two),
     )
-    pieces, kept, sent = call(
+    *pieces, kept, sent = call(
         pack_feed_kernel,
         [SMEM, whole((SHARE, FF)), whole((SHARE, FF)), whole((D, FF // 4))],
-        [((8, SHARE, 2 * UNITS), BF), ((D, UNITS), BF), ((D, UNITS), BF)],
+        [((SHARE, 2 * UNITS), BF)] * 8 + [((D, UNITS), BF)] * 2,
         (table, w_gate[0], w_up[0], w_down[0].T),
+        [pltpu.VMEM((8, SHARE, 2 * UNITS), BF)],
     )
     wqkv = sum(gather_eight(first), [])
-    wqkv[4], second, pieces, sent = lax.optimization_barrier((wqkv[4], second, pieces, sent))
-    wout = sum(gather_eight(second), [])
-    wgu = exchange_eight(pieces).reshape(2, D, 2 * UNITS)
+    second, pieces, sent = after((second, pieces, sent), wqkv[4:6])
+    wout_near = gather_near(second)
+    wgu = exchange_eight(pieces)
     other = swap_section(sent)
+    wout = sum(arranged(wout_near, gather_far(wout_near)), [])
 
     block_index = lax.axis_index("blk")
     own_block = lax.dynamic_index_in_dim(span_order, block_index, 0, keepdims=False)
@@ -567,10 +616,14 @@
     angle = whole((ROWS, HD))
     rows = whole((ROWS, D))
     row_scratch = pltpu.VMEM((LEN, HD), BF)
-    weights = [HBM] * 8
+    weights = [HBM] * 10
     half_down = whole((D, UNITS))
-
-    def forward(layer, x, meanwhile):
+    feed_scratch = [pltpu.VMEM((D, 2 * UNITS), BF), pltpu.SemaphoreType.DMA((3, 8))]
+
+    def row_specs(blocks):
+        return [whole(block.shape) for block in blocks]
+
+    def forward(layer, x, early, late):
         h1, packed = call(
             functools.partial(project_kernel, layer),
             [SMEM, rows, angle, angle] + weights,
@@ -578,8 +631,8 @@
             (table, x, cosine, sine, *wqkv),
             weight_scratch(WIDE),
         )
-        beside = meanwhile(packed)
-        packed = exchange(packed)
+        first = early(packed)
+        packed, first = lax.optimization_barrier((exchange(packed), first))
         heads, lse = call(
             attend_kernel,
             [SMEM, whole(PACK)],
@@ -588,7 +641,7 @@
             [row_scratch] * 3,
         )
         heads = exchange(heads)
-        heads, beside = lax.optimization_barrier((heads, beside))
+        heads, beside = lax.optimization_barrier((heads, late(first)))
         mixed, x2, h2 = call(
             functools.partial(mix_kernel, layer),
             [SMEM, whole(HEADS), rows] + weights,
@@ -601,12 +654,16 @@
         for group in GROUPS:
             blocks = sum([found[step] for step in group], [])
             count = len(blocks)
+            size = 2 * len(group)
+            if kept_ff:
+                blocks = after(blocks, kept_ff[-1][1])
             lin, hidden, *part = call(
                 functools.partial(feed_kernel, count, layer),
-                [SMEM] + [rows] * count + [layer_of(layer, (D, 2 * UNITS)), half_down, half_down],
-                [((count * ROWS, 2 * UNITS), F32), ((count * ROWS, UNITS), BF)]
-                + [((ROWS, D), BF)] * count,
-                (table, *blocks, wgu, kept, other),
+                [SMEM] + row_specs(blocks) + [HBM] * 8 + [half_down, half_down],
+                [((size * ROWS, 2 * UNITS), F32), ((size * ROWS, UNITS), BF)]
+                + [((ROWS, D), BF)] * size,
+                (table, *blocks, *wgu, kept, other),
+                feed_scratch,
             )
             kept_ff.append((blocks, lin, hidden))
             for number, step in enumerate(group):
@@ -614,20 +671,25 @@
         both = jnp.concatenate([h1, mixed], axis=0)
         return parts, beside, (x, both, packed, lse, x2, kept_ff)
 
-    def backward(layer, dy, found, kept_state, beside_feed, beside_attend):
+    def backward(layer, dy, found, kept_state, early, late):
         x, _, packed, lse, x2, kept_ff = kept_state
         parts, branches, lin_grads = [None] * 4, [], []
         for group, (_, lin, _) in zip(GROUPS, kept_ff):
             blocks = sum([found[step] for step in group], [])
             count = len(blocks)
+            size = 2 * len(group)
+            if lin_grads:
+                blocks = after(blocks, lin_grads[-1])
             lin_grad, *part = call(
                 functools.partial(feed_back_kernel, count, layer),
                 [SMEM]
-                + [rows] * count
-                + [whole((count * ROWS, 2 * UNITS))]
-                + [layer_of(layer, (D, 2 * UNITS)), half_down, half_down],
-                [((count * ROWS, 2 * UNITS), BF)] + [((ROWS, D), BF)] * count,
-                (table, *blocks, lin, wgu, kept, other),
+                + row_specs(blocks)
+                + [HBM] * 8
+                + [half_down, half_down]
+                + [whole((size * ROWS, 2 * UNITS))],
+                [((size * ROWS, 2 * UNITS), BF)] + [((ROWS, D), BF)] * size,
+                (table, *blocks, *wgu, kept, other, lin),
+                feed_scratch,
             )
             branches += blocks
             lin_grads.append(lin_grad)
@@ -635,26 +697,25 @@
                 parts[step] = part[2 * number : 2 * number + 2]
         dh2 = scatter_eight(parts)
         normed = sum([item[0] for item in kept_ff], [])
-        sizes = [len(item[0]) * ROWS for item in kept_ff]
+        sizes = [len(group) * 2 * ROWS for group in GROUPS]
+        lin_grads[0] = after(lin_grads[0], parts[2])
         grad_ff = call(
             feed_grads_kernel,
-            [rows] * 16
+            row_specs(normed + branches)
             + [whole((size, 2 * UNITS)) for size in sizes]
             + [whole((size, UNITS)) for size in sizes],
             [((NB, 4 * PIECE, FF_WIDTH), BF)],
             (*normed, *branches, *lin_grads, *[item[2] for item in kept_ff]),
         )[0]
-        dh2, fed = lax.optimization_barrier((dh2, beside_feed))
-        dx2, heads_grad, e_parts, grad_gain_two = call(
+        dx2, heads_grad, grad_gain_two = call(
             functools.partial(mix_back_kernel, layer),
             [SMEM, rows, rows, rows] + weights,
-            [((ROWS, D), F32), (HEADS, BF), ((8, ROWS, 128), BF), ((1, D), F32)],
+            [((ROWS, D), F32), (HEADS, BF), ((1, D), F32)],
             (table, dy, dh2, x2, *wout),
             weight_scratch(D),
         )
-        attended = beside_attend(dx2, grad_ff)
-        e_all = exchange_eight(e_parts)
-        heads_grad = exchange(heads_grad)
+        first = early(dx2)
+        heads_grad, first = lax.optimization_barrier((exchange(heads_grad), first))
         packed_grad = call(
             attend_back_kernel,
             [SMEM, whole(PACK), whole(HEADS), whole((8, LEN))],
@@ -664,29 +725,27 @@
             + [pltpu.VMEM((HD, LEN), BF)]
             + [pltpu.VMEM((LEN, HD), F32)] * 3,
         )[0]
-        packed_grad = exchange(packed_grad)
-        packed_grad, e_all, attended = lax.optimization_barrier((packed_grad, e_all, attended))
-        dx, lin_parts = call(
+        packed_grad, second = lax.optimization_barrier((exchange(packed_grad), late(first)))
+        dx, *lin_parts = call(
             functools.partial(project_back_kernel, layer),
             [SMEM, whole(PACK), rows, rows, angle, angle, whole((1, D))] + weights,
-            [((ROWS, D), F32), ((8, ROWS + 16, 256), BF)],
+            [((ROWS, D), F32)] + [((ROWS + 16, ATT_WIDTH), BF)] * 8,
             (table, packed_grad, dx2, x, cosine, sine, grad_gain_two, *wqkv),
-            weight_scratch(WIDE),
+            [pltpu.VMEM((8, ROWS + 16, ATT_WIDTH), BF)] + weight_scratch(WIDE),
         )
-        return dx, lin_parts, e_all, grad_ff, fed, attended
-
-    def attend_grads(blocks, lin_all, e_all):
+        return dx, lin_parts, grad_ff, second
+
+    def attend_grads(blocks, lin_all):
         return call(
             attend_grads_kernel,
-            [SMEM, SMEM]
-            + [whole((2 * ROWS, D))] * 8
-            + [whole((8, ROWS + 16, 256)), whole((8, ROWS, 128))],
+            [SMEM] + row_specs(blocks) + [whole((ROWS + 16, ATT_WIDTH))] * 8,
             [((NB, 4 * PIECE, ATT_WIDTH), BF)],
-            (gain_owner, table, *blocks, lin_all, e_all),
+            (gain_owner, *blocks, *lin_all),
         )[0]
 
-    def after(value, *others):
-        return lax.optimization_barrier((value, *others))[0]
+    def sum_feed(pieces):
+        flat = pieces.reshape(NB * 4 * PIECE, FF_WIDTH)
+        return lax.psum_scatter(flat, "blk", scatter_dimension=0, tiled=True)
 
     def by_section(of_first, of_second):
         own = jnp.where(section == 0, of_first, of_second)
@@ -694,37 +753,48 @@
         return jnp.where(section == 0, jnp.stack([own, other]), jnp.stack([other, own]))
 
     gain_owner = ((4 * section + shard) // 2).astype(jnp.int32).reshape(1)
-    parts, (wgu, other), kept0 = forward(0, x0, lambda packed: (wgu, other))
+    parts, (wout, wgu, other), kept0 = forward(
+        0, x0, lambda packed: (wout_near, wgu[1:3], wgu[6]), lambda first: (wout, wgu, other)
+    )
     y0 = (kept0[4] + scatter_eight(parts)).astype(BF)
-    parts1, (found, both0), kept1 = forward(
+    cot_low = cot.astype(BF)
+    parts1, (found_cot, both0), kept1 = forward(
         1,
         y0.astype(F32),
-        lambda packed: (gather_eight(after(cot.astype(BF), packed)), gather_eight(after(kept0[1], packed))),
-    )
-    dx1, lin1, e1, grad_ff1, _, both1 = backward(
-        1, cot, found, kept1, (), lambda dx2, grad_ff: gather_eight(after(kept1[1], dx2))
-    )
+        lambda packed: (gather_near(after(cot_low, packed)), gather_near(after(kept0[1], packed))),
+        lambda near: tuple(arranged(item, gather_far(item)) for item in near),
+    )
+    dx1, lin1, grad_ff1, (both1, y1) = backward(
+        1,
+        cot,
+        found_cot,
+        kept1,
+        lambda dx2: (gather_near(after(kept1[1], dx2)), dx2),
+        lambda first: (
+            arranged(first[0], gather_far(first[0])),
+            kept1[4] + scatter_eight(after(parts1, first[1])),
+        ),
+    )
+    y1 = y1.astype(BF)
     dy0 = dx1.astype(BF)
-    ff1 = sum_over_blocks(after(grad_ff1, dx1))
-
-    def beside_last(dx2, grad_ff):
-        parts = after(parts1, dx2)
-        y1 = (kept1[4] + scatter_eight(parts)).astype(BF)
-        outputs = by_section(y0, y1)
-        return exchange_eight(after(lin1, dx2)), outputs
-
-    dx0, lin0, e0, grad_ff0, ff1, (lin1, layer_outputs) = backward(
-        0, dy0.astype(F32), gather_eight(dy0), kept0, ff1, beside_last
-    )
-    ff0 = sum_over_blocks(grad_ff0)
+    ff1 = sum_feed(after(grad_ff1, dx1))
+    dx0, lin0, grad_ff0, (lin1, layer_outputs) = backward(
+        0,
+        dy0.astype(F32),
+        gather_eight(dy0),
+        kept0,
+        lambda dx2: exchange_eight(after(lin1, dx2)),
+        lambda first: (first, by_section(y0, after(y1, first[1]))),
+    )
+    ff0 = sum_feed(grad_ff0)
     upper = 2 * UNITS
     spread = jnp.stack([ff0[:, :upper], ff1[:, :upper]]).reshape(8, PIECE, upper)
-    spread = exchange_eight(spread).reshape(8 * PIECE, upper)
+    spread = lax.all_to_all(spread, EIGHT, 0, 0, tiled=True).reshape(8 * PIECE, upper)
     lower = by_section(ff0[:, upper:], ff1[:, upper:])
     lower = jnp.concatenate([lower[0], lower[1]], axis=1)
     found = lax.all_gather(jnp.concatenate([spread, lower], axis=0), "blk", axis=0)
-    att1 = sum_over_blocks(attend_grads(sum(both1, []), lin1, e1))
-    att0 = attend_grads(sum(both0, []), exchange_eight(lin0), e0)
+    att1 = sum_over_blocks(attend_grads(sum(both1, []), lin1))
+    att0 = attend_grads(sum(both0, []), exchange_eight(lin0))
     input_grads = by_section(dx0, dx1)
     att0 = sum_over_blocks(att0)
     grad_gate, grad_up, grad_down = call(
@@ -734,7 +804,7 @@
         (found,),
     )
     spread = jnp.stack([att0, att1]).reshape(8, PIECE, ATT_WIDTH)
-    spread = exchange_eight(spread).reshape(1, 8 * PIECE, ATT_WIDTH)
+    spread = lax.all_to_all(spread, EIGHT, 0, 0, tiled=True).reshape(1, 8 * PIECE, ATT_WIDTH)
     found = exchange(jnp.broadcast_to(spread, (NB, 8 * PIECE, ATT_WIDTH)))
     grad_query, grad_key, grad_value, grad_out, gain_grads = call(
         finish_attend_kernel,

time: 719 us -> 794 us (1.10)
  waiting for transfers between devices: 267 us -> 341 us
  Pallas kernels: 171 us -> 185 us
  blocking collectives: 22.1 us -> 8.7 us
    reduce_scatter x0 -> x2, waiting for transfers between devices: none -> 110 us  [sum_feed(): return lax.psum_scatter(flat, 'blk', scatter_dimension=0, tiled=True)]
    all_to_all x12 -> x11, waiting for transfers between devices: 84 us -> 48 us  [exchange(): return lax.all_to_all(array, 'blk', 0, 0, tiled=True)]
    all_to_all x6 -> x1, starting transfers between devices: 25.4 us -> 3.97 us  [body(): lax.all_to_all(spread, EIGHT, 0, 0, tiled=True).reshape(8 * PIECE, upper)]
    ppermute x96 -> x125, waiting for transfers between devices: 138 us -> 157 us  [hop(): return lax.ppermute(array, EIGHT, ring_pairs(step, flip))]
    pallas_call x32, Pallas kernels: 171 us -> 185 us  [call(): pl.pallas_call(kernel, grid=(1,), in_specs=in_specs, out_specs=[whole(sha...]
    all_to_all x2 -> x1, blocking collectives: 22.1 us -> 8.7 us  [body(): lax.all_to_all(spread, EIGHT, 0, 0, tiled=True)]
    ppermute x96 -> x125, starting transfers between devices: 92.6 us -> 104 us  [hop(): return lax.ppermute(array, EIGHT, ring_pairs(step, flip))]
    ppermute x4, waiting for transfers between devices: 30.9 us -> 20.3 us  [swap_section(): return lax.ppermute(array, 'section', [(0, 1), (1, 0)])]
  transfers between devices with their start and end apart: 119 -> 144, of which waited for: 46 -> 48; matrix products, arithmetic and copies ran while one was open for 6% -> 5% of each run, Pallas kernels for 17% -> 19%
where the time goes in v3:
time: 794 us; the launch traced here: 783 us
  waiting for transfers between devices  341 us (43%)
  Pallas kernels  185 us (23%)
  starting transfers between devices  174 us (22%)
  local copies, waits for them, and re-layouts  38.2 us (5%)
  other arithmetic  19.2 us (2%)
  between operations  17 us (2%)
  blocking collectives  8.7 us (1%)
    pallas_call x32, Pallas kernels, call(): pl.pallas_call(kernel, grid=(1,), in_specs=in_specs, out_specs=[whole(sha...  185 us
    ppermute x125, waiting for transfers between devices, hop(): return lax.ppermute(array, EIGHT, ring_pairs(step, flip))  157 us
    reduce_scatter x2, waiting for transfers between devices, sum_feed(): return lax.psum_scatter(flat, 'blk', scatter_dimension=0, tiled=True)  110 us
    ppermute x125, starting transfers between devices, hop(): return lax.ppermute(array, EIGHT, ring_pairs(step, flip))  104 us
    all_to_all x11, starting transfers between devices, exchange(): return lax.all_to_all(array, 'blk', 0, 0, tiled=True)  60.2 us
    all_to_all x11, waiting for transfers between devices, exchange(): return lax.all_to_all(array, 'blk', 0, 0, tiled=True)  48 us
    ppermute x4, waiting for transfers between devices, swap_section(): return lax.ppermute(array, 'section', [(0, 1), (1, 0)])  20.3 us
    unnamed x281, local copies, waits for them, and re-layouts  19.1 us
  transfers between devices with their start and end apart: 144, of which 48 were waited for; matrix products, arithmetic and copies ran while one was open for 5% of the time, Pallas kernels for 19%

profile of v3, /device:TPU:0, one launch (start us, length us, event | category | flops | bytes accessed | tf_op | source)
XLA Modules:
  0.0 782.6 jit_solution(9939968022460080463)
XLA Ops:
  13.0 19.0 %collective-permute-done.3.refs_8_ = bf16[256,1664]{1,0:T(8,128)(2,1)S(1)} collective-permute-done((bf16[256,1664]{1,0:T(8,128)(2,1)}, bf16[256,1664]{1,0:T(8,128)(2,1)S(1)}, u32[]{:S(2)}, u32[]{:S(2)}) %collective-permute-start.3) | collective-permute-done | bytes 852000 | tf_op jit(solution)/shard_map/ppermute | solution.py:49
  61.7 8.0 %all-to-all-start = ((bf16[16,192,128]{2,1,0:T(8,128)(2,1)}), bf16[16,192,128]{2,1,0:T(8,128)(2,1)}, u32[]{:S(2)}, u32[]{:S(2)}) async-start(bf16[16,192,128]{2,1,0:T(8,128)(2,1)} %get-tuple-element.272), calls=%async_computation | async-start | bytes 1572864 | tf_op jit(solution)/shard_map/all_to_all | solution.py:534
  73.8 12.8 %collective-permute-done.21.refs_5_.refs_7_ = bf16[240,640]{1,0:T(8,128)(2,1)S(1)} collective-permute-done((bf16[240,640]{1,0:T(8,128)(2,1)}, bf16[240,640]{1,0:T(8,128)(2,1)S(1)}, u32[]{:S(2)}, u32[]{:S(2)}) %collective-permute-start.21) | collective-permute-done | bytes 307232 | tf_op jit(solution)/shard_map/ppermute | solution.py:49
  99.6 18.0 %collective-permute-done.16.refs_4_ = bf16[128,960]{1,0:T(8,128)(2,1)} collective-permute-done((bf16[128,960]{1,0:T(8,128)(2,1)}, bf16[128,960]{1,0:T(8,128)(2,1)}, u32[]{:S(2)}, u32[]{:S(2)}) %collective-permute-start.16) | collective-permute-done | bytes 245792 | tf_op jit(solution)/shard_map/ppermute | solution.py:49
  118.1 8.1 %shard_map.206 = (bf16[16,64,128]{2,1,0:T(8,128)(2,1)}, f32[8,2048]{1,0:T(8,128)}) custom-call(s32[16]{0:T(128)} %select_reduce_fusion.place_ref, bf16[16,192,128]{2,1,0:T(8,128)(2,1)} %all-to-all-done.in_ref), custom_call_target="tpu_custom_call" | custom-call | flops 1 | bytes 1 | tf_op jit(solution)/shard_map/pallas_call | solution.py:514
  126.2 7.9 %all-to-all-start.1 = ((bf16[16,64,128]{2,1,0:T(8,128)(2,1)}), bf16[16,64,128]{2,1,0:T(8,128)(2,1)S(1)}, u32[]{:S(2)}, u32[]{:S(2)}) async-start(bf16[16,64,128]{2,1,0:T(8,128)(2,1)} %get-tuple-element.288), calls=%async_computation.1 | async-start | bytes 524288 | tf_op jit(solution)/shard_map/all_to_all | solution.py:534
  134.1 8.8 %all-to-all-done.1.in_ref = bf16[16,64,128]{2,1,0:T(8,128)(2,1)S(1)} async-done(((bf16[16,64,128]{2,1,0:T(8,128)(2,1)}), bf16[16,64,128]{2,1,0:T(8,128)(2,1)S(1)}, u32[]{:S(2)}, u32[]{:S(2)}) %all-to-all-start.1) | async-done | bytes 262176 | tf_op jit(solution)/shard_map/all_to_all | solution.py:534
  174.8 6.2 shard_map.209
  230.0 7.9 %collective-permute-done.44.refs_0_.refs_12_ = bf16[128,960]{1,0:T(8,128)(2,1)S(1)} collective-permute-done((bf16[128,960]{1,0:T(8,128)(2,1)S(1)}, bf16[128,960]{1,0:T(8,128)(2,1)S(1)}, u32[]{:S(2)}, u32[]{:S(2)}) %collective-permute-start.44) | collective-permute-done | bytes 245792 | tf_op jit(solution)/shard_map/ppermute | solution.py:49
  250.8 8.1 %shard_map.212 = (bf16[16,64,128]{2,1,0:T(8,128)(2,1)}, f32[8,2048]{1,0:T(8,128)}) custom-call(s32[16]{0:T(128)} %select_reduce_fusion.place_ref, bf16[16,192,128]{2,1,0:T(8,128)(2,1)} %copy-done.12), custom_call_target="tpu_custom_call" | custom-call | flops 1 | bytes 1 | tf_op jit(solution)/shard_map/pallas_call | solution.py:514
  258.9 6.6 all-to-all-start.3
  267.0 7.3 all-to-all-done.3.in_ref
  306.5 6.2 shard_map.216
  312.7 6.2 shard_map.217
  336.7 6.2 collective-permute-done.73
  380.2 10.4 %shard_map.221 = bf16[16,192,128]{2,1,0:T(8,128)(2,1)} custom-call(s32[16]{0:T(128)} %select_reduce_fusion.place_ref, bf16[16,192,128]{2,1,0:T(8,128)(2,1)} %copy-done.12, bf16[16,64,128]{2,1,0:T(8,128)(2,1)} %copy-done.53, f32[8,2048]{1,0:T(8,128)} %get-tuple-element.399.lse_ref), custom_call_target="tpu_custom_call" | custom-call | flops 1 | bytes 1 | tf_op jit(solution)/shard_map/pallas_call | solution.py:514
  399.5 6.9 shard_map.233
  412.2 6.9 shard_map.222
  443.9 6.1 shard_map.224
  455.6 6.9 shard_map.232
  462.6 32.9 %reduce-scatter.5.cloned.1.call-done = bf16[64,960]{1,0:T(8,128)(2,1)} async-done(((bf16[1024,960]{1,0:T(8,128)(2,1)}), bf16[64,960]{1,0:T(8,128)(2,1)}) %reduce-scatter.5.cloned.1.call-update) | async-done | bytes 122896 | tf_op jit(solution)/shard_map/reduce_scatter | solution.py:748
  496.5 76.9 %reduce-scatter.3.cloned.1.call-done = bf16[64,960]{1,0:T(8,128)(2,1)} async-done(((bf16[1024,960]{1,0:T(8,128)(2,1)}), bf16[64,960]{1,0:T(8,128)(2,1)}) %reduce-scatter.3.cloned.1.call-update) | async-done | bytes 122896 | tf_op jit(solution)/shard_map/reduce_scatter | solution.py:748
  581.5 6.1 all-to-all-done.12
  634.6 10.4 %shard_map.227 = bf16[16,192,128]{2,1,0:T(8,128)(2,1)} custom-call(s32[16]{0:T(128)} %select_reduce_fusion.place_ref, bf16[16,192,128]{2,1,0:T(8,128)(2,1)} %all-to-all-done.in_ref, bf16[16,64,128]{2,1,0:T(8,128)(2,1)} %copy-done.52, f32[8,2048]{1,0:T(8,128)} %get-tuple-element.461.lse_ref), custom_call_target="tpu_custom_call" | custom-call | flops 1 | bytes 1 | tf_op jit(solution)/shard_map/pallas_call | solution.py:514
  645.1 7.2 all-to-all-start.7
  652.5 8.0 %collective-permute-done.119 = bf16[128,960]{1,0:T(8,128)(2,1)S(1)} collective-permute-done((bf16[128,960]{1,0:T(8,128)(2,1)S(1)}, bf16[128,960]{1,0:T(8,128)(2,1)S(1)}, u32[]{:S(2)}, u32[]{:S(2)}) %collective-permute-start.119) | collective-permute-done | bytes 245792 | tf_op jit(solution)/shard_map/ppermute | solution.py:53
  660.6 6.4 all-to-all-done.7.in_ref
  675.7 6.8 shard_map.228
  703.9 7.3 all-to-all-start.8
  711.3 14.5 %all-to-all-done.8 = bf16[16,64,384]{2,1,0:T(8,128)(2,1)S(1)} async-done(((bf16[16,64,384]{2,1,0:T(8,128)(2,1)}), bf16[16,64,384]{2,1,0:T(8,128)(2,1)S(1)}, u32[]{:S(2)}, u32[]{:S(2)}) %all-to-all-start.8) | async-done | bytes 786464 | tf_op jit(solution)/shard_map/all_to_all | solution.py:534
  726.0 8.7 %all_to_all.65 = bf16[8,16,384]{2,1,0:T(8,128)(2,1)S(1)} all-to-all(bf16[8,16,384]{2,1,0:T(8,128)(2,1)S(1)} %bitcast.88), channel_id=1, replica_groups=mesh['section'=2,'blk'=16,'wshard'=4] {'section','wshard'}, dimensions={0} | all-to-all | bytes 196608 | tf_op jit(solution)/shard_map/all_to_all | solution.py:807
  743.1 12.3 %collective-permute-done.120 = f32[128,960]{1,0:T(8,128)S(1)} collective-permute-done((f32[128,960]{1,0:T(8,128)}, f32[128,960]{1,0:T(8,128)S(1)}, u32[]{:S(2)}, u32[]{:S(2)}) %collective-permute-start.120) | collective-permute-done | bytes 491552 | tf_op jit(solution)/shard_map/ppermute | solution.py:53
  (666 shorter events, 393.7 us)
Async XLA Ops:
  9.8 22.3 %collective-permute-start.3 = (bf16[256,1664]{1,0:T(8,128)(2,1)}, bf16[256,1664]{1,0:T(8,128)(2,1)S(1)}, u32[]{:S(2)}, u32[]{:S(2)}) collective-permute-start(bf16[256,1664]{1,0:T(8,128)(2,1)} %get-tuple-element.271.refs_0_), channel_id=1, source_target_pairs={{0,64},{1,65},{64,2},{65,3},{2,66},{3,67},{66,0},{67,1},{4,68},{5,... | collective-permute-start | bytes 2555912 | tf_op jit(solution)/shard_map/ppermute | solution.py:49
  11.4 21.0 %collective-permute-start.1 = (bf16[256,1664]{1,0:T(8,128)(2,1)}, bf16[256,1664]{1,0:T(8,128)(2,1)S(1)}, u32[]{:S(2)}, u32[]{:S(2)}) collective-permute-start(bf16[256,1664]{1,0:T(8,128)(2,1)} %get-tuple-element.271.refs_0_), channel_id=1, source_target_pairs={{0,66},{1,67},{64,0},{65,1},{2,64},{3,65},{66,2},{67,3},{4,70},{5,... | collective-permute-start | bytes 2555912 | tf_op jit(solution)/shard_map/ppermute | solution.py:49
  13.0 33.3 %collective-permute-start = (bf16[256,1664]{1,0:T(8,128)(2,1)}, bf16[256,1664]{1,0:T(8,128)(2,1)}, u32[]{:S(2)}, u32[]{:S(2)}) collective-permute-start(bf16[256,1664]{1,0:T(8,128)(2,1)} %get-tuple-element.271.refs_0_), channel_id=1, source_target_pairs={{0,1},{1,0},{64,65},{65,64},{2,3},{3,2},{66,67},{67,66},{4,5},{5,4... | collective-permute-start | bytes 2555912 | tf_op jit(solution)/shard_map/ppermute | solution.py:49
  48.8 37.8 %collective-permute-start.11 = (bf16[256,960]{1,0:T(8,128)(2,1)}, bf16[256,960]{1,0:T(8,128)(2,1)}, u32[]{:S(2)}, u32[]{:S(2)}) collective-permute-start(bf16[256,960]{1,0:T(8,128)(2,1)} %get-tuple-element.344.refs_0_), channel_id=1, source_target_pairs={{0,64},{1,65},{64,2},{65,3},{2,66},{3,67},{66,0},{67,1},{4,68},{5,... | collective-permute-start | bytes 1474568 | tf_op jit(solution)/shard_map/ppermute | solution.py:49
  48.8 39.0 %collective-permute-start.10 = (bf16[256,960]{1,0:T(8,128)(2,1)}, bf16[256,960]{1,0:T(8,128)(2,1)}, u32[]{:S(2)}, u32[]{:S(2)}) collective-permute-start(bf16[256,960]{1,0:T(8,128)(2,1)} %get-tuple-element.344.refs_0_), channel_id=1, source_target_pairs={{0,66},{1,67},{64,0},{65,1},{2,64},{3,65},{66,2},{67,3},{4,70},{5,... | collective-permute-start | bytes 1474568 | tf_op jit(solution)/shard_map/ppermute | solution.py:49
  54.1 32.5 %collective-permute-start.21 = (bf16[240,640]{1,0:T(8,128)(2,1)}, bf16[240,640]{1,0:T(8,128)(2,1)S(1)}, u32[]{:S(2)}, u32[]{:S(2)}) collective-permute-start(bf16[240,640]{1,0:T(8,128)(2,1)} %get-tuple-element.290), channel_id=1, source_target_pairs={{0,67},{1,66},{64,1},{65,0},{2,65},{3,64},{66,3},{67,2},{4,71},{5,... | collective-permute-start | bytes 921608 | tf_op jit(solution)/shard_map/ppermute | solution.py:49
  61.7 37.8 %all-to-all-start = ((bf16[16,192,128]{2,1,0:T(8,128)(2,1)}), bf16[16,192,128]{2,1,0:T(8,128)(2,1)}, u32[]{:S(2)}, u32[]{:S(2)}) async-start(bf16[16,192,128]{2,1,0:T(8,128)(2,1)} %get-tuple-element.272), calls=%async_computation | async-start | bytes 1572864 | tf_op jit(solution)/shard_map/all_to_all | solution.py:534
  71.2 27.6 %collective-permute-start.9 = (bf16[256,960]{1,0:T(8,128)(2,1)}, bf16[256,960]{1,0:T(8,128)(2,1)S(1)}, u32[]{:S(2)}, u32[]{:S(2)}) collective-permute-start(bf16[256,960]{1,0:T(8,128)(2,1)} %get-tuple-element.344.refs_0_), channel_id=1, source_target_pairs={{0,1},{1,0},{64,65},{65,64},{2,3},{3,2},{66,67},{67,66},{4,5},{5,4... | collective-permute-start | bytes 1474568 | tf_op jit(solution)/shard_map/ppermute | solution.py:49
  71.3 23.7 %collective-permute-start.22 = (bf16[240,640]{1,0:T(8,128)(2,1)}, bf16[240,640]{1,0:T(8,128)(2,1)S(1)}, u32[]{:S(2)}, u32[]{:S(2)}) collective-permute-start(bf16[240,640]{1,0:T(8,128)(2,1)} %get-tuple-element.291), channel_id=1, source_target_pairs={{0,2},{1,3},{64,66},{65,67},{2,0},{3,1},{66,64},{67,65},{4,6},{5,7... | collective-permute-start | bytes 921608 | tf_op jit(solution)/shard_map/ppermute | solution.py:49
  87.8 46.2 %collective-permute-start.25 = (bf16[960,320]{0,1:T(8,128)(2,1)}, bf16[960,320]{0,1:T(8,128)(2,1)}, u32[]{:S(2)}, u32[]{:S(2)}) collective-permute-start(bf16[960,320]{0,1:T(8,128)(2,1)} %copy.45), channel_id=1, source_target_pairs={{0,64},{64,0},{1,65},{65,1},{2,66},{66,2},{3,67},{67,3},{4,68},{68... | collective-permute-start | bytes 1843208 | tf_op jit(solution)/shard_map/ppermute | solution.py:53
  94.9 22.6 %collective-permute-start.16 = (bf16[128,960]{1,0:T(8,128)(2,1)}, bf16[128,960]{1,0:T(8,128)(2,1)}, u32[]{:S(2)}, u32[]{:S(2)}) collective-permute-start(bf16[128,960]{1,0:T(8,128)(2,1)} %slice.202), channel_id=1, source_target_pairs={{0,64},{1,65},{64,2},{65,3},{2,66},{3,67},{66,0},{67,1},{4,68},{5,... | collective-permute-start | bytes 737288 | tf_op jit(solution)/shard_map/ppermute | solution.py:49
  96.6 21.0 %collective-permute-start.17 = (bf16[128,960]{1,0:T(8,128)(2,1)}, bf16[128,960]{1,0:T(8,128)(2,1)}, u32[]{:S(2)}, u32[]{:S(2)}) collective-permute-start(bf16[128,960]{1,0:T(8,128)(2,1)} %slice.203), channel_id=1, source_target_pairs={{0,66},{1,67},{64,0},{65,1},{2,64},{3,65},{66,2},{67,3},{4,70},{5,... | collective-permute-start | bytes 737288 | tf_op jit(solution)/shard_map/ppermute | solution.py:49
  98.4 35.7 %collective-permute-start.20 = (bf16[256,960]{1,0:T(8,128)(2,1)}, bf16[256,960]{1,0:T(8,128)(2,1)S(1)}, u32[]{:S(2)}, u32[]{:S(2)}) collective-permute-start(bf16[256,960]{1,0:T(8,128)(2,1)} %collective-permute-done.11.refs_8_), channel_id=1, source_target_pairs={{0,1},{1,0},{64,65},{65,64},{2,3},{3,2},{66,67},{67,66},{4,5},{5,4... | collective-permute-start | bytes 1474568 | tf_op jit(solution)/shard_map/ppermute | solution.py:49
  98.8 35.3 %collective-permute-start.15 = (bf16[256,960]{1,0:T(8,128)(2,1)}, bf16[256,960]{1,0:T(8,128)(2,1)S(1)}, u32[]{:S(2)}, u32[]{:S(2)}) collective-permute-start(bf16[256,960]{1,0:T(8,128)(2,1)} %collective-permute-done.10.refs_2_), channel_id=1, source_target_pairs={{0,1},{1,0},{64,65},{65,64},{2,3},{3,2},{66,67},{67,66},{4,5},{5,4... | collective-permute-start | bytes 1474568 | tf_op jit(solution)/shard_map/ppermute | solution.py:49
  215.4 23.2 %all-to-all-start.2 = ((bf16[16,192,128]{2,1,0:T(8,128)(2,1)}), bf16[16,192,128]{2,1,0:T(8,128)(2,1)S(1)}, u32[]{:S(2)}, u32[]{:S(2)}) async-start(bf16[16,192,128]{2,1,0:T(8,128)(2,1)} %get-tuple-element.317), calls=%async_computation.2 | async-start | bytes 1572864 | tf_op jit(solution)/shard_map/all_to_all | solution.py:534
  248.9 25.5 %collective-permute-start.55 = (bf16[256,960]{1,0:T(8,128)(2,1)S(1)}, bf16[256,960]{1,0:T(8,128)(2,1)}, u32[]{:S(2)}, u32[]{:S(2)}) collective-permute-start(bf16[256,960]{1,0:T(8,128)(2,1)S(1)} %collective-permute-done.47.refs_2_), channel_id=1, source_target_pairs={{0,1},{1,0},{64,65},{65,64},{2,3},{3,2},{66,67},{67,66},{4,5},{5,4... | collective-permute-start | bytes 1474568 | tf_op jit(solution)/shard_map/ppermute | solution.py:49
  250.3 24.1 %collective-permute-start.60 = (bf16[256,960]{1,0:T(8,128)(2,1)S(1)}, bf16[256,960]{1,0:T(8,128)(2,1)}, u32[]{:S(2)}, u32[]{:S(2)}) collective-permute-start(bf16[256,960]{1,0:T(8,128)(2,1)S(1)} %collective-permute-done.48.refs_8_), channel_id=1, source_target_pairs={{0,1},{1,0},{64,65},{65,64},{2,3},{3,2},{66,67},{67,66},{4,5},{5,4... | collective-permute-start | bytes 1474568 | tf_op jit(solution)/shard_map/ppermute | solution.py:49
  290.9 29.0 %collective-permute-start.68 = (bf16[64,960]{1,0:T(8,128)(2,1)S(1)}, bf16[64,960]{1,0:T(8,128)(2,1)S(1)}, u32[]{:S(2)}, u32[]{:S(2)}) collective-permute-start(bf16[64,960]{1,0:T(8,128)(2,1)S(1)} %slice.213), channel_id=1, source_target_pairs={{0,64},{1,65},{64,2},{65,3},{2,66},{3,67},{66,0},{67,1},{4,68},{5,... | collective-permute-start | bytes 368648 | tf_op jit(solution)/shard_map/ppermute | solution.py:49
  291.0 29.4 %collective-permute-start.69 = (bf16[64,960]{1,0:T(8,128)(2,1)S(1)}, bf16[64,960]{1,0:T(8,128)(2,1)S(1)}, u32[]{:S(2)}, u32[]{:S(2)}) collective-permute-start(bf16[64,960]{1,0:T(8,128)(2,1)S(1)} %slice.214), channel_id=1, source_target_pairs={{0,66},{1,67},{64,0},{65,1},{2,64},{3,65},{66,2},{67,3},{4,70},{5,... | collective-permute-start | bytes 368648 | tf_op jit(solution)/shard_map/ppermute | solution.py:49
  320.6 30.7 %collective-permute-start.62 = (bf16[128,960]{1,0:T(8,128)(2,1)S(1)}, bf16[128,960]{1,0:T(8,128)(2,1)S(1)}, u32[]{:S(2)}, u32[]{:S(2)}) collective-permute-start(bf16[128,960]{1,0:T(8,128)(2,1)S(1)} %copy-done.120), channel_id=1, source_target_pairs={{0,1},{1,0},{64,65},{65,64},{2,3},{3,2},{66,67},{67,66},{4,5},{5,4... | collective-permute-start | bytes 737288 | tf_op jit(solution)/shard_map/ppermute | solution.py:49
  327.5 71.3 %collective-permute-start.87 = (bf16[128,960]{1,0:T(8,128)(2,1)}, bf16[128,960]{1,0:T(8,128)(2,1)S(1)}, u32[]{:S(2)}, u32[]{:S(2)}) collective-permute-start(bf16[128,960]{1,0:T(8,128)(2,1)} %get-tuple-element.413), channel_id=1, source_target_pairs={{0,1},{1,0},{64,65},{65,64},{2,3},{3,2},{66,67},{67,66},{4,5},{5,4... | collective-permute-start | bytes 737288 | tf_op jit(solution)/shard_map/ppermute | solution.py:49
  335.5 30.7 %collective-permute-start.92 = (bf16[128,960]{1,0:T(8,128)(2,1)S(1)}, bf16[128,960]{1,0:T(8,128)(2,1)S(1)}, u32[]{:S(2)}, u32[]{:S(2)}) collective-permute-start(bf16[128,960]{1,0:T(8,128)(2,1)S(1)} %copy-done.119), channel_id=1, source_target_pairs={{0,1},{1,0},{64,65},{65,64},{2,3},{3,2},{66,67},{67,66},{4,5},{5,4... | collective-permute-start | bytes 737288 | tf_op jit(solution)/shard_map/ppermute | solution.py:49
  369.9 24.3 %collective-permute-start.93 = (bf16[64,960]{1,0:T(8,128)(2,1)S(1)}, bf16[64,960]{1,0:T(8,128)(2,1)}, u32[]{:S(2)}, u32[]{:S(2)}) collective-permute-start(bf16[64,960]{1,0:T(8,128)(2,1)S(1)} %get-tuple-element.577), channel_id=1, source_target_pairs={{0,66},{1,67},{64,0},{65,1},{2,64},{3,65},{66,2},{67,3},{4,70},{5,... | collective-permute-start | bytes 368648 | tf_op jit(solution)/shard_map/ppermute | solution.py:49
  374.1 24.9 %collective-permute-start.91 = (bf16[128,960]{1,0:T(8,128)(2,1)}, bf16[128,960]{1,0:T(8,128)(2,1)}, u32[]{:S(2)}, u32[]{:S(2)}) collective-permute-start(bf16[128,960]{1,0:T(8,128)(2,1)} %pad_maximum_fusion.6), channel_id=1, source_target_pairs={{0,64},{1,65},{64,2},{65,3},{2,66},{3,67},{66,0},{67,1},{4,68},{5,... | collective-permute-start | bytes 737288 | tf_op jit(solution)/shard_map/ppermute | solution.py:49
  394.2 101.4 %reduce-scatter.5.cloned.1.call-start = ((), (), s32[]{:S(2)}) async-start(), calls=%async_computation.16 | async-start | bytes 2228224 | tf_op jit(solution)/shard_map/reduce_scatter | solution.py:748
  419.1 154.3 %reduce-scatter.3.cloned.1.call-start = ((), (), s32[]{:S(2)}) async-start(), calls=%async_computation.15 | async-start | bytes 2228224 | tf_op jit(solution)/shard_map/reduce_scatter | solution.py:748
  581.4 188.8 %all-gather.3.cloned.1.call-start = ((), (), s32[]{:S(2)}) async-start(), calls=%async_computation.17 | async-start | bytes 4177920 | tf_op jit(solution)/shard_map/all_gather | solution.py:795
  611.8 22.1 %all-to-all-start.6 = ((bf16[16,64,128]{2,1,0:T(8,128)(2,1)}), bf16[16,64,128]{2,1,0:T(8,128)(2,1)S(1)}, u32[]{:S(2)}, u32[]{:S(2)}) async-start(bf16[16,64,128]{2,1,0:T(8,128)(2,1)} %get-tuple-element.442), calls=%async_computation.6 | async-start | bytes 524288 | tf_op jit(solution)/shard_map/all_to_all | solution.py:534
  645.1 21.9 %all-to-all-start.7 = ((bf16[16,192,128]{2,1,0:T(8,128)(2,1)}), bf16[16,192,128]{2,1,0:T(8,128)(2,1)S(1)}, u32[]{:S(2)}, u32[]{:S(2)}) async-start(bf16[16,192,128]{2,1,0:T(8,128)(2,1)} %shard_map.227), calls=%async_computation.7 | async-start | bytes 1572864 | tf_op jit(solution)/shard_map/all_to_all | solution.py:534
  671.8 32.1 %all-to-all-start.9 = ((bf16[16,64,384]{2,1,0:T(8,128)(2,1)}), bf16[16,64,384]{2,1,0:T(8,128)(2,1)S(1)}, u32[]{:S(2)}, u32[]{:S(2)}) async-start(bf16[16,64,384]{2,1,0:T(8,128)(2,1)} %shard_map.230), calls=%async_computation.9 | async-start | bytes 1572864 | tf_op jit(solution)/shard_map/all_to_all | solution.py:534
  703.9 21.9 %all-to-all-start.8 = ((bf16[16,64,384]{2,1,0:T(8,128)(2,1)}), bf16[16,64,384]{2,1,0:T(8,128)(2,1)S(1)}, u32[]{:S(2)}, u32[]{:S(2)}) async-start(bf16[16,64,384]{2,1,0:T(8,128)(2,1)} %shard_map.229), calls=%async_computation.8 | async-start | bytes 1572864 | tf_op jit(solution)/shard_map/all_to_all | solution.py:534
  736.0 28.4 %all-to-all-start.11 = ((bf16[16,128,384]{2,1,0:T(8,128)(2,1)}), bf16[16,128,384]{2,1,0:T(8,128)(2,1)S(1)}, u32[]{:S(2)}, u32[]{:S(2)}) async-start(bf16[16,128,384]{2,1,0:T(8,128)(2,1)} %broadcast_in_dim.53), calls=%async_computation.11 | async-start | bytes 3145728 | tf_op jit(solution)/shard_map/all_to_all | solution.py:534
  (251 other events, 3646.5 us)
Sparse Core Ops, SparseCore 0:
  419.2 76.3 reduce-scatter.4
  499.8 73.5 reduce-scatter.2
  588.6 50.2 all-gather.2

commit v4 on v3

--- a/solution.py
+++ b/solution.py
@@ -81,8 +81,10 @@
 
 def exchange_eight(parts):
     found = [parts[0]] + [None] * 7
-    for step, flip in ((0, 1), (1, 0), (3, 0), (1, 1), (3, 1), (2, 0), (2, 1)):
+    for step, flip in ((0, 1), (1, 0), (3, 0), (1, 1), (3, 1)):
         found[2 * ((4 - step) % 4) + flip] = hop(parts[2 * step + flip], step, flip)
+    found[4] = hop(hop(parts[4], 1), 1)
+    found[5] = hop(hop(parts[5], -1), -1, 1)
     return found
 
 
@@ -166,16 +168,17 @@
     for number in range(8):
         pieces[number][...] = held_ref[4 * table_ref[2 * number] + table_ref[2 * number + 1]]
     first, second = down_ref[:, :UNITS], down_ref[:, UNITS:]
+    gap = jnp.zeros((D, 384 - UNITS), BF)
 
     @pl.when(table_ref[0] == 0)
     def _():
-        kept_ref[...] = first
-        sent_ref[...] = second
+        kept_ref[...] = jnp.concatenate([first, gap], axis=1)
+        sent_ref[...] = jnp.concatenate([second, gap], axis=1)
 
     @pl.when(table_ref[0] == 1)
     def _():
-        kept_ref[...] = second
-        sent_ref[...] = first
+        kept_ref[...] = jnp.concatenate([second, gap], axis=1)
+        sent_ref[...] = jnp.concatenate([first, gap], axis=1)
 
 
 def load_blocks(table_ref, layer, blocks, weight_ref, sems, gain_ref=None):
@@ -391,7 +394,7 @@
     gate, up = lin[:, :UNITS], lin[:, UNITS:]
     hidden = (gate * jax.nn.sigmoid(gate) * up).astype(BF)
     hidden_ref[...] = hidden
-    down = jnp.where(table_ref[0] == layer, kept_ref[...], other_ref[...])
+    down = jnp.where(table_ref[0] == layer, kept_ref[:, :UNITS], other_ref[:, :UNITS])
     part = against(hidden, down).astype(BF)
     for index, ref in enumerate(refs[12:-2]):
         ref[...] = part[index * ROWS : (index + 1) * ROWS]
@@ -403,7 +406,7 @@
     kept_ref, other_ref, lin_ref, grad_ref = refs[8:12]
     wgu_ref, sems = refs[-2:]
     load_blocks(table_ref, layer, [refs[k : k + 1] for k in range(8)], wgu_ref, sems)
-    down = jnp.where(table_ref[0] == layer, kept_ref[...], other_ref[...])
+    down = jnp.where(table_ref[0] == layer, kept_ref[:, :UNITS], other_ref[:, :UNITS])
     hidden_grad = dot(branch, down)
     gate, up = lin_ref[:, :UNITS], lin_ref[:, UNITS:]
     sig = jax.nn.sigmoid(gate)
@@ -419,9 +422,8 @@
 def feed_grads_kernel(*refs):
     normed = jnp.concatenate([ref[...] for ref in refs[:10]], axis=0)
     branch = jnp.concatenate([ref[...] for ref in refs[10:20]], axis=0)
-    lin_grad = jnp.concatenate([ref[...] for ref in refs[20:23]], axis=0)
-    hidden = jnp.concatenate([ref[...] for ref in refs[23:26]], axis=0)
-    out_ref = refs[26]
+    lin_grad, hidden = refs[20][...], refs[21][...]
+    out_ref = refs[22]
     gate_up = across(normed, lin_grad).astype(BF)
     down = across(branch, hidden).astype(BF)
     for piece in range(NB - 1):
@@ -527,7 +529,7 @@
 HBM = pl.BlockSpec(memory_space=pl.ANY)
 PACK = (NB, ROWS + ROWS // 2, 2 * HD)
 HEADS = (NB, ROWS // 2, 2 * HD)
-GROUPS = ((0,), (1, 3), (2,))
+GROUPS = ((0, 1, 2, 3),)
 
 
 def exchange(array):
@@ -590,13 +592,14 @@
     *pieces, kept, sent = call(
         pack_feed_kernel,
         [SMEM, whole((SHARE, FF)), whole((SHARE, FF)), whole((D, FF // 4))],
-        [((SHARE, 2 * UNITS), BF)] * 8 + [((D, UNITS), BF)] * 2,
+        [((SHARE, 2 * UNITS), BF)] * 8 + [((D, 384), BF)] * 2,
         (table, w_gate[0], w_up[0], w_down[0].T),
         [pltpu.VMEM((8, SHARE, 2 * UNITS), BF)],
     )
     wqkv = sum(gather_eight(first), [])
     second, pieces, sent = after((second, pieces, sent), wqkv[4:6])
     wout_near = gather_near(second)
+    pieces, sent = after((pieces, sent), wout_near)
     wgu = exchange_eight(pieces)
     other = swap_section(sent)
     wout = sum(arranged(wout_near, gather_far(wout_near)), [])
@@ -617,7 +620,7 @@
     rows = whole((ROWS, D))
     row_scratch = pltpu.VMEM((LEN, HD), BF)
     weights = [HBM] * 10
-    half_down = whole((D, UNITS))
+    half_down = whole((D, 384))
     feed_scratch = [pltpu.VMEM((D, 2 * UNITS), BF), pltpu.SemaphoreType.DMA((3, 8))]
 
     def row_specs(blocks):
@@ -696,9 +699,16 @@
             for number, step in enumerate(group):
                 parts[step] = part[2 * number : 2 * number + 2]
         dh2 = scatter_eight(parts)
+        dx2, heads_grad, grad_gain_two = call(
+            functools.partial(mix_back_kernel, layer),
+            [SMEM, rows, rows, rows] + weights,
+            [((ROWS, D), F32), (HEADS, BF), ((1, D), F32)],
+            (table, dy, dh2, x2, *wout),
+            weight_scratch(D),
+        )
         normed = sum([item[0] for item in kept_ff], [])
         sizes = [len(group) * 2 * ROWS for group in GROUPS]
-        lin_grads[0] = after(lin_grads[0], parts[2])
+        lin_grads = after(lin_grads, dx2)
         grad_ff = call(
             feed_grads_kernel,
             row_specs(normed + branches)
@@ -707,15 +717,10 @@
             [((NB, 4 * PIECE, FF_WIDTH), BF)],
             (*normed, *branches, *lin_grads, *[item[2] for item in kept_ff]),
         )[0]
-        dx2, heads_grad, grad_gain_two = call(
-            functools.partial(mix_back_kernel, layer),
-            [SMEM, rows, rows, rows] + weights,
-            [((ROWS, D), F32), (HEADS, BF), ((1, D), F32)],
-            (table, dy, dh2, x2, *wout),
-            weight_scratch(D),
+        first = early(dx2)
+        heads_grad, first, grad_ff = lax.optimization_barrier(
+            (exchange(heads_grad), first, grad_ff)
         )
-        first = early(dx2)
-        heads_grad, first = lax.optimization_barrier((exchange(heads_grad), first))
         packed_grad = call(
             attend_back_kernel,
             [SMEM, whole(PACK), whole(HEADS), whole((8, LEN))],
@@ -754,46 +759,51 @@
 
     gain_owner = ((4 * section + shard) // 2).astype(jnp.int32).reshape(1)
     parts, (wout, wgu, other), kept0 = forward(
-        0, x0, lambda packed: (wout_near, wgu[1:3], wgu[6]), lambda first: (wout, wgu, other)
+        0, x0, lambda packed: wout_near, lambda first: (wout, wgu, other)
     )
     y0 = (kept0[4] + scatter_eight(parts)).astype(BF)
     cot_low = cot.astype(BF)
-    parts1, (found_cot, both0), kept1 = forward(
+    parts1, (found_cot, near0), kept1 = forward(
         1,
         y0.astype(F32),
-        lambda packed: (gather_near(after(cot_low, packed)), gather_near(after(kept0[1], packed))),
-        lambda near: tuple(arranged(item, gather_far(item)) for item in near),
-    )
-    dx1, lin1, grad_ff1, (both1, y1) = backward(
+        lambda packed: gather_near(after(cot_low, packed)),
+        lambda near: (arranged(near, gather_far(near)), gather_near(after(kept0[1], near))),
+    )
+    dx1, lin1, grad_ff1, (both0, near1, y1) = backward(
         1,
         cot,
         found_cot,
         kept1,
-        lambda dx2: (gather_near(after(kept1[1], dx2)), dx2),
+        lambda dx2: (arranged(near0, gather_far(after(near0, dx2))), dx2),
         lambda first: (
-            arranged(first[0], gather_far(first[0])),
+            first[0],
+            gather_near(after(kept1[1], first[1])),
             kept1[4] + scatter_eight(after(parts1, first[1])),
         ),
     )
     y1 = y1.astype(BF)
     dy0 = dx1.astype(BF)
-    ff1 = sum_feed(after(grad_ff1, dx1))
-    dx0, lin0, grad_ff0, (lin1, layer_outputs) = backward(
+    ff1 = sum_feed(grad_ff1)
+    dx0, lin0, grad_ff0, (both1, lin1, layer_outputs) = backward(
         0,
         dy0.astype(F32),
         gather_eight(dy0),
         kept0,
-        lambda dx2: exchange_eight(after(lin1, dx2)),
-        lambda first: (first, by_section(y0, after(y1, first[1]))),
-    )
-    ff0 = sum_feed(grad_ff0)
+        lambda dx2: (arranged(near1, gather_far(after(near1, dx2))), dx2),
+        lambda first: (
+            first[0],
+            exchange_eight(after(lin1, first[1])),
+            by_section(y0, after(y1, first[1])),
+        ),
+    )
+    ff0, ff1 = after((sum_feed(grad_ff0), ff1), dx0)
     upper = 2 * UNITS
     spread = jnp.stack([ff0[:, :upper], ff1[:, :upper]]).reshape(8, PIECE, upper)
     spread = lax.all_to_all(spread, EIGHT, 0, 0, tiled=True).reshape(8 * PIECE, upper)
     lower = by_section(ff0[:, upper:], ff1[:, upper:])
     lower = jnp.concatenate([lower[0], lower[1]], axis=1)
     found = lax.all_gather(jnp.concatenate([spread, lower], axis=0), "blk", axis=0)
-    att1 = sum_over_blocks(attend_grads(sum(both1, []), lin1))
+    att1 = sum_over_blocks(after(attend_grads(sum(both1, []), after(lin1, dx0)), spread))
     att0 = attend_grads(sum(both0, []), exchange_eight(lin0))
     input_grads = by_section(dx0, dx1)
     att0 = sum_over_blocks(att0)

time: 794 us -> 689 us (0.87)
  waiting for transfers between devices: 341 us -> 246 us
  Pallas kernels: 185 us -> 156 us
  starting transfers between devices: 174 us -> 192 us
    reduce_scatter x2, waiting for transfers between devices: 110 us -> 32 us  [sum_feed(): return lax.psum_scatter(flat, 'blk', scatter_dimension=0, tiled=True)]
    pallas_call x32 -> x24, Pallas kernels: 185 us -> 156 us  [call(): pl.pallas_call(kernel, grid=(1,), in_specs=in_specs, out_specs=[whole(sha...]
    ppermute x125 -> x131, starting transfers between devices: 104 us -> 124 us  [hop(): return lax.ppermute(array, EIGHT, ring_pairs(step, flip))]
    ppermute x125 -> x131, waiting for transfers between devices: 157 us -> 143 us  [hop(): return lax.ppermute(array, EIGHT, ring_pairs(step, flip))]
    ppermute x4, waiting for transfers between devices: 20.3 us -> 11.3 us  [swap_section(): return lax.ppermute(array, 'section', [(0, 1), (1, 0)])]
    unnamed x281 -> x253, local copies, waits for them, and re-layouts: 19.1 us -> 17 us
  transfers between devices with their start and end apart: 144 -> 150, of which waited for: 48 -> 65; matrix products, arithmetic and copies ran while one was open for 5% -> 6% of each run, Pallas kernels for 19% -> 15%
where the time goes in v4:
time: 689 us; the launch traced here: 678 us
  waiting for transfers between devices  246 us (36%)
  starting transfers between devices  192 us (28%)
  Pallas kernels  156 us (23%)
  local copies, waits for them, and re-layouts  31.7 us (5%)
  other arithmetic  26.6 us (4%)
  between operations  16.7 us (2%)
  blocking collectives  8.49 us (1%)
    pallas_call x24, Pallas kernels, call(): pl.pallas_call(kernel, grid=(1,), in_specs=in_specs, out_specs=[whole(sha...  156 us
    ppermute x131, waiting for transfers between devices, hop(): return lax.ppermute(array, EIGHT, ring_pairs(step, flip))  143 us
    ppermute x131, starting transfers between devices, hop(): return lax.ppermute(array, EIGHT, ring_pairs(step, flip))  124 us
    all_to_all x11, starting transfers between devices, exchange(): return lax.all_to_all(array, 'blk', 0, 0, tiled=True)  61.3 us
    all_to_all x11, waiting for transfers between devices, exchange(): return lax.all_to_all(array, 'blk', 0, 0, tiled=True)  54.4 us
    reduce_scatter x2, waiting for transfers between devices, sum_feed(): return lax.psum_scatter(flat, 'blk', scatter_dimension=0, tiled=True)  32 us
    unnamed x253, local copies, waits for them, and re-layouts  17 us
  transfers between devices with their start and end apart: 150, of which 65 were waited for; matrix products, arithmetic and copies ran while one was open for 6% of the time, Pallas kernels for 15%

profile of v4, /device:TPU:0, one launch (start us, length us, event | category | flops | bytes accessed | tf_op | source)
XLA Modules:
  0.0 678.0 jit_solution(17357357531951204490)
XLA Ops:
  13.0 19.0 %collective-permute-done.3.refs_8_ = bf16[256,1664]{1,0:T(8,128)(2,1)S(1)} collective-permute-done((bf16[256,1664]{1,0:T(8,128)(2,1)}, bf16[256,1664]{1,0:T(8,128)(2,1)S(1)}, u32[]{:S(2)}, u32[]{:S(2)}) %collective-permute-start.3) | collective-permute-done | bytes 852000 | tf_op jit(solution)/shard_map/ppermute | solution.py:49
  48.9 9.0 %collective-permute-done.10.refs_2_ = bf16[256,960]{1,0:T(8,128)(2,1)} collective-permute-done((bf16[256,960]{1,0:T(8,128)(2,1)}, bf16[256,960]{1,0:T(8,128)(2,1)}, u32[]{:S(2)}, u32[]{:S(2)}) %collective-permute-start.10) | collective-permute-done | bytes 491552 | tf_op jit(solution)/shard_map/ppermute | solution.py:49
  82.9 7.7 %all-to-all-start = ((bf16[16,192,128]{2,1,0:T(8,128)(2,1)}), bf16[16,192,128]{2,1,0:T(8,128)(2,1)S(1)}, u32[]{:S(2)}, u32[]{:S(2)}) async-start(bf16[16,192,128]{2,1,0:T(8,128)(2,1)} %get-tuple-element.267), calls=%async_computation | async-start | bytes 1572864 | tf_op jit(solution)/shard_map/all_to_all | solution.py:536
  94.8 6.3 collective-permute-done.19.refs_12_
  114.1 8.1 %shard_map.206 = (bf16[16,64,128]{2,1,0:T(8,128)(2,1)}, f32[8,2048]{1,0:T(8,128)}) custom-call(s32[16]{0:T(128)} %select_reduce_fusion.place_ref, bf16[16,192,128]{2,1,0:T(8,128)(2,1)} %copy-done.7), custom_call_target="tpu_custom_call" | custom-call | flops 1 | bytes 1 | tf_op jit(solution)/shard_map/pallas_call | solution.py:516
  122.2 7.3 %all-to-all-start.1 = ((bf16[16,64,128]{2,1,0:T(8,128)(2,1)}), bf16[16,64,128]{2,1,0:T(8,128)(2,1)S(1)}, u32[]{:S(2)}, u32[]{:S(2)}) async-start(bf16[16,64,128]{2,1,0:T(8,128)(2,1)} %get-tuple-element.280), calls=%async_computation.1 | async-start | bytes 524288 | tf_op jit(solution)/shard_map/all_to_all | solution.py:536
  129.6 9.5 %all-to-all-done.1.in_ref = bf16[16,64,128]{2,1,0:T(8,128)(2,1)S(1)} async-done(((bf16[16,64,128]{2,1,0:T(8,128)(2,1)}), bf16[16,64,128]{2,1,0:T(8,128)(2,1)S(1)}, u32[]{:S(2)}, u32[]{:S(2)}) %all-to-all-start.1) | async-done | bytes 262176 | tf_op jit(solution)/shard_map/all_to_all | solution.py:536
  162.2 8.4 %shard_map.208 = (f32[1024,640]{1,0:T(8,128)}, bf16[1024,320]{1,0:T(8,128)(2,1)}, bf16[128,960]{1,0:T(8,128)(2,1)}, bf16[128,960]{1,0:T(8,128)(2,1)}, bf16[128,9...) custom-call(s32[16]{0:T(128)} %stack.115.table_ref, ...), custom_call_target="tpu_custom_call" | custom-call | flops 1 | bytes 1 | tf_op jit(solution)/shard_map/pallas_call | solution.py:516
  190.9 6.1 shard_map.209
  204.9 6.1 collective-permute-done.46.refs_2_.refs_12_
  221.3 8.1 %shard_map.210 = (bf16[16,64,128]{2,1,0:T(8,128)(2,1)}, f32[8,2048]{1,0:T(8,128)}) custom-call(s32[16]{0:T(128)} %select_reduce_fusion.place_ref, bf16[16,192,128]{2,1,0:T(8,128)(2,1)} %copy-done.8), custom_call_target="tpu_custom_call" | custom-call | flops 1 | bytes 1 | tf_op jit(solution)/shard_map/pallas_call | solution.py:516
  229.4 7.7 %all-to-all-start.3 = ((bf16[16,64,128]{2,1,0:T(8,128)(2,1)}), bf16[16,64,128]{2,1,0:T(8,128)(2,1)S(1)}, u32[]{:S(2)}, u32[]{:S(2)}) async-start(bf16[16,64,128]{2,1,0:T(8,128)(2,1)} %get-tuple-element.314), calls=%async_computation.3 | async-start | bytes 524288 | tf_op jit(solution)/shard_map/all_to_all | solution.py:536
  237.7 8.7 %all-to-all-done.3.in_ref = bf16[16,64,128]{2,1,0:T(8,128)(2,1)S(1)} async-done(((bf16[16,64,128]{2,1,0:T(8,128)(2,1)}), bf16[16,64,128]{2,1,0:T(8,128)(2,1)S(1)}, u32[]{:S(2)}, u32[]{:S(2)}) %all-to-all-start.3) | async-done | bytes 262176 | tf_op jit(solution)/shard_map/all_to_all | solution.py:536
  270.6 8.5 %shard_map.212 = (f32[1024,640]{1,0:T(8,128)}, bf16[1024,320]{1,0:T(8,128)(2,1)}, bf16[128,960]{1,0:T(8,128)(2,1)}, bf16[128,960]{1,0:T(8,128)(2,1)}, bf16[128,9...) custom-call(s32[16]{0:T(128)} %stack.115.table_ref, ...), custom_call_target="tpu_custom_call" | custom-call | flops 1 | bytes 1 | tf_op jit(solution)/shard_map/pallas_call | solution.py:516
  279.1 8.8 %shard_map.213 = (bf16[1024,640]{1,0:T(8,128)(2,1)}, bf16[128,960]{1,0:T(8,128)(2,1)}, bf16[128,960]{1,0:T(8,128)(2,1)}, bf16[128,960]{1,0:T(8,128)(2,1)}, bf16[...) custom-call(s32[16]{0:T(128)} %stack.115.table_ref, ...), custom_call_target="tpu_custom_call" | custom-call | flops 1 | bytes 1 | tf_op jit(solution)/shard_map/pallas_call | solution.py:516
  323.9 6.9 %shard_map.215 = bf16[16,64,960]{2,1,0:T(8,128)(2,1)} custom-call(bf16[128,960]{1,0:T(8,128)(2,1)} %get-tuple-element.352.refs_0_, bf16[128,960]{1,0:T(8,128)(2,1)} %copy-done.45, bf16[128,960]{1,0:T(8,128)(2,1)} %copy-done.35, bf16[128,960]{1,0:T(8,128)(2,1)} %copy-done.48, bf16[64,960]{1,0:T(8,128)(2,1)} %copy-done.68, bf16[64,960]{1,0:T(8,128)(2,1)} %copy-done.69, ...), custom_call_target="tpu_custom_call" | custom-call | flops 1 | bytes 1 | tf_op jit(solution)/shard_map/pallas_call | solution.py:516
  332.6 10.4 %shard_map.216 = bf16[16,192,128]{2,1,0:T(8,128)(2,1)} custom-call(s32[16]{0:T(128)} %select_reduce_fusion.place_ref, bf16[16,192,128]{2,1,0:T(8,128)(2,1)} %copy-done.8, bf16[16,64,128]{2,1,0:T(8,128)(2,1)} %copy-done.53, f32[8,2048]{1,0:T(8,128)} %get-tuple-element.375.lse_ref), custom_call_target="tpu_custom_call" | custom-call | flops 1 | bytes 1 | tf_op jit(solution)/shard_map/pallas_call | solution.py:516
  343.0 6.2 all-to-all-start.5
  369.4 7.4 %collective-permute-done.81.refs_2_ = bf16[256,960]{1,0:T(8,128)(2,1)S(1)} collective-permute-done((bf16[256,960]{1,0:T(8,128)(2,1)S(1)}, bf16[256,960]{1,0:T(8,128)(2,1)S(1)}, u32[]{:S(2)}, u32[]{:S(2)}) %collective-permute-start.81) | collective-permute-done | bytes 491552 | tf_op jit(solution)/shard_map/ppermute | solution.py:49
  377.8 6.9 %shard_map.217 = (f32[128,960]{1,0:T(8,128)}, bf16[144,384]{1,0:T(8,128)(2,1)}, bf16[144,384]{1,0:T(8,128)(2,1)}, bf16[144,384]{1,0:T(8,128)(2,1)}, bf16[144,384...) custom-call(s32[16]{0:T(128)} %stack.115.table_ref, ...), custom_call_target="tpu_custom_call" | custom-call | flops 1 | bytes 1 | tf_op jit(solution)/shard_map/pallas_call | solution.py:516
  404.3 8.9 %shard_map.218 = (bf16[1024,640]{1,0:T(8,128)(2,1)}, bf16[128,960]{1,0:T(8,128)(2,1)}, bf16[128,960]{1,0:T(8,128)(2,1)}, bf16[128,960]{1,0:T(8,128)(2,1)}, bf16[...) custom-call(s32[16]{0:T(128)} %stack.115.table_ref, ...), custom_call_target="tpu_custom_call" | custom-call | flops 1 | bytes 1 | tf_op jit(solution)/shard_map/pallas_call | solution.py:516
  444.3 6.9 %all-to-all-start.6 = ((bf16[16,64,128]{2,1,0:T(8,128)(2,1)}), bf16[16,64,128]{2,1,0:T(8,128)(2,1)S(1)}, u32[]{:S(2)}, u32[]{:S(2)}) async-start(bf16[16,64,128]{2,1,0:T(8,128)(2,1)} %get-tuple-element.418), calls=%async_computation.6 | async-start | bytes 524288 | tf_op jit(solution)/shard_map/all_to_all | solution.py:536
  451.8 7.0 %shard_map.220 = bf16[16,64,960]{2,1,0:T(8,128)(2,1)} custom-call(bf16[128,960]{1,0:T(8,128)(2,1)} %get-tuple-element.301.refs_0_, bf16[128,960]{1,0:T(8,128)(2,1)} %copy-done.39, bf16[128,960]{1,0:T(8,128)(2,1)} %copy-done.29, bf16[128,960]{1,0:T(8,128)(2,1)} %copy-done.40, bf16[64,960]{1,0:T(8,128)(2,1)} %copy-done.64, bf16[64,960]{1,0:T(8,128)(2,1)} %copy-done.65, ...), custom_call_target="tpu_custom_call" | custom-call | flops 1 | bytes 1 | tf_op jit(solution)/shard_map/pallas_call | solution.py:516
  460.8 10.5 %shard_map.221 = bf16[16,192,128]{2,1,0:T(8,128)(2,1)} custom-call(s32[16]{0:T(128)} %select_reduce_fusion.place_ref, bf16[16,192,128]{2,1,0:T(8,128)(2,1)} %copy-done.7, bf16[16,64,128]{2,1,0:T(8,128)(2,1)} %copy-done.54, f32[8,2048]{1,0:T(8,128)} %get-tuple-element.430.lse_ref), custom_call_target="tpu_custom_call" | custom-call | flops 1 | bytes 1 | tf_op jit(solution)/shard_map/pallas_call | solution.py:516
  471.2 6.2 all-to-all-start.7
  501.8 7.0 %shard_map.222 = (f32[128,960]{1,0:T(8,128)}, bf16[144,384]{1,0:T(8,128)(2,1)}, bf16[144,384]{1,0:T(8,128)(2,1)}, bf16[144,384]{1,0:T(8,128)(2,1)}, bf16[144,384...) custom-call(s32[16]{0:T(128)} %stack.115.table_ref, ...), custom_call_target="tpu_custom_call" | custom-call | flops 1 | bytes 1 | tf_op jit(solution)/shard_map/pallas_call | solution.py:516
  508.9 31.9 %reduce-scatter.3.cloned.1.call-done = bf16[64,960]{1,0:T(8,128)(2,1)} async-done(((bf16[1024,960]{1,0:T(8,128)(2,1)}), bf16[64,960]{1,0:T(8,128)(2,1)}) %reduce-scatter.3.cloned.1.call-update) | async-done | bytes 122896 | tf_op jit(solution)/shard_map/reduce_scatter | solution.py:753
  549.7 6.2 all-to-all-done.9
  588.6 17.0 %all-to-all-done.8 = bf16[16,64,384]{2,1,0:T(8,128)(2,1)S(1)} async-done(((bf16[16,64,384]{2,1,0:T(8,128)(2,1)}), bf16[16,64,384]{2,1,0:T(8,128)(2,1)S(1)}, u32[]{:S(2)}, u32[]{:S(2)}) %all-to-all-start.8) | async-done | bytes 786464 | tf_op jit(solution)/shard_map/all_to_all | solution.py:536
  609.3 12.2 %all-to-all-done.10 = bf16[16,64,384]{2,1,0:T(8,128)(2,1)S(1)} async-done(((bf16[16,64,384]{2,1,0:T(8,128)(2,1)}), bf16[16,64,384]{2,1,0:T(8,128)(2,1)S(1)}, u32[]{:S(2)}, u32[]{:S(2)}) %all-to-all-start.10) | async-done | bytes 786464 | tf_op jit(solution)/shard_map/all_to_all | solution.py:536
  621.6 8.5 %all_to_all.65 = bf16[8,16,384]{2,1,0:T(8,128)(2,1)S(1)} all-to-all(bf16[8,16,384]{2,1,0:T(8,128)(2,1)S(1)} %bitcast.88), channel_id=1, replica_groups=mesh['section'=2,'blk'=16,'wshard'=4] {'section','wshard'}, dimensions={0} | all-to-all | bytes 196608 | tf_op jit(solution)/shard_map/all_to_all | solution.py:817
  639.6 11.3 %collective-permute-done.124 = f32[128,960]{1,0:T(8,128)S(1)} collective-permute-done((f32[128,960]{1,0:T(8,128)}, f32[128,960]{1,0:T(8,128)S(1)}, u32[]{:S(2)}, u32[]{:S(2)}) %collective-permute-start.124) | collective-permute-done | bytes 491552 | tf_op jit(solution)/shard_map/ppermute | solution.py:53
  (639 shorter events, 361.0 us)
Async XLA Ops:
  9.8 22.3 %collective-permute-start.3 = (bf16[256,1664]{1,0:T(8,128)(2,1)}, bf16[256,1664]{1,0:T(8,128)(2,1)S(1)}, u32[]{:S(2)}, u32[]{:S(2)}) collective-permute-start(bf16[256,1664]{1,0:T(8,128)(2,1)} %get-tuple-element.266.refs_0_), channel_id=1, source_target_pairs={{0,64},{1,65},{64,2},{65,3},{2,66},{3,67},{66,0},{67,1},{4,68},{5,... | collective-permute-start | bytes 2555912 | tf_op jit(solution)/shard_map/ppermute | solution.py:49
  11.4 21.0 %collective-permute-start.1 = (bf16[256,1664]{1,0:T(8,128)(2,1)}, bf16[256,1664]{1,0:T(8,128)(2,1)S(1)}, u32[]{:S(2)}, u32[]{:S(2)}) collective-permute-start(bf16[256,1664]{1,0:T(8,128)(2,1)} %get-tuple-element.266.refs_0_), channel_id=1, source_target_pairs={{0,66},{1,67},{64,0},{65,1},{2,64},{3,65},{66,2},{67,3},{4,70},{5,... | collective-permute-start | bytes 2555912 | tf_op jit(solution)/shard_map/ppermute | solution.py:49
  48.3 20.3 %collective-permute-start = (bf16[256,1664]{1,0:T(8,128)(2,1)S(1)}, bf16[256,1664]{1,0:T(8,128)(2,1)S(1)}, u32[]{:S(2)}, u32[]{:S(2)}) collective-permute-start(bf16[256,1664]{1,0:T(8,128)(2,1)S(1)} %copy-done.2), channel_id=1, source_target_pairs={{0,1},{1,0},{64,65},{65,64},{2,3},{3,2},{66,67},{67,66},{4,5},{5,4... | collective-permute-start | bytes 2555912 | tf_op jit(solution)/shard_map/ppermute | solution.py:49
  48.8 23.6 %collective-permute-start.2 = (bf16[256,1664]{1,0:T(8,128)(2,1)S(1)}, bf16[256,1664]{1,0:T(8,128)(2,1)}, u32[]{:S(2)}, u32[]{:S(2)}) collective-permute-start(bf16[256,1664]{1,0:T(8,128)(2,1)S(1)} %collective-permute-done.1.refs_2_), channel_id=1, source_target_pairs={{0,1},{1,0},{64,65},{65,64},{2,3},{3,2},{66,67},{67,66},{4,5},{5,4... | collective-permute-start | bytes 2555912 | tf_op jit(solution)/shard_map/ppermute | solution.py:49
  57.9 17.9 %collective-permute-start.8 = (bf16[256,1664]{1,0:T(8,128)(2,1)S(1)}, bf16[256,1664]{1,0:T(8,128)(2,1)}, u32[]{:S(2)}, u32[]{:S(2)}) collective-permute-start(bf16[256,1664]{1,0:T(8,128)(2,1)S(1)} %collective-permute-done.3.refs_8_), channel_id=1, source_target_pairs={{0,1},{1,0},{64,65},{65,64},{2,3},{3,2},{66,67},{67,66},{4,5},{5,4... | collective-permute-start | bytes 2555912 | tf_op jit(solution)/shard_map/ppermute | solution.py:49
  68.7 22.8 %collective-permute-start.21 = (bf16[240,640]{1,0:T(8,128)(2,1)}, bf16[240,640]{1,0:T(8,128)(2,1)}, u32[]{:S(2)}, u32[]{:S(2)}) collective-permute-start(bf16[240,640]{1,0:T(8,128)(2,1)} %get-tuple-element.294), channel_id=1, source_target_pairs={{0,64},{1,65},{64,2},{65,3},{2,66},{3,67},{66,0},{67,1},{4,68},{5,... | collective-permute-start | bytes 921608 | tf_op jit(solution)/shard_map/ppermute | solution.py:49
  68.7 24.3 %collective-permute-start.23 = (bf16[240,640]{1,0:T(8,128)(2,1)}, bf16[240,640]{1,0:T(8,128)(2,1)}, u32[]{:S(2)}, u32[]{:S(2)}) collective-permute-start(bf16[240,640]{1,0:T(8,128)(2,1)} %get-tuple-element.295), channel_id=1, source_target_pairs={{0,66},{1,67},{64,0},{65,1},{2,64},{3,65},{66,2},{67,3},{4,70},{5,... | collective-permute-start | bytes 921608 | tf_op jit(solution)/shard_map/ppermute | solution.py:49
  72.5 18.2 %collective-permute-start.13 = (bf16[128,960]{1,0:T(8,128)(2,1)}, bf16[128,960]{1,0:T(8,128)(2,1)}, u32[]{:S(2)}, u32[]{:S(2)}) collective-permute-start(bf16[128,960]{1,0:T(8,128)(2,1)} %slice.202), channel_id=1, source_target_pairs={{0,64},{1,65},{64,2},{65,3},{2,66},{3,67},{66,0},{67,1},{4,68},{5,... | collective-permute-start | bytes 737288 | tf_op jit(solution)/shard_map/ppermute | solution.py:49
  72.5 19.0 %collective-permute-start.14 = (bf16[128,960]{1,0:T(8,128)(2,1)}, bf16[128,960]{1,0:T(8,128)(2,1)}, u32[]{:S(2)}, u32[]{:S(2)}) collective-permute-start(bf16[128,960]{1,0:T(8,128)(2,1)} %slice.203), channel_id=1, source_target_pairs={{0,66},{1,67},{64,0},{65,1},{2,64},{3,65},{66,2},{67,3},{4,70},{5,... | collective-permute-start | bytes 737288 | tf_op jit(solution)/shard_map/ppermute | solution.py:49
  75.8 18.4 %collective-permute-start.18 = (bf16[240,640]{1,0:T(8,128)(2,1)}, bf16[240,640]{1,0:T(8,128)(2,1)S(1)}, u32[]{:S(2)}, u32[]{:S(2)}) collective-permute-start(bf16[240,640]{1,0:T(8,128)(2,1)} %get-tuple-element.291), channel_id=1, source_target_pairs={{0,1},{1,0},{64,65},{65,64},{2,3},{3,2},{66,67},{67,66},{4,5},{5,4... | collective-permute-start | bytes 921608 | tf_op jit(solution)/shard_map/ppermute | solution.py:49
  82.9 30.2 %all-to-all-start = ((bf16[16,192,128]{2,1,0:T(8,128)(2,1)}), bf16[16,192,128]{2,1,0:T(8,128)(2,1)S(1)}, u32[]{:S(2)}, u32[]{:S(2)}) async-start(bf16[16,192,128]{2,1,0:T(8,128)(2,1)} %get-tuple-element.267), calls=%async_computation | async-start | bytes 1572864 | tf_op jit(solution)/shard_map/all_to_all | solution.py:536
  94.2 35.4 %collective-permute-start.27 = (bf16[960,384]{1,0:T(8,128)(2,1)}, bf16[960,384]{1,0:T(8,128)(2,1)S(1)}, u32[]{:S(2)}, u32[]{:S(2)}) collective-permute-start(bf16[960,384]{1,0:T(8,128)(2,1)} %get-tuple-element.298), channel_id=1, source_target_pairs={{0,64},{64,0},{1,65},{65,1},{2,66},{66,2},{3,67},{67,3},{4,68},{68... | collective-permute-start | bytes 2211848 | tf_op jit(solution)/shard_map/ppermute | solution.py:53
  107.7 21.7 %collective-permute-start.12 = (bf16[256,960]{1,0:T(8,128)(2,1)}, bf16[256,960]{1,0:T(8,128)(2,1)S(1)}, u32[]{:S(2)}, u32[]{:S(2)}) collective-permute-start(bf16[256,960]{1,0:T(8,128)(2,1)} %collective-permute-done.10.refs_2_), channel_id=1, source_target_pairs={{0,1},{1,0},{64,65},{65,64},{2,3},{3,2},{66,67},{67,66},{4,5},{5,4... | collective-permute-start | bytes 1474568 | tf_op jit(solution)/shard_map/ppermute | solution.py:49
  109.2 20.3 %collective-permute-start.17 = (bf16[256,960]{1,0:T(8,128)(2,1)}, bf16[256,960]{1,0:T(8,128)(2,1)S(1)}, u32[]{:S(2)}, u32[]{:S(2)}) collective-permute-start(bf16[256,960]{1,0:T(8,128)(2,1)} %collective-permute-done.11.refs_8_), channel_id=1, source_target_pairs={{0,1},{1,0},{64,65},{65,64},{2,3},{3,2},{66,67},{67,66},{4,5},{5,4... | collective-permute-start | bytes 1474568 | tf_op jit(solution)/shard_map/ppermute | solution.py:49
  109.9 19.7 %collective-permute-start.22 = (bf16[240,640]{1,0:T(8,128)(2,1)}, bf16[240,640]{1,0:T(8,128)(2,1)}, u32[]{:S(2)}, u32[]{:S(2)}) collective-permute-start(bf16[240,640]{1,0:T(8,128)(2,1)} %collective-permute-done.21), channel_id=1, source_target_pairs={{0,64},{1,65},{64,2},{65,3},{2,66},{3,67},{66,0},{67,1},{4,68},{5,... | collective-permute-start | bytes 921608 | tf_op jit(solution)/shard_map/ppermute | solution.py:49
  110.4 19.2 %collective-permute-start.24 = (bf16[240,640]{1,0:T(8,128)(2,1)}, bf16[240,640]{1,0:T(8,128)(2,1)}, u32[]{:S(2)}, u32[]{:S(2)}) collective-permute-start(bf16[240,640]{1,0:T(8,128)(2,1)} %collective-permute-done.23), channel_id=1, source_target_pairs={{0,67},{1,66},{64,1},{65,0},{2,65},{3,64},{66,3},{67,2},{4,71},{5,... | collective-permute-start | bytes 921608 | tf_op jit(solution)/shard_map/ppermute | solution.py:49
  217.8 28.7 %collective-permute-start.54 = (bf16[256,960]{1,0:T(8,128)(2,1)S(1)}, bf16[256,960]{1,0:T(8,128)(2,1)}, u32[]{:S(2)}, u32[]{:S(2)}) collective-permute-start(bf16[256,960]{1,0:T(8,128)(2,1)S(1)} %pad_maximum_fusion.refs_0_), channel_id=1, source_target_pairs={{0,1},{1,0},{64,65},{65,64},{2,3},{3,2},{66,67},{67,66},{4,5},{5,4... | collective-permute-start | bytes 1474568 | tf_op jit(solution)/shard_map/ppermute | solution.py:49
  217.8 28.7 %collective-permute-start.55 = (bf16[256,960]{1,0:T(8,128)(2,1)S(1)}, bf16[256,960]{1,0:T(8,128)(2,1)S(1)}, u32[]{:S(2)}, u32[]{:S(2)}) collective-permute-start(bf16[256,960]{1,0:T(8,128)(2,1)S(1)} %pad_maximum_fusion.refs_0_), channel_id=1, source_target_pairs={{0,66},{1,67},{64,0},{65,1},{2,64},{3,65},{66,2},{67,3},{4,70},{5,... | collective-permute-start | bytes 1474568 | tf_op jit(solution)/shard_map/ppermute | solution.py:49
  219.8 26.7 %collective-permute-start.56 = (bf16[256,960]{1,0:T(8,128)(2,1)S(1)}, bf16[256,960]{1,0:T(8,128)(2,1)}, u32[]{:S(2)}, u32[]{:S(2)}) collective-permute-start(bf16[256,960]{1,0:T(8,128)(2,1)S(1)} %pad_maximum_fusion.refs_0_), channel_id=1, source_target_pairs={{0,64},{1,65},{64,2},{65,3},{2,66},{3,67},{66,0},{67,1},{4,68},{5,... | collective-permute-start | bytes 1474568 | tf_op jit(solution)/shard_map/ppermute | solution.py:49
  331.5 17.8 %collective-permute-start.85 = (bf16[128,960]{1,0:T(8,128)(2,1)}, bf16[128,960]{1,0:T(8,128)(2,1)S(1)}, u32[]{:S(2)}, u32[]{:S(2)}) collective-permute-start(bf16[128,960]{1,0:T(8,128)(2,1)} %get-tuple-element.403), channel_id=1, source_target_pairs={{0,1},{1,0},{64,65},{65,64},{2,3},{3,2},{66,67},{67,66},{4,5},{5,4... | collective-permute-start | bytes 737288 | tf_op jit(solution)/shard_map/ppermute | solution.py:49
  331.6 18.1 %collective-permute-start.84 = (bf16[128,960]{1,0:T(8,128)(2,1)}, bf16[128,960]{1,0:T(8,128)(2,1)}, u32[]{:S(2)}, u32[]{:S(2)}) collective-permute-start(bf16[128,960]{1,0:T(8,128)(2,1)} %get-tuple-element.401), channel_id=1, source_target_pairs={{0,1},{1,0},{64,65},{65,64},{2,3},{3,2},{66,67},{67,66},{4,5},{5,4... | collective-permute-start | bytes 737288 | tf_op jit(solution)/shard_map/ppermute | solution.py:49
  332.0 22.0 %collective-permute-start.88 = (bf16[128,960]{1,0:T(8,128)(2,1)}, bf16[128,960]{1,0:T(8,128)(2,1)S(1)}, u32[]{:S(2)}, u32[]{:S(2)}) collective-permute-start(bf16[128,960]{1,0:T(8,128)(2,1)} %get-tuple-element.405), channel_id=1, source_target_pairs={{0,1},{1,0},{64,65},{65,64},{2,3},{3,2},{66,67},{67,66},{4,5},{5,4... | collective-permute-start | bytes 737288 | tf_op jit(solution)/shard_map/ppermute | solution.py:49
  332.1 29.1 %collective-permute-start.83 = (bf16[128,960]{1,0:T(8,128)(2,1)}, bf16[128,960]{1,0:T(8,128)(2,1)}, u32[]{:S(2)}, u32[]{:S(2)}) collective-permute-start(bf16[128,960]{1,0:T(8,128)(2,1)} %get-tuple-element.399), channel_id=1, source_target_pairs={{0,1},{1,0},{64,65},{65,64},{2,3},{3,2},{66,67},{67,66},{4,5},{5,4... | collective-permute-start | bytes 737288 | tf_op jit(solution)/shard_map/ppermute | solution.py:49
  343.0 33.9 %all-to-all-start.5 = ((bf16[16,192,128]{2,1,0:T(8,128)(2,1)}), bf16[16,192,128]{2,1,0:T(8,128)(2,1)S(1)}, u32[]{:S(2)}, u32[]{:S(2)}) async-start(bf16[16,192,128]{2,1,0:T(8,128)(2,1)} %shard_map.216), calls=%async_computation.5 | async-start | bytes 1572864 | tf_op jit(solution)/shard_map/all_to_all | solution.py:536
  349.2 159.7 %reduce-scatter.5.cloned.1.call-start = ((), (), s32[]{:S(2)}) async-start(), calls=%async_computation.16 | async-start | bytes 2228224 | tf_op jit(solution)/shard_map/reduce_scatter | solution.py:753
  439.3 20.5 %collective-permute-start.108 = (bf16[256,960]{1,0:T(8,128)(2,1)S(1)}, bf16[256,960]{1,0:T(8,128)(2,1)S(1)}, u32[]{:S(2)}, u32[]{:S(2)}) collective-permute-start(bf16[256,960]{1,0:T(8,128)(2,1)S(1)} %collective-permute-done.81.refs_2_), channel_id=1, source_target_pairs={{0,1},{1,0},{64,65},{65,64},{2,3},{3,2},{66,67},{67,66},{4,5},{5,4... | collective-permute-start | bytes 1474568 | tf_op jit(solution)/shard_map/ppermute | solution.py:49
  440.8 19.1 %collective-permute-start.113 = (bf16[256,960]{1,0:T(8,128)(2,1)S(1)}, bf16[256,960]{1,0:T(8,128)(2,1)S(1)}, u32[]{:S(2)}, u32[]{:S(2)}) collective-permute-start(bf16[256,960]{1,0:T(8,128)(2,1)S(1)} %collective-permute-done.82.refs_8_), channel_id=1, source_target_pairs={{0,1},{1,0},{64,65},{65,64},{2,3},{3,2},{66,67},{67,66},{4,5},{5,4... | collective-permute-start | bytes 1474568 | tf_op jit(solution)/shard_map/ppermute | solution.py:49
  451.2 89.7 %reduce-scatter.3.cloned.1.call-start = ((), (), s32[]{:S(2)}) async-start(), calls=%async_computation.15 | async-start | bytes 2228224 | tf_op jit(solution)/shard_map/reduce_scatter | solution.py:753
  471.2 29.6 %all-to-all-start.7 = ((bf16[16,192,128]{2,1,0:T(8,128)(2,1)}), bf16[16,192,128]{2,1,0:T(8,128)(2,1)S(1)}, u32[]{:S(2)}, u32[]{:S(2)}) async-start(bf16[16,192,128]{2,1,0:T(8,128)(2,1)} %shard_map.221), calls=%async_computation.7 | async-start | bytes 1572864 | tf_op jit(solution)/shard_map/all_to_all | solution.py:536
  549.6 116.0 %all-gather.3.cloned.1.call-start = ((), (), s32[]{:S(2)}) async-start(), calls=%async_computation.17 | async-start | bytes 4177920 | tf_op jit(solution)/shard_map/all_gather | solution.py:805
  578.9 26.7 %all-to-all-start.8 = ((bf16[16,64,384]{2,1,0:T(8,128)(2,1)}), bf16[16,64,384]{2,1,0:T(8,128)(2,1)S(1)}, u32[]{:S(2)}, u32[]{:S(2)}) async-start(bf16[16,64,384]{2,1,0:T(8,128)(2,1)} %shard_map.223), calls=%async_computation.8 | async-start | bytes 1572864 | tf_op jit(solution)/shard_map/all_to_all | solution.py:536
  631.5 28.4 %all-to-all-start.12 = ((bf16[16,128,384]{2,1,0:T(8,128)(2,1)}), bf16[16,128,384]{2,1,0:T(8,128)(2,1)S(1)}, u32[]{:S(2)}, u32[]{:S(2)}) async-start(bf16[16,128,384]{2,1,0:T(8,128)(2,1)} %broadcast_in_dim.53), calls=%async_computation.14 | async-start | bytes 3145728 | tf_op jit(solution)/shard_map/all_to_all | solution.py:536
  (243 other events, 3317.9 us)
Sparse Core Ops, SparseCore 0:
  363.4 74.2 reduce-scatter.4
  460.0 80.7 reduce-scatter.2
  556.8 60.7 all-gather.2

commit v5 on v4

--- a/solution.py
+++ b/solution.py
@@ -224,7 +224,7 @@
 def project_kernel(layer, table_ref, x_ref, cos_ref, sin_ref, *refs):
     blocks, (h_ref, out_ref, w_ref, gain_ref, sems) = by_block(refs), refs[10:]
     gain = load_blocks(table_ref, layer, blocks, w_ref, sems, gain_ref)
-    x = x_ref[...]
+    x = x_ref[...].astype(F32)
     h = (x * norm_factor(x) * gain).astype(BF)
     h_ref[...] = h
     cosine, sine = cos_ref[...], sin_ref[...]
@@ -325,7 +325,7 @@
     gain = load_blocks(table_ref, layer, blocks, w_ref, sems, gain_ref)
     mixed = jnp.concatenate([unfold(in_ref[index]) for index in range(H)], axis=1)
     o_ref[...] = mixed
-    x2 = x_ref[...] + dot(mixed, w_ref[...])
+    x2 = x_ref[...].astype(F32) + dot(mixed, w_ref[...])
     x2_ref[...] = x2
     h_ref[...] = (x2 * norm_factor(x2) * gain).astype(BF)
 
@@ -334,7 +334,7 @@
     blocks, (dx2_ref, out_ref, gg_ref, w_ref, gain_ref, sems) = by_block(refs), refs[10:]
     gain = load_blocks(table_ref, layer, blocks, w_ref, sems, gain_ref)
     part, grad_gain = norm_backward(x2_ref[...], gain, dh_ref[...])
-    dx2 = dy_ref[...] + part
+    dx2 = dy_ref[...].astype(F32) + part
     dx2_ref[...] = dx2
     gg_ref[...] = grad_gain
     low = dx2.astype(BF)
@@ -361,7 +361,7 @@
         keys.append(rotate_back(pair[:, :HD], cosine, sine).astype(BF))
         values.append(pair[:, HD:].astype(BF))
     lin_grad = jnp.concatenate(queries + keys + values, axis=1)
-    part, grad_gain = norm_backward(x_ref[...], gain, against(lin_grad, w_ref[:, :QKV]))
+    part, grad_gain = norm_backward(x_ref[...].astype(F32), gain, against(lin_grad, w_ref[:, :QKV]))
     dx_ref[...] = dx2_ref[...] + part
     gains = jnp.concatenate([grad_gain, gg_ref[...], jnp.zeros((14, D), F32)], axis=0).astype(BF)
     low = dx2_ref[...].astype(BF)
@@ -574,8 +574,8 @@
             owners += [there % 2, 2 * (there // 2) + (core ^ flip)]
     table = jnp.stack(owners).astype(jnp.int32)
 
-    x0 = lax.dynamic_index_in_dim(tokens[:, 0], section, 0, keepdims=False).astype(F32)
-    cot = lax.dynamic_index_in_dim(cotangent[:, 0], section, 0, keepdims=False).astype(F32)
+    x0 = lax.dynamic_index_in_dim(tokens[:, 0], section, 0, keepdims=False)
+    cot = lax.dynamic_index_in_dim(cotangent[:, 0], section, 0, keepdims=False)
     first, second = call(
         pack_attend_kernel,
         [
@@ -597,12 +597,7 @@
         [pltpu.VMEM((8, SHARE, 2 * UNITS), BF)],
     )
     wqkv = sum(gather_eight(first), [])
-    second, pieces, sent = after((second, pieces, sent), wqkv[4:6])
-    wout_near = gather_near(second)
-    pieces, sent = after((pieces, sent), wout_near)
-    wgu = exchange_eight(pieces)
-    other = swap_section(sent)
-    wout = sum(arranged(wout_near, gather_far(wout_near)), [])
+    later = {}
 
     block_index = lax.axis_index("blk")
     own_block = lax.dynamic_index_in_dim(span_order, block_index, 0, keepdims=False)
@@ -645,11 +640,13 @@
         )
         heads = exchange(heads)
         heads, beside = lax.optimization_barrier((heads, late(first)))
+        if layer == 0:
+            later.update(beside)
         mixed, x2, h2 = call(
             functools.partial(mix_kernel, layer),
             [SMEM, whole(HEADS), rows] + weights,
             [((ROWS, D), BF), ((ROWS, D), F32), ((ROWS, D), BF)],
-            (table, heads, x, *wout),
+            (table, heads, x, *later["out"]),
             weight_scratch(D),
         )
         found = gather_eight(h2)
@@ -665,7 +662,7 @@
                 [SMEM] + row_specs(blocks) + [HBM] * 8 + [half_down, half_down],
                 [((size * ROWS, 2 * UNITS), F32), ((size * ROWS, UNITS), BF)]
                 + [((ROWS, D), BF)] * size,
-                (table, *blocks, *wgu, kept, other),
+                (table, *blocks, *later["feed"], kept, later["down"]),
                 feed_scratch,
             )
             kept_ff.append((blocks, lin, hidden))
@@ -691,7 +688,7 @@
                 + [half_down, half_down]
                 + [whole((size * ROWS, 2 * UNITS))],
                 [((size * ROWS, 2 * UNITS), BF)] + [((ROWS, D), BF)] * size,
-                (table, *blocks, *wgu, kept, other, lin),
+                (table, *blocks, *later["feed"], kept, later["down"], lin),
                 feed_scratch,
             )
             branches += blocks
@@ -703,7 +700,7 @@
             functools.partial(mix_back_kernel, layer),
             [SMEM, rows, rows, rows] + weights,
             [((ROWS, D), F32), (HEADS, BF), ((1, D), F32)],
-            (table, dy, dh2, x2, *wout),
+            (table, dy, dh2, x2, *later["out"]),
             weight_scratch(D),
         )
         normed = sum([item[0] for item in kept_ff], [])
@@ -758,18 +755,31 @@
         return jnp.where(section == 0, jnp.stack([own, other]), jnp.stack([other, own]))
 
     gain_owner = ((4 * section + shard) // 2).astype(jnp.int32).reshape(1)
-    parts, (wout, wgu, other), kept0 = forward(
-        0, x0, lambda packed: wout_near, lambda first: (wout, wgu, other)
-    )
+    def first_weights(packed):
+        later["near"] = gather_near(after(second, packed))
+        return later["near"]
+
+    def last_weights(first):
+        near = later.pop("near")
+        ready = after(pieces, near)
+        for number in (3, 4, 5, 7):
+            ready[number] = after(pieces[number], first)
+        halves = after(sent, first)
+        return {
+            "out": sum(arranged(near, gather_far(near)), []),
+            "feed": exchange_eight(ready),
+            "down": swap_section(halves),
+        }
+
+    parts, _, kept0 = forward(0, x0, first_weights, last_weights)
     y0 = (kept0[4] + scatter_eight(parts)).astype(BF)
-    cot_low = cot.astype(BF)
     parts1, (found_cot, near0), kept1 = forward(
         1,
-        y0.astype(F32),
-        lambda packed: gather_near(after(cot_low, packed)),
+        y0,
+        lambda packed: gather_near(after(cot, packed)),
         lambda near: (arranged(near, gather_far(near)), gather_near(after(kept0[1], near))),
     )
-    dx1, lin1, grad_ff1, (both0, near1, y1) = backward(
+    dx1, lin1, grad_ff1, (both0, near1) = backward(
         1,
         cot,
         found_cot,
@@ -778,35 +788,35 @@
         lambda first: (
             first[0],
             gather_near(after(kept1[1], first[1])),
-            kept1[4] + scatter_eight(after(parts1, first[1])),
         ),
     )
-    y1 = y1.astype(BF)
     dy0 = dx1.astype(BF)
     ff1 = sum_feed(grad_ff1)
-    dx0, lin0, grad_ff0, (both1, lin1, layer_outputs) = backward(
+    dx0, lin0, grad_ff0, (both1, lin1) = backward(
         0,
-        dy0.astype(F32),
+        dy0,
         gather_eight(dy0),
         kept0,
         lambda dx2: (arranged(near1, gather_far(after(near1, dx2))), dx2),
         lambda first: (
             first[0],
             exchange_eight(after(lin1, first[1])),
-            by_section(y0, after(y1, first[1])),
         ),
     )
-    ff0, ff1 = after((sum_feed(grad_ff0), ff1), dx0)
+    att1 = attend_grads(sum(both1, []), after(lin1, dx0))
+    lin0 = exchange_eight(lin0)
+    ff0, ff1, lin0 = after((sum_feed(grad_ff0), ff1, lin0), att1)
+    att0 = attend_grads(sum(both0, []), lin0)
+    y1 = (kept1[4] + scatter_eight(after(parts1, att0))).astype(BF)
+    layer_outputs = by_section(y0, y1)
     upper = 2 * UNITS
     spread = jnp.stack([ff0[:, :upper], ff1[:, :upper]]).reshape(8, PIECE, upper)
     spread = lax.all_to_all(spread, EIGHT, 0, 0, tiled=True).reshape(8 * PIECE, upper)
     lower = by_section(ff0[:, upper:], ff1[:, upper:])
     lower = jnp.concatenate([lower[0], lower[1]], axis=1)
     found = lax.all_gather(jnp.concatenate([spread, lower], axis=0), "blk", axis=0)
-    att1 = sum_over_blocks(after(attend_grads(sum(both1, []), after(lin1, dx0)), spread))
-    att0 = attend_grads(sum(both0, []), exchange_eight(lin0))
     input_grads = by_section(dx0, dx1)
-    att0 = sum_over_blocks(att0)
+    att1, att0 = sum_over_blocks(att1), sum_over_blocks(att0)
     grad_gate, grad_up, grad_down = call(
         finish_feed_kernel,
         [whole(found.shape)],

time: 689 us -> 668 us (0.970)
  starting transfers between devices: 192 us -> 180 us
  local copies, waits for them, and re-layouts: 31.7 us -> 22.7 us
  blocking collectives: 8.49 us -> 16.6 us
  other arithmetic: 26.6 us -> 19 us
    ppermute x131, waiting for transfers between devices: 143 us -> 169 us  [hop(): return lax.ppermute(array, EIGHT, ring_pairs(step, flip))]
    all_to_all x11 -> x10, waiting for transfers between devices: 54.4 us -> 34 us  [exchange(): return lax.all_to_all(array, 'blk', 0, 0, tiled=True)]
    all_to_all x11 -> x10, starting transfers between devices: 61.3 us -> 50.1 us  [exchange(): return lax.all_to_all(array, 'blk', 0, 0, tiled=True)]
    reduce_scatter x2, waiting for transfers between devices: 32 us -> 22.2 us  [sum_feed(): return lax.psum_scatter(flat, 'blk', scatter_dimension=0, tiled=True)]
    all_to_all x1, blocking collectives: 8.49 us -> 16.6 us  [exchange(): return lax.all_to_all(array, 'blk', 0, 0, tiled=True)]
    unnamed x253 -> x250, local copies, waits for them, and re-layouts: 17 us -> 10.4 us
  transfers between devices with their start and end apart: 150 -> 150, of which waited for: 65 -> 68; matrix products, arithmetic and copies ran while one was open for 6% -> 4% of each run, Pallas kernels for 15% -> 13%
where the time goes in v5:
time: 668 us; the launch traced here: 656 us
  waiting for transfers between devices  245 us (37%)
  starting transfers between devices  180 us (27%)
  Pallas kernels  156 us (23%)
  local copies, waits for them, and re-layouts  22.7 us (3%)
  other arithmetic  19 us (3%)
  between operations  17.1 us (3%)
  blocking collectives  16.6 us (2%)
    ppermute x131, waiting for transfers between devices, hop(): return lax.ppermute(array, EIGHT, ring_pairs(step, flip))  169 us
    pallas_call x24, Pallas kernels, call(): pl.pallas_call(kernel, grid=(1,), in_specs=in_specs, out_specs=[whole(sha...  156 us
    ppermute x131, starting transfers between devices, hop(): return lax.ppermute(array, EIGHT, ring_pairs(step, flip))  119 us
    all_to_all x10, starting transfers between devices, exchange(): return lax.all_to_all(array, 'blk', 0, 0, tiled=True)  50.1 us
    all_to_all x10, waiting for transfers between devices, exchange(): return lax.all_to_all(array, 'blk', 0, 0, tiled=True)  34 us
    reduce_scatter x2, waiting for transfers between devices, sum_feed(): return lax.psum_scatter(flat, 'blk', scatter_dimension=0, tiled=True)  22.2 us
    all_to_all x1, blocking collectives, exchange(): return lax.all_to_all(array, 'blk', 0, 0, tiled=True)  16.6 us
  transfers between devices with their start and end apart: 150, of which 68 were waited for; matrix products, arithmetic and copies ran while one was open for 4% of the time, Pallas kernels for 13%

profile of v5, /device:TPU:0, one launch (start us, length us, event | category | flops | bytes accessed | tf_op | source)
XLA Modules:
  0.0 656.0 jit_solution(7742435467685755387)
XLA Ops:
  13.0 19.0 %collective-permute-done.3.refs_8_ = bf16[256,1664]{1,0:T(8,128)(2,1)S(1)} collective-permute-done((bf16[256,1664]{1,0:T(8,128)(2,1)}, bf16[256,1664]{1,0:T(8,128)(2,1)S(1)}, u32[]{:S(2)}, u32[]{:S(2)}) %collective-permute-start.3) | collective-permute-done | bytes 852000 | tf_op jit(solution)/shard_map/ppermute | solution.py:49
  48.6 5.9 shard_map.204
  58.3 7.8 %all-to-all-start = ((bf16[16,192,128]{2,1,0:T(8,128)(2,1)}), bf16[16,192,128]{2,1,0:T(8,128)(2,1)}, u32[]{:S(2)}, u32[]{:S(2)}) async-start(bf16[16,192,128]{2,1,0:T(8,128)(2,1)} %get-tuple-element.263), calls=%async_computation | async-start | bytes 1572864 | tf_op jit(solution)/shard_map/all_to_all | solution.py:536
  99.5 17.1 %collective-permute-done.16 = bf16[240,640]{1,0:T(8,128)(2,1)S(1)} collective-permute-done((bf16[240,640]{1,0:T(8,128)(2,1)}, bf16[240,640]{1,0:T(8,128)(2,1)S(1)}, u32[]{:S(2)}, u32[]{:S(2)}) %collective-permute-start.16) | collective-permute-done | bytes 307232 | tf_op jit(solution)/shard_map/ppermute | solution.py:49
  119.6 8.1 %shard_map.205 = (bf16[16,64,128]{2,1,0:T(8,128)(2,1)}, f32[8,2048]{1,0:T(8,128)}) custom-call(s32[16]{0:T(128)} %select_reduce_fusion.place_ref, bf16[16,192,128]{2,1,0:T(8,128)(2,1)} %all-to-all-done.in_ref), custom_call_target="tpu_custom_call" | custom-call | flops 1 | bytes 1 | tf_op jit(solution)/shard_map/pallas_call | solution.py:516
  127.7 16.6 %all_to_all.65.in_ref = bf16[16,64,128]{2,1,0:T(8,128)(2,1)} all-to-all(bf16[16,64,128]{2,1,0:T(8,128)(2,1)} %get-tuple-element.267), channel_id=1, replica_groups=mesh['section'=2,'blk'=16,'wshard'=4] {'blk'}, dimensions={0} | all-to-all | bytes 524288 | tf_op jit(solution)/shard_map/all_to_all | solution.py:536
  153.6 6.3 collective-permute-done.31.refs_8_
  169.4 8.4 %shard_map.208 = (f32[1024,640]{1,0:T(8,128)}, bf16[1024,320]{1,0:T(8,128)(2,1)}, bf16[128,960]{1,0:T(8,128)(2,1)}, bf16[128,960]{1,0:T(8,128)(2,1)}, bf16[128,9...) custom-call(s32[16]{0:T(128)} %stack.115.table_ref, ...), custom_call_target="tpu_custom_call" | custom-call | flops 1 | bytes 1 | tf_op jit(solution)/shard_map/pallas_call | solution.py:516
  201.7 6.0 shard_map.209
  213.9 6.5 collective-permute-done.46.refs_2_.refs_12_
  231.9 8.1 %shard_map.210 = (bf16[16,64,128]{2,1,0:T(8,128)(2,1)}, f32[8,2048]{1,0:T(8,128)}) custom-call(s32[16]{0:T(128)} %select_reduce_fusion.place_ref, bf16[16,192,128]{2,1,0:T(8,128)(2,1)} %copy-done.11), custom_call_target="tpu_custom_call" | custom-call | flops 1 | bytes 1 | tf_op jit(solution)/shard_map/pallas_call | solution.py:516
  245.0 8.7 %all-to-all-done.3.in_ref = bf16[16,64,128]{2,1,0:T(8,128)(2,1)S(1)} async-done(((bf16[16,64,128]{2,1,0:T(8,128)(2,1)}), bf16[16,64,128]{2,1,0:T(8,128)(2,1)S(1)}, u32[]{:S(2)}, u32[]{:S(2)}) %all-to-all-start.3) | async-done | bytes 262176 | tf_op jit(solution)/shard_map/all_to_all | solution.py:536
  262.9 6.0 collective-permute-done.60.refs_8_
  278.0 8.5 %shard_map.212 = (f32[1024,640]{1,0:T(8,128)}, bf16[1024,320]{1,0:T(8,128)(2,1)}, bf16[128,960]{1,0:T(8,128)(2,1)}, bf16[128,960]{1,0:T(8,128)(2,1)}, bf16[128,9...) custom-call(s32[16]{0:T(128)} %stack.115.table_ref, ...), custom_call_target="tpu_custom_call" | custom-call | flops 1 | bytes 1 | tf_op jit(solution)/shard_map/pallas_call | solution.py:516
  286.6 8.7 %shard_map.213 = (bf16[1024,640]{1,0:T(8,128)(2,1)}, bf16[128,960]{1,0:T(8,128)(2,1)}, bf16[128,960]{1,0:T(8,128)(2,1)}, bf16[128,960]{1,0:T(8,128)(2,1)}, bf16[...) custom-call(s32[16]{0:T(128)} %stack.115.table_ref, ...), custom_call_target="tpu_custom_call" | custom-call | flops 1 | bytes 1 | tf_op jit(solution)/shard_map/pallas_call | solution.py:516
  335.0 6.9 %shard_map.215 = bf16[16,64,960]{2,1,0:T(8,128)(2,1)} custom-call(bf16[128,960]{1,0:T(8,128)(2,1)} %get-tuple-element.334.refs_0_, bf16[128,960]{1,0:T(8,128)(2,1)} %copy-done.48, bf16[128,960]{1,0:T(8,128)(2,1)} %copy-done.38, bf16[128,960]{1,0:T(8,128)(2,1)} %copy-done.51, bf16[64,960]{1,0:T(8,128)(2,1)} %copy-done.68, bf16[64,960]{1,0:T(8,128)(2,1)} %copy-done.69, ...), custom_call_target="tpu_custom_call" | custom-call | flops 1 | bytes 1 | tf_op jit(solution)/shard_map/pallas_call | solution.py:516
  342.7 10.4 %shard_map.216 = bf16[16,192,128]{2,1,0:T(8,128)(2,1)} custom-call(s32[16]{0:T(128)} %select_reduce_fusion.place_ref, bf16[16,192,128]{2,1,0:T(8,128)(2,1)} %copy-done.11, bf16[16,64,128]{2,1,0:T(8,128)(2,1)} %copy-done.55, f32[8,2048]{1,0:T(8,128)} %get-tuple-element.374.lse_ref), custom_call_target="tpu_custom_call" | custom-call | flops 1 | bytes 1 | tf_op jit(solution)/shard_map/pallas_call | solution.py:516
  361.1 12.1 %collective-permute-done.81.refs_2_ = bf16[256,960]{1,0:T(8,128)(2,1)S(1)} collective-permute-done((bf16[256,960]{1,0:T(8,128)(2,1)S(1)}, bf16[256,960]{1,0:T(8,128)(2,1)S(1)}, u32[]{:S(2)}, u32[]{:S(2)}) %collective-permute-start.81) | collective-permute-done | bytes 491552 | tf_op jit(solution)/shard_map/ppermute | solution.py:49
  376.7 6.9 %shard_map.217 = (f32[128,960]{1,0:T(8,128)}, bf16[144,384]{1,0:T(8,128)(2,1)}, bf16[144,384]{1,0:T(8,128)(2,1)}, bf16[144,384]{1,0:T(8,128)(2,1)}, bf16[144,384...) custom-call(s32[16]{0:T(128)} %stack.115.table_ref, ...), custom_call_target="tpu_custom_call" | custom-call | flops 1 | bytes 1 | tf_op jit(solution)/shard_map/pallas_call | solution.py:516
  401.8 8.8 %shard_map.218 = (bf16[1024,640]{1,0:T(8,128)(2,1)}, bf16[128,960]{1,0:T(8,128)(2,1)}, bf16[128,960]{1,0:T(8,128)(2,1)}, bf16[128,960]{1,0:T(8,128)(2,1)}, bf16[...) custom-call(s32[16]{0:T(128)} %stack.115.table_ref, ...), custom_call_target="tpu_custom_call" | custom-call | flops 1 | bytes 1 | tf_op jit(solution)/shard_map/pallas_call | solution.py:516
  442.8 7.4 %all-to-all-start.6 = ((bf16[16,64,128]{2,1,0:T(8,128)(2,1)}), bf16[16,64,128]{2,1,0:T(8,128)(2,1)S(1)}, u32[]{:S(2)}, u32[]{:S(2)}) async-start(bf16[16,64,128]{2,1,0:T(8,128)(2,1)} %get-tuple-element.409), calls=%async_computation.6 | async-start | bytes 524288 | tf_op jit(solution)/shard_map/all_to_all | solution.py:536
  450.9 6.9 %shard_map.220 = bf16[16,64,960]{2,1,0:T(8,128)(2,1)} custom-call(bf16[128,960]{1,0:T(8,128)(2,1)} %get-tuple-element.302.refs_0_, bf16[128,960]{1,0:T(8,128)(2,1)} %copy-done.43, bf16[128,960]{1,0:T(8,128)(2,1)} %copy-done.32, bf16[128,960]{1,0:T(8,128)(2,1)} %copy-done.44, bf16[64,960]{1,0:T(8,128)(2,1)} %copy-done.64, bf16[64,960]{1,0:T(8,128)(2,1)} %copy-done.65, ...), custom_call_target="tpu_custom_call" | custom-call | flops 1 | bytes 1 | tf_op jit(solution)/shard_map/pallas_call | solution.py:516
  459.9 10.5 %shard_map.221 = bf16[16,192,128]{2,1,0:T(8,128)(2,1)} custom-call(s32[16]{0:T(128)} %select_reduce_fusion.place_ref, bf16[16,192,128]{2,1,0:T(8,128)(2,1)} %all-to-all-done.in_ref, bf16[16,64,128]{2,1,0:T(8,128)(2,1)} %copy-done.54, f32[8,2048]{1,0:T(8,128)} %get-tuple-element.423.lse_ref), custom_call_target="tpu_custom_call" | custom-call | flops 1 | bytes 1 | tf_op jit(solution)/shard_map/pallas_call | solution.py:516
  470.5 6.0 all-to-all-start.7
  494.2 6.8 %shard_map.222 = (f32[128,960]{1,0:T(8,128)}, bf16[144,384]{1,0:T(8,128)(2,1)}, bf16[144,384]{1,0:T(8,128)(2,1)}, bf16[144,384]{1,0:T(8,128)(2,1)}, bf16[144,384...) custom-call(s32[16]{0:T(128)} %stack.115.table_ref, ...), custom_call_target="tpu_custom_call" | custom-call | flops 1 | bytes 1 | tf_op jit(solution)/shard_map/pallas_call | solution.py:516
  517.2 22.1 %reduce-scatter.3.cloned.1.call-done = bf16[64,960]{1,0:T(8,128)(2,1)} async-done(((bf16[1024,960]{1,0:T(8,128)(2,1)}), bf16[64,960]{1,0:T(8,128)(2,1)}) %reduce-scatter.3.cloned.1.call-update) | async-done | bytes 122896 | tf_op jit(solution)/shard_map/reduce_scatter | solution.py:750
  548.3 6.2 all-to-all-done.12
  564.9 11.8 %all-to-all-done.9 = bf16[16,64,384]{2,1,0:T(8,128)(2,1)S(1)} async-done(((bf16[16,64,384]{2,1,0:T(8,128)(2,1)}), bf16[16,64,384]{2,1,0:T(8,128)(2,1)S(1)}, u32[]{:S(2)}, u32[]{:S(2)}) %all-to-all-start.9) | async-done | bytes 786464 | tf_op jit(solution)/shard_map/all_to_all | solution.py:536
  588.1 9.4 %all-to-all-done.8 = bf16[16,64,384]{2,1,0:T(8,128)(2,1)S(1)} async-done(((bf16[16,64,384]{2,1,0:T(8,128)(2,1)}), bf16[16,64,384]{2,1,0:T(8,128)(2,1)S(1)}, u32[]{:S(2)}, u32[]{:S(2)}) %all-to-all-start.8) | async-done | bytes 786464 | tf_op jit(solution)/shard_map/all_to_all | solution.py:536
  615.1 7.7 %collective-permute-done.128 = bf16[128,960]{1,0:T(8,128)(2,1)S(1)} collective-permute-done((bf16[128,960]{1,0:T(8,128)(2,1)S(1)}, bf16[128,960]{1,0:T(8,128)(2,1)S(1)}, u32[]{:S(2)}, u32[]{:S(2)}) %collective-permute-start.128) | collective-permute-done | bytes 245792 | tf_op jit(solution)/shard_map/ppermute | solution.py:49
  624.6 7.4 %collective-permute-done.133 = f32[128,960]{1,0:T(8,128)S(1)} collective-permute-done((f32[128,960]{1,0:T(8,128)S(1)}, f32[128,960]{1,0:T(8,128)S(1)}, u32[]{:S(2)}, u32[]{:S(2)}) %collective-permute-start.133) | collective-permute-done | bytes 491552 | tf_op jit(solution)/shard_map/ppermute | solution.py:53
  643.6 5.6 shard_map.226
  (635 shorter events, 344.1 us)
Async XLA Ops:
  9.8 22.3 %collective-permute-start.3 = (bf16[256,1664]{1,0:T(8,128)(2,1)}, bf16[256,1664]{1,0:T(8,128)(2,1)S(1)}, u32[]{:S(2)}, u32[]{:S(2)}) collective-permute-start(bf16[256,1664]{1,0:T(8,128)(2,1)} %get-tuple-element.262.refs_0_), channel_id=1, source_target_pairs={{0,64},{1,65},{64,2},{65,3},{2,66},{3,67},{66,0},{67,1},{4,68},{5,... | collective-permute-start | bytes 2555912 | tf_op jit(solution)/shard_map/ppermute | solution.py:49
  11.5 21.7 %collective-permute-start.1 = (bf16[256,1664]{1,0:T(8,128)(2,1)}, bf16[256,1664]{1,0:T(8,128)(2,1)S(1)}, u32[]{:S(2)}, u32[]{:S(2)}) collective-permute-start(bf16[256,1664]{1,0:T(8,128)(2,1)} %get-tuple-element.262.refs_0_), channel_id=1, source_target_pairs={{0,66},{1,67},{64,0},{65,1},{2,64},{3,65},{66,2},{67,3},{4,70},{5,... | collective-permute-start | bytes 2555912 | tf_op jit(solution)/shard_map/ppermute | solution.py:49
  55.1 20.6 %collective-permute-start.9 = (bf16[256,960]{1,0:T(8,128)(2,1)}, bf16[256,960]{1,0:T(8,128)(2,1)S(1)}, u32[]{:S(2)}, u32[]{:S(2)}) collective-permute-start(bf16[256,960]{1,0:T(8,128)(2,1)} %get-tuple-element.291.refs_0_), channel_id=1, source_target_pairs={{0,1},{1,0},{64,65},{65,64},{2,3},{3,2},{66,67},{67,66},{4,5},{5,4... | collective-permute-start | bytes 1474568 | tf_op jit(solution)/shard_map/ppermute | solution.py:49
  55.2 20.6 %collective-permute-start.10 = (bf16[256,960]{1,0:T(8,128)(2,1)}, bf16[256,960]{1,0:T(8,128)(2,1)S(1)}, u32[]{:S(2)}, u32[]{:S(2)}) collective-permute-start(bf16[256,960]{1,0:T(8,128)(2,1)} %get-tuple-element.291.refs_0_), channel_id=1, source_target_pairs={{0,66},{1,67},{64,0},{65,1},{2,64},{3,65},{66,2},{67,3},{4,70},{5,... | collective-permute-start | bytes 1474568 | tf_op jit(solution)/shard_map/ppermute | solution.py:49
  58.3 28.5 %all-to-all-start = ((bf16[16,192,128]{2,1,0:T(8,128)(2,1)}), bf16[16,192,128]{2,1,0:T(8,128)(2,1)}, u32[]{:S(2)}, u32[]{:S(2)}) async-start(bf16[16,192,128]{2,1,0:T(8,128)(2,1)} %get-tuple-element.263), calls=%async_computation | async-start | bytes 1572864 | tf_op jit(solution)/shard_map/all_to_all | solution.py:536
  75.8 18.3 %collective-permute-start.22 = (bf16[256,960]{1,0:T(8,128)(2,1)S(1)}, bf16[256,960]{1,0:T(8,128)(2,1)S(1)}, u32[]{:S(2)}, u32[]{:S(2)}) collective-permute-start(bf16[256,960]{1,0:T(8,128)(2,1)S(1)} %collective-permute-done.10.refs_2_), channel_id=1, source_target_pairs={{0,1},{1,0},{64,65},{65,64},{2,3},{3,2},{66,67},{67,66},{4,5},{5,4... | collective-permute-start | bytes 1474568 | tf_op jit(solution)/shard_map/ppermute | solution.py:49
  92.1 52.3 %collective-permute-start.12 = (bf16[960,384]{1,0:T(8,128)(2,1)}, bf16[960,384]{1,0:T(8,128)(2,1)S(1)}, u32[]{:S(2)}, u32[]{:S(2)}) collective-permute-start(bf16[960,384]{1,0:T(8,128)(2,1)} %get-tuple-element.273), channel_id=1, source_target_pairs={{0,64},{64,0},{1,65},{65,1},{2,66},{66,2},{3,67},{67,3},{4,68},{68... | collective-permute-start | bytes 2211848 | tf_op jit(solution)/shard_map/ppermute | solution.py:53
  92.7 23.8 %collective-permute-start.16 = (bf16[240,640]{1,0:T(8,128)(2,1)}, bf16[240,640]{1,0:T(8,128)(2,1)S(1)}, u32[]{:S(2)}, u32[]{:S(2)}) collective-permute-start(bf16[240,640]{1,0:T(8,128)(2,1)} %get-tuple-element.286), channel_id=1, source_target_pairs={{0,64},{1,65},{64,2},{65,3},{2,66},{3,67},{66,0},{67,1},{4,68},{5,... | collective-permute-start | bytes 921608 | tf_op jit(solution)/shard_map/ppermute | solution.py:49
  94.1 24.8 %collective-permute-start.18 = (bf16[240,640]{1,0:T(8,128)(2,1)}, bf16[240,640]{1,0:T(8,128)(2,1)S(1)}, u32[]{:S(2)}, u32[]{:S(2)}) collective-permute-start(bf16[240,640]{1,0:T(8,128)(2,1)} %get-tuple-element.287), channel_id=1, source_target_pairs={{0,66},{1,67},{64,0},{65,1},{2,64},{3,65},{66,2},{67,3},{4,70},{5,... | collective-permute-start | bytes 921608 | tf_op jit(solution)/shard_map/ppermute | solution.py:49
  97.7 46.6 %collective-permute-start.15 = (bf16[240,640]{1,0:T(8,128)(2,1)}, bf16[240,640]{1,0:T(8,128)(2,1)S(1)}, u32[]{:S(2)}, u32[]{:S(2)}) collective-permute-start(bf16[240,640]{1,0:T(8,128)(2,1)} %get-tuple-element.285), channel_id=1, source_target_pairs={{0,67},{1,66},{64,1},{65,0},{2,65},{3,64},{66,3},{67,2},{4,71},{5,... | collective-permute-start | bytes 921608 | tf_op jit(solution)/shard_map/ppermute | solution.py:49
  99.4 44.9 %collective-permute-start.21 = (bf16[240,640]{1,0:T(8,128)(2,1)}, bf16[240,640]{1,0:T(8,128)(2,1)S(1)}, u32[]{:S(2)}, u32[]{:S(2)}) collective-permute-start(bf16[240,640]{1,0:T(8,128)(2,1)} %get-tuple-element.289), channel_id=1, source_target_pairs={{0,65},{1,64},{64,3},{65,2},{2,67},{3,66},{66,1},{67,0},{4,69},{5,... | collective-permute-start | bytes 921608 | tf_op jit(solution)/shard_map/ppermute | solution.py:49
  116.6 27.7 %collective-permute-start.17 = (bf16[240,640]{1,0:T(8,128)(2,1)S(1)}, bf16[240,640]{1,0:T(8,128)(2,1)S(1)}, u32[]{:S(2)}, u32[]{:S(2)}) collective-permute-start(bf16[240,640]{1,0:T(8,128)(2,1)S(1)} %collective-permute-done.16), channel_id=1, source_target_pairs={{0,64},{1,65},{64,2},{65,3},{2,66},{3,67},{66,0},{67,1},{4,68},{5,... | collective-permute-start | bytes 921608 | tf_op jit(solution)/shard_map/ppermute | solution.py:49
  118.9 25.4 %collective-permute-start.19 = (bf16[240,640]{1,0:T(8,128)(2,1)S(1)}, bf16[240,640]{1,0:T(8,128)(2,1)S(1)}, u32[]{:S(2)}, u32[]{:S(2)}) collective-permute-start(bf16[240,640]{1,0:T(8,128)(2,1)S(1)} %collective-permute-done.18), channel_id=1, source_target_pairs={{0,67},{1,66},{64,1},{65,0},{2,65},{3,64},{66,3},{67,2},{4,71},{5,... | collective-permute-start | bytes 921608 | tf_op jit(solution)/shard_map/ppermute | solution.py:49
  227.8 26.0 %collective-permute-start.54 = (bf16[256,960]{1,0:T(8,128)(2,1)S(1)}, bf16[256,960]{1,0:T(8,128)(2,1)}, u32[]{:S(2)}, u32[]{:S(2)}) collective-permute-start(bf16[256,960]{1,0:T(8,128)(2,1)S(1)} %pad_maximum_fusion.refs_0_), channel_id=1, source_target_pairs={{0,1},{1,0},{64,65},{65,64},{2,3},{3,2},{66,67},{67,66},{4,5},{5,4... | collective-permute-start | bytes 1474568 | tf_op jit(solution)/shard_map/ppermute | solution.py:49
  227.8 26.0 %collective-permute-start.55 = (bf16[256,960]{1,0:T(8,128)(2,1)S(1)}, bf16[256,960]{1,0:T(8,128)(2,1)S(1)}, u32[]{:S(2)}, u32[]{:S(2)}) collective-permute-start(bf16[256,960]{1,0:T(8,128)(2,1)S(1)} %pad_maximum_fusion.refs_0_), channel_id=1, source_target_pairs={{0,66},{1,67},{64,0},{65,1},{2,64},{3,65},{66,2},{67,3},{4,70},{5,... | collective-permute-start | bytes 1474568 | tf_op jit(solution)/shard_map/ppermute | solution.py:49
  228.0 25.8 %collective-permute-start.56 = (bf16[256,960]{1,0:T(8,128)(2,1)S(1)}, bf16[256,960]{1,0:T(8,128)(2,1)S(1)}, u32[]{:S(2)}, u32[]{:S(2)}) collective-permute-start(bf16[256,960]{1,0:T(8,128)(2,1)S(1)} %pad_maximum_fusion.refs_0_), channel_id=1, source_target_pairs={{0,64},{1,65},{64,2},{65,3},{2,66},{3,67},{66,0},{67,1},{4,68},{5,... | collective-permute-start | bytes 1474568 | tf_op jit(solution)/shard_map/ppermute | solution.py:49
  324.0 18.0 %collective-permute-start.79 = (bf16[256,960]{1,0:T(8,128)(2,1)S(1)}, bf16[256,960]{1,0:T(8,128)(2,1)S(1)}, u32[]{:S(2)}, u32[]{:S(2)}) collective-permute-start(bf16[256,960]{1,0:T(8,128)(2,1)S(1)} %collective-permute-done.56.refs_8_), channel_id=1, source_target_pairs={{0,1},{1,0},{64,65},{65,64},{2,3},{3,2},{66,67},{67,66},{4,5},{5,4... | collective-permute-start | bytes 1474568 | tf_op jit(solution)/shard_map/ppermute | solution.py:49
  324.1 17.9 %collective-permute-start.74 = (bf16[256,960]{1,0:T(8,128)(2,1)S(1)}, bf16[256,960]{1,0:T(8,128)(2,1)S(1)}, u32[]{:S(2)}, u32[]{:S(2)}) collective-permute-start(bf16[256,960]{1,0:T(8,128)(2,1)S(1)} %collective-permute-done.55.refs_2_), channel_id=1, source_target_pairs={{0,1},{1,0},{64,65},{65,64},{2,3},{3,2},{66,67},{67,66},{4,5},{5,4... | collective-permute-start | bytes 1474568 | tf_op jit(solution)/shard_map/ppermute | solution.py:49
  353.1 22.7 %all-to-all-start.5 = ((bf16[16,192,128]{2,1,0:T(8,128)(2,1)}), bf16[16,192,128]{2,1,0:T(8,128)(2,1)S(1)}, u32[]{:S(2)}, u32[]{:S(2)}) async-start(bf16[16,192,128]{2,1,0:T(8,128)(2,1)} %shard_map.216), calls=%async_computation.5 | async-start | bytes 1572864 | tf_op jit(solution)/shard_map/all_to_all | solution.py:536
  357.8 159.3 %reduce-scatter.5.cloned.1.call-start = ((), (), s32[]{:S(2)}) async-start(), calls=%async_computation.16 | async-start | bytes 2228224 | tf_op jit(solution)/shard_map/reduce_scatter | solution.py:750
  438.7 20.4 %collective-permute-start.100 = (bf16[256,960]{1,0:T(8,128)(2,1)S(1)}, bf16[256,960]{1,0:T(8,128)(2,1)S(1)}, u32[]{:S(2)}, u32[]{:S(2)}) collective-permute-start(bf16[256,960]{1,0:T(8,128)(2,1)S(1)} %collective-permute-done.81.refs_2_), channel_id=1, source_target_pairs={{0,1},{1,0},{64,65},{65,64},{2,3},{3,2},{66,67},{67,66},{4,5},{5,4... | collective-permute-start | bytes 1474568 | tf_op jit(solution)/shard_map/ppermute | solution.py:49
  439.3 19.7 %collective-permute-start.105 = (bf16[256,960]{1,0:T(8,128)(2,1)S(1)}, bf16[256,960]{1,0:T(8,128)(2,1)S(1)}, u32[]{:S(2)}, u32[]{:S(2)}) collective-permute-start(bf16[256,960]{1,0:T(8,128)(2,1)S(1)} %collective-permute-done.82.refs_8_), channel_id=1, source_target_pairs={{0,1},{1,0},{64,65},{65,64},{2,3},{3,2},{66,67},{67,66},{4,5},{5,4... | collective-permute-start | bytes 1474568 | tf_op jit(solution)/shard_map/ppermute | solution.py:49
  450.2 89.1 %reduce-scatter.3.cloned.1.call-start = ((), (), s32[]{:S(2)}) async-start(), calls=%async_computation.15 | async-start | bytes 2228224 | tf_op jit(solution)/shard_map/reduce_scatter | solution.py:750
  470.5 22.7 %all-to-all-start.7 = ((bf16[16,192,128]{2,1,0:T(8,128)(2,1)}), bf16[16,192,128]{2,1,0:T(8,128)(2,1)S(1)}, u32[]{:S(2)}, u32[]{:S(2)}) async-start(bf16[16,192,128]{2,1,0:T(8,128)(2,1)} %shard_map.221), calls=%async_computation.9 | async-start | bytes 1572864 | tf_op jit(solution)/shard_map/all_to_all | solution.py:536
  548.1 95.5 %all-gather.3.cloned.1.call-start = ((), (), s32[]{:S(2)}) async-start(), calls=%async_computation.17 | async-start | bytes 4177920 | tf_op jit(solution)/shard_map/all_gather | solution.py:817
  555.2 21.5 %all-to-all-start.9 = ((bf16[16,64,384]{2,1,0:T(8,128)(2,1)}), bf16[16,64,384]{2,1,0:T(8,128)(2,1)S(1)}, u32[]{:S(2)}, u32[]{:S(2)}) async-start(bf16[16,64,384]{2,1,0:T(8,128)(2,1)} %shard_map.223), calls=%async_computation.11 | async-start | bytes 1572864 | tf_op jit(solution)/shard_map/all_to_all | solution.py:536
  564.8 16.7 %collective-permute-start.126 = (bf16[128,960]{1,0:T(8,128)(2,1)}, bf16[128,960]{1,0:T(8,128)(2,1)S(1)}, u32[]{:S(2)}, u32[]{:S(2)}) collective-permute-start(bf16[128,960]{1,0:T(8,128)(2,1)} %get-tuple-element.500), channel_id=1, source_target_pairs={{0,1},{1,0},{64,65},{65,64},{2,3},{3,2},{66,67},{67,66},{4,5},{5,4... | collective-permute-start | bytes 737288 | tf_op jit(solution)/shard_map/ppermute | solution.py:49
  576.8 20.7 %all-to-all-start.8 = ((bf16[16,64,384]{2,1,0:T(8,128)(2,1)}), bf16[16,64,384]{2,1,0:T(8,128)(2,1)S(1)}, u32[]{:S(2)}, u32[]{:S(2)}) async-start(bf16[16,64,384]{2,1,0:T(8,128)(2,1)} %shard_map.224), calls=%async_computation.10 | async-start | bytes 1572864 | tf_op jit(solution)/shard_map/all_to_all | solution.py:536
  581.4 33.7 %collective-permute-start.124 = (bf16[128,960]{1,0:T(8,128)(2,1)}, bf16[128,960]{1,0:T(8,128)(2,1)S(1)}, u32[]{:S(2)}, u32[]{:S(2)}) collective-permute-start(bf16[128,960]{1,0:T(8,128)(2,1)} %get-tuple-element.496), channel_id=1, source_target_pairs={{0,1},{1,0},{64,65},{65,64},{2,3},{3,2},{66,67},{67,66},{4,5},{5,4... | collective-permute-start | bytes 737288 | tf_op jit(solution)/shard_map/ppermute | solution.py:49
  582.8 29.6 %collective-permute-start.127 = (bf16[64,960]{1,0:T(8,128)(2,1)}, bf16[64,960]{1,0:T(8,128)(2,1)}, u32[]{:S(2)}, u32[]{:S(2)}) collective-permute-start(bf16[64,960]{1,0:T(8,128)(2,1)} %get-tuple-element.541), channel_id=1, source_target_pairs={{0,64},{1,65},{64,2},{65,3},{2,66},{3,67},{66,0},{67,1},{4,68},{5,... | collective-permute-start | bytes 368648 | tf_op jit(solution)/shard_map/ppermute | solution.py:49
  608.6 29.2 %all-to-all-start.11 = ((bf16[16,128,384]{2,1,0:T(8,128)(2,1)}), bf16[16,128,384]{2,1,0:T(8,128)(2,1)S(1)}, u32[]{:S(2)}, u32[]{:S(2)}) async-start(bf16[16,128,384]{2,1,0:T(8,128)(2,1)} %broadcast_in_dim.50), calls=%async_computation.13 | async-start | bytes 3145728 | tf_op jit(solution)/shard_map/all_to_all | solution.py:536
  614.2 17.8 %collective-permute-start.133 = (f32[128,960]{1,0:T(8,128)S(1)}, f32[128,960]{1,0:T(8,128)S(1)}, u32[]{:S(2)}, u32[]{:S(2)}) collective-permute-start(f32[128,960]{1,0:T(8,128)S(1)} %get-tuple-element.538), channel_id=1, source_target_pairs={{0,64},{64,0},{1,65},{65,1},{2,66},{66,2},{3,67},{67,3},{4,68},{68... | collective-permute-start | bytes 1474568 | tf_op jit(solution)/shard_map/ppermute | solution.py:53
  (242 other events, 3102.0 us)
Sparse Core Ops, SparseCore 0:
  362.5 74.5 reduce-scatter.4
  459.3 79.9 reduce-scatter.2
  555.3 53.7 all-gather.2

commit v6 on v5

--- a/solution.py
+++ b/solution.py
@@ -81,10 +81,8 @@
 
 def exchange_eight(parts):
     found = [parts[0]] + [None] * 7
-    for step, flip in ((0, 1), (1, 0), (3, 0), (1, 1), (3, 1)):
+    for step, flip in ((0, 1), (1, 0), (3, 0), (1, 1), (3, 1), (2, 0), (2, 1)):
         found[2 * ((4 - step) % 4) + flip] = hop(parts[2 * step + flip], step, flip)
-    found[4] = hop(hop(parts[4], 1), 1)
-    found[5] = hop(hop(parts[5], -1), -1, 1)
     return found
 
 
@@ -803,10 +801,10 @@
             exchange_eight(after(lin1, first[1])),
         ),
     )
-    att1 = attend_grads(sum(both1, []), after(lin1, dx0))
+    att1 = sum_over_blocks(attend_grads(sum(both1, []), after(lin1, dx0)))
     lin0 = exchange_eight(lin0)
-    ff0, ff1, lin0 = after((sum_feed(grad_ff0), ff1, lin0), att1)
     att0 = attend_grads(sum(both0, []), lin0)
+    ff0, ff1, att0 = after((sum_feed(grad_ff0), ff1, att0), att1)
     y1 = (kept1[4] + scatter_eight(after(parts1, att0))).astype(BF)
     layer_outputs = by_section(y0, y1)
     upper = 2 * UNITS
@@ -816,7 +814,7 @@
     lower = jnp.concatenate([lower[0], lower[1]], axis=1)
     found = lax.all_gather(jnp.concatenate([spread, lower], axis=0), "blk", axis=0)
     input_grads = by_section(dx0, dx1)
-    att1, att0 = sum_over_blocks(att1), sum_over_blocks(att0)
+    att0 = sum_over_blocks(att0)
     grad_gate, grad_up, grad_down = call(
         finish_feed_kernel,
         [whole(found.shape)],

time: 668 us -> 645 us (0.966)
  waiting for transfers between devices: 245 us -> 221 us
    reduce_scatter x2, waiting for transfers between devices: 22.2 us -> 10.7 us  [sum_feed(): return lax.psum_scatter(flat, 'blk', scatter_dimension=0, tiled=True)]
    ppermute x131 -> x125, waiting for transfers between devices: 169 us -> 159 us  [hop(): return lax.ppermute(array, EIGHT, ring_pairs(step, flip))]
    all_to_all x10, starting transfers between devices: 50.1 us -> 58 us  [exchange(): return lax.all_to_all(array, 'blk', 0, 0, tiled=True)]
    ppermute x131 -> x125, starting transfers between devices: 119 us -> 113 us  [hop(): return lax.ppermute(array, EIGHT, ring_pairs(step, flip))]
  transfers between devices with their start and end apart: 150 -> 144, of which waited for: 68 -> 67; matrix products, arithmetic and copies ran while one was open for 4% -> 4% of each run, Pallas kernels for 13% -> 13%
where the time goes in v6:
time: 645 us; the launch traced here: 634 us
  waiting for transfers between devices  221 us (34%)
  starting transfers between devices  181 us (28%)
  Pallas kernels  155 us (24%)
  local copies, waits for them, and re-layouts  23.4 us (4%)
  other arithmetic  19 us (3%)
  between operations  17.2 us (3%)
  blocking collectives  16.6 us (3%)
    ppermute x125, waiting for transfers between devices, hop(): return lax.ppermute(array, EIGHT, ring_pairs(step, flip))  159 us
    pallas_call x24, Pallas kernels, call(): pl.pallas_call(kernel, grid=(1,), in_specs=in_specs, out_specs=[whole(sha...  155 us
    ppermute x125, starting transfers between devices, hop(): return lax.ppermute(array, EIGHT, ring_pairs(step, flip))  113 us
    all_to_all x10, starting transfers between devices, exchange(): return lax.all_to_all(array, 'blk', 0, 0, tiled=True)  58 us
    all_to_all x10, waiting for transfers between devices, exchange(): return lax.all_to_all(array, 'blk', 0, 0, tiled=True)  32.6 us
    all_to_all x1, blocking collectives, exchange(): return lax.all_to_all(array, 'blk', 0, 0, tiled=True)  16.6 us
  transfers between devices with their start and end apart: 144, of which 67 were waited for; matrix products, arithmetic and copies ran while one was open for 4% of the time, Pallas kernels for 13%

profile of v6, /device:TPU:0, one launch (start us, length us, event | category | flops | bytes accessed | tf_op | source)
XLA Modules:
  0.0 633.9 jit_solution(4102689176300755134)
XLA Ops:
  13.0 19.0 %collective-permute-done.3.refs_8_ = bf16[256,1664]{1,0:T(8,128)(2,1)S(1)} collective-permute-done((bf16[256,1664]{1,0:T(8,128)(2,1)}, bf16[256,1664]{1,0:T(8,128)(2,1)S(1)}, u32[]{:S(2)}, u32[]{:S(2)}) %collective-permute-start.3) | collective-permute-done | bytes 852000 | tf_op jit(solution)/shard_map/ppermute | solution.py:49
  58.0 7.8 %all-to-all-start = ((bf16[16,192,128]{2,1,0:T(8,128)(2,1)}), bf16[16,192,128]{2,1,0:T(8,128)(2,1)}, u32[]{:S(2)}, u32[]{:S(2)}) async-start(bf16[16,192,128]{2,1,0:T(8,128)(2,1)} %get-tuple-element.256), calls=%async_computation | async-start | bytes 1572864 | tf_op jit(solution)/shard_map/all_to_all | solution.py:534
  81.9 7.7 %collective-permute-done.14.refs_12_ = bf16[240,640]{1,0:T(8,128)(2,1)} collective-permute-done((bf16[240,640]{1,0:T(8,128)(2,1)}, bf16[240,640]{1,0:T(8,128)(2,1)}, u32[]{:S(2)}, u32[]{:S(2)}) %collective-permute-start.14) | collective-permute-done | bytes 307232 | tf_op jit(solution)/shard_map/ppermute | solution.py:49
  96.8 8.1 %shard_map.205 = (bf16[16,64,128]{2,1,0:T(8,128)(2,1)}, f32[8,2048]{1,0:T(8,128)}) custom-call(s32[16]{0:T(128)} %select_reduce_fusion.place_ref, bf16[16,192,128]{2,1,0:T(8,128)(2,1)} %all-to-all-done.in_ref), custom_call_target="tpu_custom_call" | custom-call | flops 1 | bytes 1 | tf_op jit(solution)/shard_map/pallas_call | solution.py:514
  105.0 16.6 %all_to_all.65.in_ref = bf16[16,64,128]{2,1,0:T(8,128)(2,1)} all-to-all(bf16[16,64,128]{2,1,0:T(8,128)(2,1)} %get-tuple-element.260), channel_id=1, replica_groups=mesh['section'=2,'blk'=16,'wshard'=4] {'blk'}, dimensions={0} | all-to-all | bytes 524288 | tf_op jit(solution)/shard_map/all_to_all | solution.py:534
  131.8 6.7 %collective-permute-done.29.refs_8_ = bf16[128,960]{1,0:T(8,128)(2,1)S(1)} collective-permute-done((bf16[128,960]{1,0:T(8,128)(2,1)}, bf16[128,960]{1,0:T(8,128)(2,1)S(1)}, u32[]{:S(2)}, u32[]{:S(2)}) %collective-permute-start.29) | collective-permute-done | bytes 245792 | tf_op jit(solution)/shard_map/ppermute | solution.py:49
  147.8 8.4 %shard_map.208 = (f32[1024,640]{1,0:T(8,128)}, bf16[1024,320]{1,0:T(8,128)(2,1)}, bf16[128,960]{1,0:T(8,128)(2,1)}, bf16[128,960]{1,0:T(8,128)(2,1)}, bf16[128,9...) custom-call(s32[16]{0:T(128)} %stack.115.table_ref, ...), custom_call_target="tpu_custom_call" | custom-call | flops 1 | bytes 1 | tf_op jit(solution)/shard_map/pallas_call | solution.py:514
  180.1 6.0 shard_map.209
  186.1 7.9 %all-to-all-start.2 = ((bf16[16,192,128]{2,1,0:T(8,128)(2,1)}), bf16[16,192,128]{2,1,0:T(8,128)(2,1)S(1)}, u32[]{:S(2)}, u32[]{:S(2)}) async-start(bf16[16,192,128]{2,1,0:T(8,128)(2,1)} %get-tuple-element.314), calls=%async_computation.2 | async-start | bytes 1572864 | tf_op jit(solution)/shard_map/all_to_all | solution.py:534
  196.5 6.5 %collective-permute-done.44.refs_2_.refs_12_ = bf16[128,960]{1,0:T(8,128)(2,1)S(1)} collective-permute-done((bf16[128,960]{1,0:T(8,128)(2,1)S(1)}, bf16[128,960]{1,0:T(8,128)(2,1)S(1)}, u32[]{:S(2)}, u32[]{:S(2)}) %collective-permute-start.44) | collective-permute-done | bytes 245792 | tf_op jit(solution)/shard_map/ppermute | solution.py:49
  214.2 8.1 %shard_map.210 = (bf16[16,64,128]{2,1,0:T(8,128)(2,1)}, f32[8,2048]{1,0:T(8,128)}) custom-call(s32[16]{0:T(128)} %select_reduce_fusion.place_ref, bf16[16,192,128]{2,1,0:T(8,128)(2,1)} %copy-done.11), custom_call_target="tpu_custom_call" | custom-call | flops 1 | bytes 1 | tf_op jit(solution)/shard_map/pallas_call | solution.py:514
  227.6 8.7 %all-to-all-done.3.in_ref = bf16[16,64,128]{2,1,0:T(8,128)(2,1)S(1)} async-done(((bf16[16,64,128]{2,1,0:T(8,128)(2,1)}), bf16[16,64,128]{2,1,0:T(8,128)(2,1)S(1)}, u32[]{:S(2)}, u32[]{:S(2)}) %all-to-all-start.3) | async-done | bytes 262176 | tf_op jit(solution)/shard_map/all_to_all | solution.py:534
  245.5 6.0 collective-permute-done.58.refs_8_
  260.7 8.5 %shard_map.212 = (f32[1024,640]{1,0:T(8,128)}, bf16[1024,320]{1,0:T(8,128)(2,1)}, bf16[128,960]{1,0:T(8,128)(2,1)}, bf16[128,960]{1,0:T(8,128)(2,1)}, bf16[128,9...) custom-call(s32[16]{0:T(128)} %stack.115.table_ref, ...), custom_call_target="tpu_custom_call" | custom-call | flops 1 | bytes 1 | tf_op jit(solution)/shard_map/pallas_call | solution.py:514
  269.2 8.7 %shard_map.213 = (bf16[1024,640]{1,0:T(8,128)(2,1)}, bf16[128,960]{1,0:T(8,128)(2,1)}, bf16[128,960]{1,0:T(8,128)(2,1)}, bf16[128,960]{1,0:T(8,128)(2,1)}, bf16[...) custom-call(s32[16]{0:T(128)} %stack.115.table_ref, ...), custom_call_target="tpu_custom_call" | custom-call | flops 1 | bytes 1 | tf_op jit(solution)/shard_map/pallas_call | solution.py:514
  317.7 6.9 %shard_map.215 = bf16[16,64,960]{2,1,0:T(8,128)(2,1)} custom-call(bf16[128,960]{1,0:T(8,128)(2,1)} %get-tuple-element.327.refs_0_, bf16[128,960]{1,0:T(8,128)(2,1)} %copy-done.49, bf16[128,960]{1,0:T(8,128)(2,1)} %copy-done.39, bf16[128,960]{1,0:T(8,128)(2,1)} %copy-done.52, bf16[64,960]{1,0:T(8,128)(2,1)} %copy-done.69, bf16[64,960]{1,0:T(8,128)(2,1)} %copy-done.70, ...), custom_call_target="tpu_custom_call" | custom-call | flops 1 | bytes 1 | tf_op jit(solution)/shard_map/pallas_call | solution.py:514
  325.4 10.4 %shard_map.216 = bf16[16,192,128]{2,1,0:T(8,128)(2,1)} custom-call(s32[16]{0:T(128)} %select_reduce_fusion.place_ref, bf16[16,192,128]{2,1,0:T(8,128)(2,1)} %copy-done.11, bf16[16,64,128]{2,1,0:T(8,128)(2,1)} %copy-done.56, f32[8,2048]{1,0:T(8,128)} %get-tuple-element.367.lse_ref), custom_call_target="tpu_custom_call" | custom-call | flops 1 | bytes 1 | tf_op jit(solution)/shard_map/pallas_call | solution.py:514
  343.7 12.1 %collective-permute-done.79.refs_2_ = bf16[256,960]{1,0:T(8,128)(2,1)S(1)} collective-permute-done((bf16[256,960]{1,0:T(8,128)(2,1)S(1)}, bf16[256,960]{1,0:T(8,128)(2,1)S(1)}, u32[]{:S(2)}, u32[]{:S(2)}) %collective-permute-start.79) | collective-permute-done | bytes 491552 | tf_op jit(solution)/shard_map/ppermute | solution.py:49
  359.4 6.9 %shard_map.217 = (f32[128,960]{1,0:T(8,128)}, bf16[144,384]{1,0:T(8,128)(2,1)}, bf16[144,384]{1,0:T(8,128)(2,1)}, bf16[144,384]{1,0:T(8,128)(2,1)}, bf16[144,384...) custom-call(s32[16]{0:T(128)} %stack.115.table_ref, ...), custom_call_target="tpu_custom_call" | custom-call | flops 1 | bytes 1 | tf_op jit(solution)/shard_map/pallas_call | solution.py:514
  384.5 8.8 %shard_map.218 = (bf16[1024,640]{1,0:T(8,128)(2,1)}, bf16[128,960]{1,0:T(8,128)(2,1)}, bf16[128,960]{1,0:T(8,128)(2,1)}, bf16[128,960]{1,0:T(8,128)(2,1)}, bf16[...) custom-call(s32[16]{0:T(128)} %stack.115.table_ref, ...), custom_call_target="tpu_custom_call" | custom-call | flops 1 | bytes 1 | tf_op jit(solution)/shard_map/pallas_call | solution.py:514
  425.5 7.4 %all-to-all-start.6 = ((bf16[16,64,128]{2,1,0:T(8,128)(2,1)}), bf16[16,64,128]{2,1,0:T(8,128)(2,1)S(1)}, u32[]{:S(2)}, u32[]{:S(2)}) async-start(bf16[16,64,128]{2,1,0:T(8,128)(2,1)} %get-tuple-element.392), calls=%async_computation.6 | async-start | bytes 524288 | tf_op jit(solution)/shard_map/all_to_all | solution.py:534
  433.6 6.9 %shard_map.220 = bf16[16,64,960]{2,1,0:T(8,128)(2,1)} custom-call(bf16[128,960]{1,0:T(8,128)(2,1)} %get-tuple-element.295.refs_0_, bf16[128,960]{1,0:T(8,128)(2,1)} %copy-done.44, bf16[128,960]{1,0:T(8,128)(2,1)} %copy-done.33, bf16[128,960]{1,0:T(8,128)(2,1)} %copy-done.45, bf16[64,960]{1,0:T(8,128)(2,1)} %copy-done.65, bf16[64,960]{1,0:T(8,128)(2,1)} %copy-done.66, ...), custom_call_target="tpu_custom_call" | custom-call | flops 1 | bytes 1 | tf_op jit(solution)/shard_map/pallas_call | solution.py:514
  442.6 10.5 %shard_map.221 = bf16[16,192,128]{2,1,0:T(8,128)(2,1)} custom-call(s32[16]{0:T(128)} %select_reduce_fusion.place_ref, bf16[16,192,128]{2,1,0:T(8,128)(2,1)} %all-to-all-done.in_ref, bf16[16,64,128]{2,1,0:T(8,128)(2,1)} %copy-done.55, f32[8,2048]{1,0:T(8,128)} %get-tuple-element.416.lse_ref), custom_call_target="tpu_custom_call" | custom-call | flops 1 | bytes 1 | tf_op jit(solution)/shard_map/pallas_call | solution.py:514
  453.2 6.0 all-to-all-start.7
  476.0 6.8 %shard_map.222 = (f32[128,960]{1,0:T(8,128)}, bf16[144,384]{1,0:T(8,128)(2,1)}, bf16[144,384]{1,0:T(8,128)(2,1)}, bf16[144,384]{1,0:T(8,128)(2,1)}, bf16[144,384...) custom-call(s32[16]{0:T(128)} %stack.115.table_ref, ...), custom_call_target="tpu_custom_call" | custom-call | flops 1 | bytes 1 | tf_op jit(solution)/shard_map/pallas_call | solution.py:514
  487.7 7.1 %all-to-all-start.8 = ((bf16[16,64,384]{2,1,0:T(8,128)(2,1)}), bf16[16,64,384]{2,1,0:T(8,128)(2,1)S(1)}, u32[]{:S(2)}, u32[]{:S(2)}) async-start(bf16[16,64,384]{2,1,0:T(8,128)(2,1)} %shard_map.224), calls=%async_computation.10 | async-start | bytes 1572864 | tf_op jit(solution)/shard_map/all_to_all | solution.py:534
  516.7 10.7 %reduce-scatter.3.cloned.1.call-done = bf16[64,960]{1,0:T(8,128)(2,1)} async-done(((bf16[1024,960]{1,0:T(8,128)(2,1)}), bf16[64,960]{1,0:T(8,128)(2,1)}) %reduce-scatter.3.cloned.1.call-update) | async-done | bytes 122896 | tf_op jit(solution)/shard_map/reduce_scatter | solution.py:748
  536.4 6.1 all-to-all-done.12
  555.6 10.0 %all-to-all-done.9 = bf16[16,64,384]{2,1,0:T(8,128)(2,1)S(1)} async-done(((bf16[16,64,384]{2,1,0:T(8,128)(2,1)}), bf16[16,64,384]{2,1,0:T(8,128)(2,1)S(1)}, u32[]{:S(2)}, u32[]{:S(2)}) %all-to-all-start.9) | async-done | bytes 786464 | tf_op jit(solution)/shard_map/all_to_all | solution.py:534
  583.3 7.6 %collective-permute-done.122 = bf16[128,960]{1,0:T(8,128)(2,1)S(1)} collective-permute-done((bf16[128,960]{1,0:T(8,128)(2,1)S(1)}, bf16[128,960]{1,0:T(8,128)(2,1)S(1)}, u32[]{:S(2)}, u32[]{:S(2)}) %collective-permute-start.122) | collective-permute-done | bytes 245792 | tf_op jit(solution)/shard_map/ppermute | solution.py:49
  592.9 7.4 %collective-permute-done.127 = f32[128,960]{1,0:T(8,128)S(1)} collective-permute-done((f32[128,960]{1,0:T(8,128)S(1)}, f32[128,960]{1,0:T(8,128)S(1)}, u32[]{:S(2)}, u32[]{:S(2)}) %collective-permute-start.127) | collective-permute-done | bytes 491552 | tf_op jit(solution)/shard_map/ppermute | solution.py:53
  605.7 10.0 %all-to-all-done.11.in_ref = bf16[16,128,384]{2,1,0:T(8,128)(2,1)S(1)} async-done(((bf16[16,128,384]{2,1,0:T(8,128)(2,1)}), bf16[16,128,384]{2,1,0:T(8,128)(2,1)S(1)}, u32[]{:S(2)}, u32[]{:S(2)}) %all-to-all-start.11) | async-done | bytes 1572896 | tf_op jit(solution)/shard_map/all_to_all | solution.py:534
  (639 shorter events, 340.2 us)
Async XLA Ops:
  9.8 22.3 %collective-permute-start.3 = (bf16[256,1664]{1,0:T(8,128)(2,1)}, bf16[256,1664]{1,0:T(8,128)(2,1)S(1)}, u32[]{:S(2)}, u32[]{:S(2)}) collective-permute-start(bf16[256,1664]{1,0:T(8,128)(2,1)} %get-tuple-element.255.refs_0_), channel_id=1, source_target_pairs={{0,64},{1,65},{64,2},{65,3},{2,66},{3,67},{66,0},{67,1},{4,68},{5,... | collective-permute-start | bytes 2555912 | tf_op jit(solution)/shard_map/ppermute | solution.py:49
  11.5 21.7 %collective-permute-start.1 = (bf16[256,1664]{1,0:T(8,128)(2,1)}, bf16[256,1664]{1,0:T(8,128)(2,1)S(1)}, u32[]{:S(2)}, u32[]{:S(2)}) collective-permute-start(bf16[256,1664]{1,0:T(8,128)(2,1)} %get-tuple-element.255.refs_0_), channel_id=1, source_target_pairs={{0,66},{1,67},{64,0},{65,1},{2,64},{3,65},{66,2},{67,3},{4,70},{5,... | collective-permute-start | bytes 2555912 | tf_op jit(solution)/shard_map/ppermute | solution.py:49
  54.6 15.9 %collective-permute-start.11 = (bf16[256,960]{1,0:T(8,128)(2,1)}, bf16[256,960]{1,0:T(8,128)(2,1)S(1)}, u32[]{:S(2)}, u32[]{:S(2)}) collective-permute-start(bf16[256,960]{1,0:T(8,128)(2,1)} %get-tuple-element.284.refs_0_), channel_id=1, source_target_pairs={{0,64},{1,65},{64,2},{65,3},{2,66},{3,67},{66,0},{67,1},{4,68},{5,... | collective-permute-start | bytes 1474568 | tf_op jit(solution)/shard_map/ppermute | solution.py:49
  55.2 15.4 %collective-permute-start.10 = (bf16[256,960]{1,0:T(8,128)(2,1)}, bf16[256,960]{1,0:T(8,128)(2,1)S(1)}, u32[]{:S(2)}, u32[]{:S(2)}) collective-permute-start(bf16[256,960]{1,0:T(8,128)(2,1)} %get-tuple-element.284.refs_0_), channel_id=1, source_target_pairs={{0,66},{1,67},{64,0},{65,1},{2,64},{3,65},{66,2},{67,3},{4,70},{5,... | collective-permute-start | bytes 1474568 | tf_op jit(solution)/shard_map/ppermute | solution.py:49
  58.0 21.0 %collective-permute-start.9 = (bf16[256,960]{1,0:T(8,128)(2,1)}, bf16[256,960]{1,0:T(8,128)(2,1)S(1)}, u32[]{:S(2)}, u32[]{:S(2)}) collective-permute-start(bf16[256,960]{1,0:T(8,128)(2,1)} %get-tuple-element.284.refs_0_), channel_id=1, source_target_pairs={{0,1},{1,0},{64,65},{65,64},{2,3},{3,2},{66,67},{67,66},{4,5},{5,4... | collective-permute-start | bytes 1474568 | tf_op jit(solution)/shard_map/ppermute | solution.py:49
  58.0 23.8 %all-to-all-start = ((bf16[16,192,128]{2,1,0:T(8,128)(2,1)}), bf16[16,192,128]{2,1,0:T(8,128)(2,1)}, u32[]{:S(2)}, u32[]{:S(2)}) async-start(bf16[16,192,128]{2,1,0:T(8,128)(2,1)} %get-tuple-element.256), calls=%async_computation | async-start | bytes 1572864 | tf_op jit(solution)/shard_map/all_to_all | solution.py:534
  81.8 42.0 %collective-permute-start.12 = (bf16[960,384]{1,0:T(8,128)(2,1)}, bf16[960,384]{1,0:T(8,128)(2,1)S(1)}, u32[]{:S(2)}, u32[]{:S(2)}) collective-permute-start(bf16[960,384]{1,0:T(8,128)(2,1)} %get-tuple-element.266), channel_id=1, source_target_pairs={{0,64},{64,0},{1,65},{65,1},{2,66},{66,2},{3,67},{67,3},{4,68},{68... | collective-permute-start | bytes 2211848 | tf_op jit(solution)/shard_map/ppermute | solution.py:53
  90.5 31.0 %collective-permute-start.15 = (bf16[240,640]{1,0:T(8,128)(2,1)}, bf16[240,640]{1,0:T(8,128)(2,1)S(1)}, u32[]{:S(2)}, u32[]{:S(2)}) collective-permute-start(bf16[240,640]{1,0:T(8,128)(2,1)} %get-tuple-element.278), channel_id=1, source_target_pairs={{0,67},{1,66},{64,1},{65,0},{2,65},{3,64},{66,3},{67,2},{4,71},{5,... | collective-permute-start | bytes 921608 | tf_op jit(solution)/shard_map/ppermute | solution.py:49
  91.1 30.5 %collective-permute-start.16 = (bf16[240,640]{1,0:T(8,128)(2,1)}, bf16[240,640]{1,0:T(8,128)(2,1)S(1)}, u32[]{:S(2)}, u32[]{:S(2)}) collective-permute-start(bf16[240,640]{1,0:T(8,128)(2,1)} %get-tuple-element.279), channel_id=1, source_target_pairs={{0,2},{1,3},{64,66},{65,67},{2,0},{3,1},{66,64},{67,65},{4,6},{5,7... | collective-permute-start | bytes 921608 | tf_op jit(solution)/shard_map/ppermute | solution.py:49
  94.0 27.5 %collective-permute-start.17 = (bf16[240,640]{1,0:T(8,128)(2,1)}, bf16[240,640]{1,0:T(8,128)(2,1)S(1)}, u32[]{:S(2)}, u32[]{:S(2)}) collective-permute-start(bf16[240,640]{1,0:T(8,128)(2,1)} %get-tuple-element.280), channel_id=1, source_target_pairs={{0,3},{1,2},{64,67},{65,66},{2,1},{3,0},{66,65},{67,64},{4,7},{5,6... | collective-permute-start | bytes 921608 | tf_op jit(solution)/shard_map/ppermute | solution.py:49
  94.6 29.3 %collective-permute-start.19 = (bf16[240,640]{1,0:T(8,128)(2,1)}, bf16[240,640]{1,0:T(8,128)(2,1)S(1)}, u32[]{:S(2)}, u32[]{:S(2)}) collective-permute-start(bf16[240,640]{1,0:T(8,128)(2,1)} %get-tuple-element.282), channel_id=1, source_target_pairs={{0,65},{1,64},{64,3},{65,2},{2,67},{3,66},{66,1},{67,0},{4,69},{5,... | collective-permute-start | bytes 921608 | tf_op jit(solution)/shard_map/ppermute | solution.py:49
  186.1 20.6 %all-to-all-start.2 = ((bf16[16,192,128]{2,1,0:T(8,128)(2,1)}), bf16[16,192,128]{2,1,0:T(8,128)(2,1)S(1)}, u32[]{:S(2)}, u32[]{:S(2)}) async-start(bf16[16,192,128]{2,1,0:T(8,128)(2,1)} %get-tuple-element.314), calls=%async_computation.2 | async-start | bytes 1572864 | tf_op jit(solution)/shard_map/all_to_all | solution.py:534
  210.1 26.3 %collective-permute-start.52 = (bf16[256,960]{1,0:T(8,128)(2,1)S(1)}, bf16[256,960]{1,0:T(8,128)(2,1)}, u32[]{:S(2)}, u32[]{:S(2)}) collective-permute-start(bf16[256,960]{1,0:T(8,128)(2,1)S(1)} %pad_maximum_fusion.refs_0_), channel_id=1, source_target_pairs={{0,1},{1,0},{64,65},{65,64},{2,3},{3,2},{66,67},{67,66},{4,5},{5,4... | collective-permute-start | bytes 1474568 | tf_op jit(solution)/shard_map/ppermute | solution.py:49
  210.1 26.3 %collective-permute-start.53 = (bf16[256,960]{1,0:T(8,128)(2,1)S(1)}, bf16[256,960]{1,0:T(8,128)(2,1)S(1)}, u32[]{:S(2)}, u32[]{:S(2)}) collective-permute-start(bf16[256,960]{1,0:T(8,128)(2,1)S(1)} %pad_maximum_fusion.refs_0_), channel_id=1, source_target_pairs={{0,66},{1,67},{64,0},{65,1},{2,64},{3,65},{66,2},{67,3},{4,70},{5,... | collective-permute-start | bytes 1474568 | tf_op jit(solution)/shard_map/ppermute | solution.py:49
  210.3 26.1 %collective-permute-start.54 = (bf16[256,960]{1,0:T(8,128)(2,1)S(1)}, bf16[256,960]{1,0:T(8,128)(2,1)S(1)}, u32[]{:S(2)}, u32[]{:S(2)}) collective-permute-start(bf16[256,960]{1,0:T(8,128)(2,1)S(1)} %pad_maximum_fusion.refs_0_), channel_id=1, source_target_pairs={{0,64},{1,65},{64,2},{65,3},{2,66},{3,67},{66,0},{67,1},{4,68},{5,... | collective-permute-start | bytes 1474568 | tf_op jit(solution)/shard_map/ppermute | solution.py:49
  306.7 18.0 %collective-permute-start.77 = (bf16[256,960]{1,0:T(8,128)(2,1)S(1)}, bf16[256,960]{1,0:T(8,128)(2,1)S(1)}, u32[]{:S(2)}, u32[]{:S(2)}) collective-permute-start(bf16[256,960]{1,0:T(8,128)(2,1)S(1)} %collective-permute-done.54.refs_8_), channel_id=1, source_target_pairs={{0,1},{1,0},{64,65},{65,64},{2,3},{3,2},{66,67},{67,66},{4,5},{5,4... | collective-permute-start | bytes 1474568 | tf_op jit(solution)/shard_map/ppermute | solution.py:49
  306.8 17.9 %collective-permute-start.72 = (bf16[256,960]{1,0:T(8,128)(2,1)S(1)}, bf16[256,960]{1,0:T(8,128)(2,1)S(1)}, u32[]{:S(2)}, u32[]{:S(2)}) collective-permute-start(bf16[256,960]{1,0:T(8,128)(2,1)S(1)} %collective-permute-done.53.refs_2_), channel_id=1, source_target_pairs={{0,1},{1,0},{64,65},{65,64},{2,3},{3,2},{66,67},{67,66},{4,5},{5,4... | collective-permute-start | bytes 1474568 | tf_op jit(solution)/shard_map/ppermute | solution.py:49
  335.8 22.7 %all-to-all-start.5 = ((bf16[16,192,128]{2,1,0:T(8,128)(2,1)}), bf16[16,192,128]{2,1,0:T(8,128)(2,1)S(1)}, u32[]{:S(2)}, u32[]{:S(2)}) async-start(bf16[16,192,128]{2,1,0:T(8,128)(2,1)} %shard_map.216), calls=%async_computation.5 | async-start | bytes 1572864 | tf_op jit(solution)/shard_map/all_to_all | solution.py:534
  340.5 176.2 %reduce-scatter.5.cloned.1.call-start = ((), (), s32[]{:S(2)}) async-start(), calls=%async_computation.16 | async-start | bytes 2228224 | tf_op jit(solution)/shard_map/reduce_scatter | solution.py:748
  343.5 15.0 %collective-permute-start.80 = (bf16[256,960]{1,0:T(8,128)(2,1)S(1)}, bf16[256,960]{1,0:T(8,128)(2,1)S(1)}, u32[]{:S(2)}, u32[]{:S(2)}) collective-permute-start(bf16[256,960]{1,0:T(8,128)(2,1)S(1)} %pad_maximum_fusion.1.refs_0_), channel_id=1, source_target_pairs={{0,64},{1,65},{64,2},{65,3},{2,66},{3,67},{66,0},{67,1},{4,68},{5,... | collective-permute-start | bytes 1474568 | tf_op jit(solution)/shard_map/ppermute | solution.py:49
  421.4 20.4 %collective-permute-start.98 = (bf16[256,960]{1,0:T(8,128)(2,1)S(1)}, bf16[256,960]{1,0:T(8,128)(2,1)S(1)}, u32[]{:S(2)}, u32[]{:S(2)}) collective-permute-start(bf16[256,960]{1,0:T(8,128)(2,1)S(1)} %collective-permute-done.79.refs_2_), channel_id=1, source_target_pairs={{0,1},{1,0},{64,65},{65,64},{2,3},{3,2},{66,67},{67,66},{4,5},{5,4... | collective-permute-start | bytes 1474568 | tf_op jit(solution)/shard_map/ppermute | solution.py:49
  422.0 19.7 %collective-permute-start.103 = (bf16[256,960]{1,0:T(8,128)(2,1)S(1)}, bf16[256,960]{1,0:T(8,128)(2,1)S(1)}, u32[]{:S(2)}, u32[]{:S(2)}) collective-permute-start(bf16[256,960]{1,0:T(8,128)(2,1)S(1)} %collective-permute-done.80.refs_8_), channel_id=1, source_target_pairs={{0,1},{1,0},{64,65},{65,64},{2,3},{3,2},{66,67},{67,66},{4,5},{5,4... | collective-permute-start | bytes 1474568 | tf_op jit(solution)/shard_map/ppermute | solution.py:49
  425.5 16.3 %all-to-all-start.6 = ((bf16[16,64,128]{2,1,0:T(8,128)(2,1)}), bf16[16,64,128]{2,1,0:T(8,128)(2,1)S(1)}, u32[]{:S(2)}, u32[]{:S(2)}) async-start(bf16[16,64,128]{2,1,0:T(8,128)(2,1)} %get-tuple-element.392), calls=%async_computation.6 | async-start | bytes 524288 | tf_op jit(solution)/shard_map/all_to_all | solution.py:534
  432.9 94.5 %reduce-scatter.3.cloned.1.call-start = ((), (), s32[]{:S(2)}) async-start(), calls=%async_computation.15 | async-start | bytes 2228224 | tf_op jit(solution)/shard_map/reduce_scatter | solution.py:748
  453.2 21.9 %all-to-all-start.7 = ((bf16[16,192,128]{2,1,0:T(8,128)(2,1)}), bf16[16,192,128]{2,1,0:T(8,128)(2,1)S(1)}, u32[]{:S(2)}, u32[]{:S(2)}) async-start(bf16[16,192,128]{2,1,0:T(8,128)(2,1)} %shard_map.221), calls=%async_computation.9 | async-start | bytes 1572864 | tf_op jit(solution)/shard_map/all_to_all | solution.py:534
  487.7 28.9 %all-to-all-start.8 = ((bf16[16,64,384]{2,1,0:T(8,128)(2,1)}), bf16[16,64,384]{2,1,0:T(8,128)(2,1)S(1)}, u32[]{:S(2)}, u32[]{:S(2)}) async-start(bf16[16,64,384]{2,1,0:T(8,128)(2,1)} %shard_map.224), calls=%async_computation.10 | async-start | bytes 1572864 | tf_op jit(solution)/shard_map/all_to_all | solution.py:534
  536.3 85.2 %all-gather.3.cloned.1.call-start = ((), (), s32[]{:S(2)}) async-start(), calls=%async_computation.17 | async-start | bytes 4177920 | tf_op jit(solution)/shard_map/all_gather | solution.py:815
  543.4 22.2 %all-to-all-start.9 = ((bf16[16,64,384]{2,1,0:T(8,128)(2,1)}), bf16[16,64,384]{2,1,0:T(8,128)(2,1)S(1)}, u32[]{:S(2)}, u32[]{:S(2)}) async-start(bf16[16,64,384]{2,1,0:T(8,128)(2,1)} %shard_map.223), calls=%async_computation.11 | async-start | bytes 1572864 | tf_op jit(solution)/shard_map/all_to_all | solution.py:534
  548.9 34.4 %collective-permute-start.118 = (bf16[128,960]{1,0:T(8,128)(2,1)}, bf16[128,960]{1,0:T(8,128)(2,1)S(1)}, u32[]{:S(2)}, u32[]{:S(2)}) collective-permute-start(bf16[128,960]{1,0:T(8,128)(2,1)} %get-tuple-element.482), channel_id=1, source_target_pairs={{0,1},{1,0},{64,65},{65,64},{2,3},{3,2},{66,67},{67,66},{4,5},{5,4... | collective-permute-start | bytes 737288 | tf_op jit(solution)/shard_map/ppermute | solution.py:49
  551.0 29.7 %collective-permute-start.121 = (bf16[64,960]{1,0:T(8,128)(2,1)}, bf16[64,960]{1,0:T(8,128)(2,1)}, u32[]{:S(2)}, u32[]{:S(2)}) collective-permute-start(bf16[64,960]{1,0:T(8,128)(2,1)} %get-tuple-element.527), channel_id=1, source_target_pairs={{0,64},{1,65},{64,2},{65,3},{2,66},{3,67},{66,0},{67,1},{4,68},{5,... | collective-permute-start | bytes 368648 | tf_op jit(solution)/shard_map/ppermute | solution.py:49
  576.8 38.9 %all-to-all-start.11 = ((bf16[16,128,384]{2,1,0:T(8,128)(2,1)}), bf16[16,128,384]{2,1,0:T(8,128)(2,1)S(1)}, u32[]{:S(2)}, u32[]{:S(2)}) async-start(bf16[16,128,384]{2,1,0:T(8,128)(2,1)} %broadcast_in_dim.50), calls=%async_computation.13 | async-start | bytes 3145728 | tf_op jit(solution)/shard_map/all_to_all | solution.py:534
  582.5 17.8 %collective-permute-start.127 = (f32[128,960]{1,0:T(8,128)S(1)}, f32[128,960]{1,0:T(8,128)S(1)}, u32[]{:S(2)}, u32[]{:S(2)}) collective-permute-start(f32[128,960]{1,0:T(8,128)S(1)} %get-tuple-element.524), channel_id=1, source_target_pairs={{0,64},{64,0},{1,65},{65,1},{2,66},{66,2},{3,67},{67,3},{4,68},{68... | collective-permute-start | bytes 1474568 | tf_op jit(solution)/shard_map/ppermute | solution.py:53
  (244 other events, 2792.8 us)
Sparse Core Ops, SparseCore 0:
  345.2 74.5 reduce-scatter.4
  442.0 85.3 reduce-scatter.2
  543.5 69.3 all-gather.2
